TPU v7x, 128 devices: a whole 4x4x4 slice. The times are simulated.
128 devices in a mesh: dp: 16 (over z_hi, y, core), blk: 8 (over x, z_lo).
Axes of the slice: x: 4, y: 4, z: 4 (z_hi: 2, z_lo: 2; z = z_hi * 2 + z_lo), core: 2. Of those that a mesh axis runs over, the one named last changes fastest.
Arguments:
- teacher_image: bfloat16 [16384, 1152], P(('dp', 'blk')), may hold values from -7 to 7
- teacher_text: bfloat16 [16384, 1152], P(('dp', 'blk')), may hold values from -7 to 7
- student_image: bfloat16 [16384, 768], P(('dp', 'blk')), may hold values from -0.21875 to 0.21875
- student_text: bfloat16 [16384, 768], P(('dp', 'blk')), may hold values from -0.21875 to 0.21875
Outputs:
- image_grad: float32 [16384, 768], P(('dp', 'blk'))
- text_grad: float32 [16384, 768], P(('dp', 'blk'))
- kd_loss: float32 [], replicated
All inputs are finite; a program needn't handle non-finite values.
Results may differ from a plain program's by a relative error of at most 0.0045.
Values may be sent and summed in bfloat16 or wider, within the bound.
No kernel may reach another device: no remote copies, remote signals or barrier semaphores. Data moves between devices by JAX's collectives and lax.ppermute only.
A program may use at most 64 MiB of HBM per device.

v0:
```python
from functools import partial

import jax
import jax.numpy as jnp
from jax import lax
from jax.sharding import PartitionSpec as P

eps = 1e-06
scale_t = 10.0
bias_t = -2.0
scale_s = 10.0
bias_s = -2.0


def unit_rows(values):
    wide = values.astype(jnp.float32)
    norms = jnp.sqrt(jnp.sum(wide * wide, axis=-1, keepdims=True) + eps)
    return (wide / norms, norms)


def tile_terms(rows_t, rows_s, piece_t, piece_s):
    teach_logit = jnp.dot(rows_t, piece_t.T, preferred_element_type=jnp.float32) * scale_t + bias_t
    target = jax.nn.sigmoid(teach_logit)
    stud_logit = jnp.dot(rows_s, piece_s.T, preferred_element_type=jnp.float32) * scale_s + bias_s
    loss_part = jnp.sum(jax.nn.softplus(stud_logit) - target * stud_logit)
    coef = ((jax.nn.sigmoid(stud_logit) - target) * scale_s).astype(jnp.bfloat16)
    img_part = jnp.dot(coef, piece_s, preferred_element_type=jnp.float32)
    text_part = jnp.dot(coef.T, rows_s, preferred_element_type=jnp.float32)
    return (loss_part, img_part, text_part)


def pair_tile(running, pieces, offset, rows_t, rows_s):
    piece_t, piece_s = pieces
    loss_part, img_part, text_part = tile_terms(rows_t, rows_s, piece_t, piece_s)
    return (loss_part, img_part, text_part)


def body(teacher_image, teacher_text, student_image, student_text):
    rows_dev = teacher_image.shape[0]
    width_s = student_image.shape[1]
    teach_img = unit_rows(teacher_image)[0].astype(jnp.bfloat16)
    teach_txt = unit_rows(teacher_text)[0].astype(jnp.bfloat16)
    unit_img, norm_img = unit_rows(student_image)
    unit_txt, norm_txt = unit_rows(student_text)
    stud_img = unit_img.astype(jnp.bfloat16)
    stud_txt = unit_txt.astype(jnp.bfloat16)
    rows_t, rows_s = (
        lax.all_gather(teach_img, "blk", axis=0, tiled=True),
        lax.all_gather(stud_img, "blk", axis=0, tiled=True),
    )
    fold_fn = partial(pair_tile, rows_t=rows_t, rows_s=rows_s)
    init = (
        jnp.zeros((), jnp.float32),
        jnp.zeros((rows_t.shape[0], width_s), jnp.float32),
        jnp.zeros((rows_dev * lax.axis_size("dp"), width_s), jnp.float32),
    )
    loss_sum, img_acc, text_acc = fold_fn(
        init,
        (
            lax.all_gather(teach_txt, "dp", axis=0, tiled=True),
            lax.all_gather(stud_txt, "dp", axis=0, tiled=True),
        ),
        jnp.int32(0),
    )
    grad_txt = lax.psum_scatter(text_acc, "dp", scatter_dimension=0, tiled=True)
    grad_img = lax.psum_scatter(img_acc, "blk", scatter_dimension=0, tiled=True)
    loss_all = lax.psum(loss_sum, ("dp", "blk"))
    pair_count = float(rows_dev * lax.axis_size("dp") * lax.axis_size("blk"))
    kd_loss = loss_all / (pair_count * pair_count)
    image_grad = (
        grad_img - jnp.sum(grad_img * unit_img, axis=-1, keepdims=True) * unit_img
    ) / norm_img
    text_grad = (
        grad_txt - jnp.sum(grad_txt * unit_txt, axis=-1, keepdims=True) * unit_txt
    ) / norm_txt
    return (image_grad, text_grad, kd_loss)


def solution(mesh):
    in_specs = (
        P(("dp", "blk"), None),
        P(("dp", "blk"), None),
        P(("dp", "blk"), None),
        P(("dp", "blk"), None),
    )
    out_specs = (P(("dp", "blk"), None), P(("dp", "blk"), None), P())
    return jax.shard_map(body, mesh=mesh, in_specs=in_specs, out_specs=out_specs, check_vma=False)
```

profile of v0, /device:TPU:0, one launch (start us, length us, event | category | flops | bytes accessed | tf_op | source)
XLA Modules:
  0.0 431.8 jit_solution(17899891751091603031)
XLA Ops:
  7.2 0.0 all-gather.5.cloned.1.call-start
  7.2 1.0 fusion.6
  8.3 1.7 fusion.8
  10.0 0.0 all-gather.5.cloned.1.call-update
  10.0 0.0 all-gather.7.cloned.1.call-start
  10.1 1.0 fusion.7
  11.1 1.7 fusion.9
  12.8 0.0 all-gather.7.cloned.1.call-update
  12.9 0.0 all-gather.9.cloned.1.call-start
  12.9 1.1 fusion.2
  14.0 1.8 fusion.3
  15.8 0.0 all-gather.9.cloned.1.call-update
  15.8 0.0 all-gather.11.cloned.1.call-start
  15.9 1.1 fusion.4
  17.0 1.8 fusion.5
  18.8 0.0 all-gather.11.cloned.1.call-update
  18.8 0.0 reduce-scatter.3.cloned.1.call-start
  18.9 37.3 %all-gather.5.cloned.1.call-done = bf16[1024,768]{1,0:T(8,128)(2,1)} async-done(((bf16[128,768]{1,0:T(8,128)(2,1)}), bf16[1024,768]{1,0:T(8,128)(2,1)}) %all-gather.5.cloned.1.call-update) | async-done | bytes 1572880 | tf_op jit(solution)/shard_map/all_gather | solution.py:49
  56.1 54.9 %all-gather.7.cloned.1.call-done = bf16[2048,768]{1,0:T(8,128)(2,1)} async-done(((bf16[128,768]{1,0:T(8,128)(2,1)}), bf16[2048,768]{1,0:T(8,128)(2,1)}) %all-gather.7.cloned.1.call-update) | async-done | bytes 3145744 | tf_op jit(solution)/shard_map/all_gather | solution.py:61
  111.1 9.0 %fusion.10 = f32[1024,2048]{1,0:T(8,128)} fusion(bf16[1024,768]{1,0:T(8,128)(2,1)} %all-gather.5.cloned.1.call-done, bf16[2048,768]{1,0:T(8,128)(2,1)} %all-gather.7.cloned.1.call-done), kind=kOutput, calls=%fused_computation.30 | convolution fusion | flops 3221225472 | bytes 13107200 | tf_op jit(solution)/shard_map/dot_general | solution.py:24
  120.1 0.0 copy-start.2
  120.1 47.9 %all-gather.9.cloned.1.call-done = bf16[1024,1152]{1,0:T(8,128)(2,1)} async-done(((bf16[128,1152]{1,0:T(8,128)(2,1)}), bf16[1024,1152]{1,0:T(8,128)(2,1)}) %all-gather.9.cloned.1.call-update) | async-done | bytes 2359312 | tf_op jit(solution)/shard_map/all_gather | solution.py:48
  168.0 62.0 %all-gather.11.cloned.1.call-done = bf16[2048,1152]{1,0:T(8,128)(2,1)} async-done(((bf16[128,1152]{1,0:T(8,128)(2,1)}), bf16[2048,1152]{1,0:T(8,128)(2,1)}) %all-gather.11.cloned.1.call-update) | async-done | bytes 4718608 | tf_op jit(solution)/shard_map/all_gather | solution.py:60
  230.0 18.1 %fusion.1 = (f32[]{:T(128)}, bf16[1024,2048]{1,0:T(8,128)(2,1)S(1)}) fusion(f32[1024,2048]{1,0:T(8,128)} %fusion.10, bf16[1024,1152]{1,0:T(8,128)(2,1)} %all-gather.9.cloned.1.call-done, bf16[2048,1152]{1,0:T(8,128)(2,1)} %all-gather.11.cloned.1.call-done), kind=kOutput, calls=%fused_computation.2 | convolution fusion | flops 4877975552 | bytes 19660804 | tf_op jit(solution)/shard_map/dot_general | solution.py:22
  248.0 0.0 copy-start.3
  248.0 2.0 copy-done.3
  250.1 0.0 copy-done.2
  250.1 5.2 %fusion.11 = f32[1024,768]{1,0:T(8,128)} fusion(bf16[1024,2048]{1,0:T(8,128)(2,1)S(1)} %get-tuple-element.4, bf16[2048,768]{1,0:T(8,128)(2,1)S(1)} %copy-done.2), kind=kOutput, calls=%fused_computation.31 | convolution fusion | flops 3221225472 | bytes 10485760 | tf_op jit(solution)/shard_map/dot_general | solution.py:27
  255.3 0.0 reduce-scatter.3.cloned.1.call-update
  255.3 0.2 reduce-scatter.5.cloned.1.call-start
  255.5 8.9 %fusion.12 = f32[2048,768]{1,0:T(8,128)} fusion(bf16[1024,2048]{1,0:T(8,128)(2,1)} %copy-done.3, bf16[1024,768]{1,0:T(8,128)(2,1)} %all-gather.5.cloned.1.call-done), kind=kOutput, calls=%fused_computation.32 | convolution fusion | flops 3221225472 | bytes 12058624 | tf_op jit(solution)/shard_map/dot_general | solution.py:28
  264.4 0.0 copy-start
  264.4 0.0 copy-start.1
  264.4 0.0 reduce-scatter.5.cloned.1.call-update
  264.4 71.9 %psum.7 = f32[]{:T(128)} all-reduce(f32[]{:T(128)} %get-tuple-element.3), channel_id=1, replica_groups=mesh['dp'=16,'blk'=8] {'dp','blk'}, use_global_device_ids=true, to_apply=%region_9.10 | all-reduce | flops 1 | bytes 8 | tf_op jit(solution)/shard_map/psum | solution.py:67
  337.0 0.0 reduce-scatter.3.cloned.1.call-done
  337.0 0.0 copy-done
  337.0 1.2 multiply_reduce_fusion.1
  338.2 1.9 subtract_divide_fusion.1
  340.1 80.6 %reduce-scatter.5.cloned.1.call-done = f32[128,768]{1,0:T(8,128)} async-done(((f32[2048,768]{1,0:T(8,128)}), f32[128,768]{1,0:T(8,128)}) %reduce-scatter.5.cloned.1.call-update) | async-done | bytes 393232 | tf_op jit(solution)/shard_map/reduce_scatter | solution.py:65
  420.7 0.0 copy-done.1
  420.7 1.2 multiply_reduce_fusion
  421.9 1.9 subtract_divide_fusion
  (4 shorter events, 0.0 us)
Async XLA Ops:
  7.2 49.0 %all-gather.5.cloned.1.call-start = ((), (), s32[]{:S(2)}) async-start(), calls=%async_computation.2 | async-start | bytes 1769472 | tf_op jit(solution)/shard_map/all_gather | solution.py:49
  10.0 101.1 %all-gather.7.cloned.1.call-start = ((), (), s32[]{:S(2)}) async-start(), calls=%async_computation.3 | async-start | bytes 3342336 | tf_op jit(solution)/shard_map/all_gather | solution.py:61
  12.9 155.1 %all-gather.9.cloned.1.call-start = ((), (), s32[]{:S(2)}) async-start(), calls=%async_computation.4 | async-start | bytes 2654208 | tf_op jit(solution)/shard_map/all_gather | solution.py:48
  15.8 214.1 %all-gather.11.cloned.1.call-start = ((), (), s32[]{:S(2)}) async-start(), calls=%async_computation.5 | async-start | bytes 5013504 | tf_op jit(solution)/shard_map/all_gather | solution.py:60
  18.8 318.1 %reduce-scatter.3.cloned.1.call-start = ((), (), s32[]{:S(2)}) async-start(), calls=%async_computation.6 | async-start | bytes 3538944 | tf_op jit(solution)/shard_map/reduce_scatter | solution.py:66
  120.1 130.0 %copy-start.2 = (bf16[2048,768]{1,0:T(8,128)(2,1)S(1)}, bf16[2048,768]{1,0:T(8,128)(2,1)}, u32[]{:S(2)}) copy-start(bf16[2048,768]{1,0:T(8,128)(2,1)} %all-gather.7.cloned.1.call-done) | copy-start | bytes 9437188
  248.0 2.0 copy-start.3
  255.3 165.4 %reduce-scatter.5.cloned.1.call-start = ((), (), s32[]{:S(2)}) async-start(), calls=%async_computation.7 | async-start | bytes 6684672 | tf_op jit(solution)/shard_map/reduce_scatter | solution.py:65
  264.4 72.6 %copy-start = (bf16[128,768]{1,0:T(8,128)(2,1)S(1)}, bf16[128,768]{1,0:T(8,128)(2,1)}, u32[]{:S(2)}) copy-start(bf16[128,768]{1,0:T(8,128)(2,1)} %param.6) | copy-start | bytes 589828
  264.4 156.3 %copy-start.1 = (bf16[128,768]{1,0:T(8,128)(2,1)S(1)}, bf16[128,768]{1,0:T(8,128)(2,1)}, u32[]{:S(2)}) copy-start(bf16[128,768]{1,0:T(8,128)(2,1)} %param.7) | copy-start | bytes 589828
Sparse Core Ops, SparseCore 0:
  10.1 45.9 all-gather.4
  58.6 52.4 all-gather.6
  113.3 54.6 all-gather.8
  170.8 59.1 all-gather.10
  255.4 70.3 reduce-scatter.2
  329.9 90.8 reduce-scatter.4
where the time goes:
time: 432 us
  waiting for transfers between devices  283 us (66%)
  blocking collectives  71.9 us (17%)
  matrix products  41.1 us (10%)
  other arithmetic  17.6 us (4%)
  between operations  15.9 us (4%)
    reduce_scatter x1, waiting for transfers between devices, body(): grad_txt = lax.psum_scatter(text_acc, 'dp', scatter_dimension=0, tiled=True)  80.6 us
    psum x1, blocking collectives, body(): loss_all = lax.psum(loss_sum, ('dp', 'blk'))  71.9 us
    all_gather x1, waiting for transfers between devices, body(): lax.all_gather(teach_txt, 'dp', axis=0, tiled=True)  62 us
    all_gather x1, waiting for transfers between devices, body(): lax.all_gather(stud_txt, 'dp', axis=0, tiled=True)  54.9 us
    all_gather x1, waiting for transfers between devices, body(): lax.all_gather(teach_img, 'blk', axis=0, tiled=True)  47.9 us
    all_gather x1, waiting for transfers between devices, body(): lax.all_gather(stud_img, 'blk', axis=0, tiled=True)  37.3 us
    dot_general x1, matrix products, tile_terms(): jnp.dot(rows_t, piece_t.T, preferred_element_type=jnp.float32) * scale_t  18.1 us
    dot_general x1, matrix products, tile_terms(): jnp.dot(rows_s, piece_s.T, preferred_element_type=jnp.float32) * scale_s  9.04 us
  transfers between devices with their start and end apart: 6, of which 5 were waited for; matrix products, arithmetic and copies ran while one was open for 7% of the time, Pallas kernels for 0%

commit v1 on v0

v1 whole, which is shorter than its diff:
```python
import functools
import itertools

import jax
import jax.numpy as jnp
from jax import lax
from jax.experimental import pallas as pl
from jax.experimental.pallas import tpu as pltpu
from jax.sharding import PartitionSpec as P

eps = 1e-06
scale = 10.0
bias = -2.0
AXES = ("dp", "blk")
f32, bf16 = jnp.float32, jnp.bfloat16

ZH, Y, C, X, ZL = 2, 4, 2, 4, 2
NT = (((1,), (1,)), ((), ()))
TN = (((0,), (0,)), ((), ()))


def place(zh, y, c, x, zl):
    return ((zh * Y + y) * C + c) * (X * ZL) + x * ZL + zl


def permute(value, move):
    pairs = [
        (place(*at), place(*move(*at)))
        for at in itertools.product(range(ZH), range(Y), range(C), range(X), range(ZL))
    ]
    return lax.ppermute(value, AXES, pairs)


def to_x(value, step):
    return permute(value, lambda zh, y, c, x, zl: (zh, y, c, (x + step) % X, zl))


def to_y(value, step):
    return permute(value, lambda zh, y, c, x, zl: (zh, (y + step) % Y, c, x, zl))


def flip_x(value, bits):
    return permute(value, lambda zh, y, c, x, zl: (zh, y, c, x ^ bits, zl))


def flip_y(value, bits):
    return permute(value, lambda zh, y, c, x, zl: (zh, y ^ bits, c, x, zl))


def to_core(value):
    return permute(value, lambda zh, y, c, x, zl: (zh, y, 1 - c, x, zl))


def to_image_z(value):
    return permute(value, lambda zh, y, c, x, zl: (zh, y, c, x, 1 - zl))


def to_text_z(value):
    return permute(value, lambda zh, y, c, x, zl: (1 - zh, y, c, x, 1 - zl))


def to_far_z(value):
    return permute(value, lambda zh, y, c, x, zl: (1 - zh, y, c, x, zl))


def call(kernel, name, args, outs, limit=16, far=(), keep=True, flops=0, scratch=()):
    vmem = pl.BlockSpec(memory_space=pltpu.VMEM)
    near = [
        pltpu.with_memory_space_constraint(v, pltpu.HBM if any(v is w for w in far) else pltpu.VMEM) for v in args
    ]
    shape_of = pltpu.VMEM if keep else jax.ShapeDtypeStruct
    return pl.pallas_call(
        kernel,
        out_shape=tuple(shape_of(shape, dtype) for shape, dtype in outs),
        in_specs=[vmem] * len(args),
        out_specs=(vmem,) * len(outs),
        scratch_shapes=[pltpu.VMEM(shape, dtype) for shape, dtype in scratch],
        compiler_params=pltpu.CompilerParams(vmem_limit_bytes=limit * 2**20),
        cost_estimate=pl.CostEstimate(
            flops=flops, transcendentals=0, bytes_accessed=sum(v.size * v.dtype.itemsize for v in args),
        ),
        name=name,
    )(*near)


def norm_of(wide):
    return jnp.sqrt(jnp.sum(wide * wide, axis=-1, keepdims=True) + eps)


def units_kernel(ti, si, tt, st, img, txt):
    for teach, stud, out in ((ti, si, img), (tt, st, txt)):
        wide = teach[...].astype(f32)
        split = wide.shape[1]
        out[:, :split] = (wide / norm_of(wide)).astype(bf16)
        wide = stud[...].astype(f32)
        out[:, split:] = (wide / norm_of(wide)).astype(bf16)


def tile_terms(cos_t, cos_s):
    half_s = cos_s * (0.5 * scale) + 0.5 * bias
    tanh_t = jnp.tanh(cos_t * (0.5 * scale) + 0.5 * bias)
    tanh_s = jnp.tanh(half_s)
    coef = ((tanh_s - tanh_t) * (0.5 * scale)).astype(bf16)
    left = 1.0 - tanh_s
    for _ in range(3):
        rows = left.shape[0] // 2
        left = left[:rows] * left[rows:]
    line = half_s + half_s * tanh_t
    fold = lambda v: jnp.sum(v.reshape(-1, 8, v.shape[1]), axis=0)
    loss = -(fold(jnp.log(left)) + fold(line))
    return coef, sum(loss[:, k:k + 128] for k in range(0, loss.shape[1], 128))


def stack(refs, cols):
    return jnp.concatenate([r[:, cols] for r in refs], axis=0)


def dot(a, b, dims=(((1,), (0,)), ((), ()))):
    return lax.dot_general(a, b, dims, preferred_element_type=f32)


def near_tile_kernel(width_t, *refs):
    imgs, txt, oth, (g_img, g_txt, g_oth, loss_ref) = refs[:3], refs[3:6], refs[6:9], refs[9:]
    cols_t, cols_s = slice(0, width_t), slice(width_t, None)
    img_t, img_s = stack(imgs, cols_t), stack(imgs, cols_s)
    text_s = stack(list(txt) + list(oth), cols_s)
    coef, loss = tile_terms(dot(img_t, stack(list(txt) + list(oth), cols_t), NT), dot(img_s, text_s, NT))
    loss_ref[...] = loss
    g_img[...] = dot(coef, text_s)
    half = g_txt.shape[0]
    g_txt[...] = dot(coef[:, :half], img_s, TN)
    g_oth[...] = dot(coef[:, half:], img_s, TN)


def first_tile_kernel(width_t, *refs):
    imgs, txt, oth, refs = refs[:5], refs[5:10], refs[10:15], refs[15:]
    p_img, p_txt, p_oth, p_loss, g_img, g_txt, g_oth, loss_ref, coef_n, coef_f = refs
    cols_t, cols_s = slice(0, width_t), slice(width_t, None)
    own, zed, left, right, far = range(5)
    near = [[txt[own], txt[zed]], [oth[own], oth[zed]], [txt[left], oth[left]]]
    wide = [[txt[right]], [txt[far]], [oth[right]], [oth[far]]]
    total = p_loss[...]
    img_t, img_s = stack(imgs, cols_t), stack(imgs, cols_s)
    far_t, far_s = stack(imgs[3:], cols_t), stack(imgs[3:], cols_s)
    for n, texts in enumerate(wide):
        part, loss = tile_terms(dot(img_t, stack(texts, cols_t), NT), dot(img_s, stack(texts, cols_s), NT))
        coef_f[:, n * 256:(n + 1) * 256] = part
        total = total + loss
    for n, texts in enumerate(near):
        part, loss = tile_terms(dot(far_t, stack(texts, cols_t), NT), dot(far_s, stack(texts, cols_s), NT))
        coef_n[:, n * 256:(n + 1) * 256] = part
        total = total + loss
    loss_ref[...] = total
    wide_s = jnp.concatenate([stack(texts, cols_s) for texts in wide], axis=0)
    near_s = jnp.concatenate([stack(texts, cols_s) for texts in near], axis=0)
    g_img[0:384, :] = p_img[...] + dot(coef_f[0:384, :], wide_s)
    g_img[384:, :] = dot(coef_f[384:, :], wide_s) + dot(coef_n[...], near_s)
    for n, (ref, row) in enumerate([(g_txt, 384), (g_txt, 640), (g_oth, 384), (g_oth, 640)]):
        ref[row:row + 256, :] = dot(coef_f[:, n * 256:(n + 1) * 256], img_s, TN)
    g_txt[0:256, :] = p_txt[0:256, :] + dot(coef_n[:, 0:256], far_s, TN)
    g_oth[0:256, :] = p_oth[0:256, :] + dot(coef_n[:, 256:512], far_s, TN)
    grad = dot(coef_n[:, 512:768], far_s, TN)
    g_txt[256:384, :] = p_txt[256:, :] + grad[:128]
    g_oth[256:384, :] = p_oth[256:, :] + grad[128:]


def last_coef_kernel(width_t, *refs):
    imgs, texts, (p_loss, coef_a, coef_b, loss_ref) = refs[:6], refs[6:18], refs[18:]
    cols_t, cols_s = slice(0, width_t), slice(width_t, None)
    last_i, last_t = imgs[5], [texts[5], texts[11]]
    part_a, loss_a = tile_terms(
        dot(stack(texts, cols_t), last_i[:, cols_t], NT), dot(stack(texts, cols_s), last_i[:, cols_s], NT)
    )
    part_b, loss_b = tile_terms(
        dot(stack(imgs[:5], cols_t), stack(last_t, cols_t), NT), dot(stack(imgs[:5], cols_s), stack(last_t, cols_s), NT)
    )
    coef_a[...] = part_a
    coef_b[...] = part_b
    loss_ref[...] = p_loss[...] + loss_a + loss_b


def other_grad_kernel(width_t, *refs):
    imgs, (coef_a, coef_b, part, out) = refs[:6], refs[6:]
    most = part.shape[0]
    grad = dot(coef_a[most + 128:, :], imgs[5][:, width_t:])
    out[:most, :] = (part[...] + grad[:most]).astype(bf16)
    last = dot(coef_b[:, 128:], stack(imgs[:5], slice(width_t, None)), TN)
    out[most:, :] = (grad[most:] + last).astype(bf16)


def text_grad_kernel(width_t, *refs):
    imgs, (coef_a, coef_b, part, from_core, t0, t1, t2, t3, t4) = refs[:6], refs[6:]
    most = part.shape[0]
    grad = dot(coef_a[:most + 128, :], imgs[5][:, width_t:]) + from_core[...].astype(f32)
    last = dot(coef_b[:, :128], stack(imgs[:5], slice(width_t, None)), TN)
    at = lambda low, high: part[low:high, :] + grad[low:high]
    t0[...] = at(0, 256)
    t1[0:128, :] = at(256, 384).astype(bf16)
    t1[128:256, :] = at(640, 768).astype(bf16)
    t2[...] = at(384, 640).astype(bf16)
    t3[...] = at(768, 896)
    t4[...] = (grad[most:] + last).astype(bf16)


def image_grad_kernel(width_t, *refs):
    texts, (coef_a, coef_b, part, loss, i0, i1, i2, i3, i4) = refs[:12], refs[12:]
    cols_s = slice(width_t, None)
    grad = part[...] + dot(coef_b[...], stack([texts[5], texts[11]], cols_s))
    i0[...] = grad[0:256]
    i1[0:128, :] = grad[256:384].astype(bf16)
    i1[128:256, :] = grad[640:768].astype(bf16)
    i2[0:256, :] = grad[384:640].astype(bf16)
    i3[...] = grad[768:896]
    i4[...] = dot(coef_a[...], stack(texts, cols_s), TN).astype(bf16)
    for ref in (i1, i2):
        put_pieces(ref, 256, loss[...])


def join(*parts):
    return jnp.concatenate(parts, axis=0)


def put_pieces(ref, row, value):
    ref[row:row + 16, :] = jnp.zeros((16, ref.shape[1]), bf16)
    first = value.astype(bf16)
    second = (value - first.astype(f32)).astype(bf16)
    third = (value - first.astype(f32) - second.astype(f32)).astype(bf16)
    ref[row:row + 16, 0:128] = jnp.concatenate([first, first], axis=0)
    ref[row:row + 16, 128:256] = jnp.concatenate([second, second], axis=0)
    ref[row:row + 16, 256:384] = jnp.concatenate([third, third], axis=0)


def get_pieces(ref, row):
    at = lambda k: ref[row:row + 16, k:k + 128].astype(f32)[:8]
    return at(0) + at(128) + at(256)


def ring_sum_kernel(*refs):
    ins, (loss, loss_x), outs = refs[:10], refs[10:12], refs[12:]
    total_loss = loss[...] + loss_x[...] + get_pieces(ins[6], 256) + get_pieces(ins[7], 256)
    outs[6][...] = total_loss
    for n in range(2):
        (own, one, two, far, from_z), (near, to_z, to_far) = ins[5 * n:5 * n + 5], outs[3 * n:3 * n + 3]
        rows = near.shape[0]
        total = own[...] + one[:2 * rows, :].astype(f32) + two[:2 * rows, :].astype(f32)
        near[...] = total[:rows]
        to_z[:rows, :] = total[rows:].astype(bf16)
        put_pieces(to_z, rows, total_loss)
        to_far[...] = (far[...] + from_z[...].astype(f32)).astype(bf16)


def finish_kernel(
    scale_loss, loss, loss_far, txt, txt_z, txt_x, img, img_z, img_x, si, st, img_out, txt_out, loss_out
):
    rows = txt.shape[0]
    for stud, near, far, ring, out in ((si, img, img_z, img_x, img_out), (st, txt, txt_z, txt_x, txt_out)):
        wide = stud[...].astype(f32)
        norm = norm_of(wide)
        unit = wide / norm
        grad = near[...] + far[:rows, :].astype(f32) + ring[...].astype(f32)
        out[...] = (grad - jnp.sum(grad * unit, axis=-1, keepdims=True) * unit) / norm
    total = (loss[...] + loss_far[...]) + (get_pieces(img_z, rows) + get_pieces(txt_z, rows))
    loss_out[...] = jnp.sum(total, keepdims=True) * scale_loss + jnp.log(2.0)


def body(teacher_image, teacher_text, student_image, student_text):
    rows, width_t = teacher_image.shape
    width_s = student_image.shape[1]
    width = width_t + width_s
    img, txt = call(
        units_kernel, "units", (teacher_image, student_image, teacher_text, student_text),
        [((rows, width), bf16)] * 2,
        far=(teacher_image, student_image, teacher_text, student_text),
    )

    hold = lax.optimization_barrier
    txt_z, img_z, txt_l, img_l = hold((to_text_z(txt), to_image_z(img), to_y(txt, 1), to_x(img, 1)))
    core_1 = to_core(join(txt, txt_z, txt_l))
    txt_r, img_r = to_y(join(txt, txt_z), -1), to_x(join(img, img_z), -1)
    txt_q, img_q = to_y(join(txt_z, txt_l), 1), to_x(join(img_z, img_l), 1)
    imgs, own = [img, img_z, img_l], [txt, txt_z, txt_l]
    other = [core_1[n * rows:(n + 1) * rows] for n in range(3)]
    most, some = 7 * rows, 3 * rows
    near = call(
        functools.partial(near_tile_kernel, width_t), "near_tile", (*imgs, *own, *other),
        [((some, width_s), f32)] * 3 + [((8, 128), f32)],
        flops=2 * some * 2 * some * (width + 2 * width_s),
    )
    txt_r, img_r, txt_q, img_q, near_loss = hold((txt_r, img_r, txt_q, img_q, near[3]))
    near = [*near[:3], near_loss]
    cut = rows // 2
    core_2 = to_core(join(txt_r, txt_q))
    txt_h = [to_y(txt_q[:cut], 1), to_y(txt_r[-cut:], -1)]
    img_h = [to_x(img_q[:cut], 1), to_x(img_r[-cut:], -1)]
    imgs += [img_r, img_q]
    own += [txt_r, txt_q]
    other += [core_2[:2 * rows], core_2[2 * rows:]]
    p_img, p_txt, p_oth, p_loss = call(
        functools.partial(first_tile_kernel, width_t), "first_tile", (*imgs, *own, *other, *near),
        [((most, width_s), f32)] * 3 + [((8, 128), f32)], limit=24,
        flops=2 * (most * 2 * most - some * 2 * some) * (width + 2 * width_s),
        scratch=[((4 * rows, 6 * rows), bf16), ((most, 8 * rows), bf16)],
    )
    txt_h, img_h, p_loss = hold((txt_h, img_h, p_loss))
    txt_h, img_h = join(*txt_h), join(*img_h)
    core_3 = to_core(txt_h)
    pair = 2 * rows
    imgs, texts = [*imgs, img_h], [*own, txt_h, *other, core_3]
    work = 2 * 2 * most * rows
    coef_a, coef_b, loss = call(
        functools.partial(last_coef_kernel, width_t), "last_coef", (*imgs, *texts, p_loss),
        [((2 * (most + rows), rows), bf16), ((most, pair), bf16), ((8, 128), f32)], flops=2 * work * width,
    )
    loss = loss + to_core(loss)
    grad_o = call(
        functools.partial(other_grad_kernel, width_t), "other_grad", (*imgs, coef_a, coef_b, p_oth),
        [((most + rows, width_s), bf16)], flops=work * width_s,
    )[0]
    from_core = to_core(grad_o)
    loss = loss + to_y(loss, 1) + to_y(loss, -1) + to_y(loss, 2)
    sums = [((rows, width_s), f32), ((rows, width_s), bf16)]
    t0, t1, t2, t3, t4 = call(
        functools.partial(text_grad_kernel, width_t), "text_grad", (*imgs, coef_a, coef_b, p_txt, from_core),
        [((pair, width_s), f32)] + [((pair, width_s), bf16)] * 2 + sums, flops=work * width_s,
    )
    i0, i1, i2, i3, i4 = call(
        functools.partial(image_grad_kernel, width_t), "image_grad", (*texts, coef_a, coef_b, p_img, loss),
        [((pair, width_s), f32)] + [((pair + 16, width_s), bf16)] * 2 + sums, flops=2 * work * width_s,
    )
    t1, t2, t4 = to_y(t1, -1), to_y(t2, 1), to_text_z(t4)
    i1, i2, i4 = to_x(i1, -1), to_x(i2, 1), to_image_z(i4)
    loss_x = to_x(loss, 2)
    txt, txt_z, txt_x, img, img_z, img_x, loss = call(
        ring_sum_kernel, "ring_sum", (t0, t1, t2, t3, t4, i0, i1, i2, i3, i4, loss, loss_x),
        [((rows, width_s), f32), ((rows + 16, width_s), bf16), ((rows, width_s), bf16)] * 2 + [((8, 128), f32)],
    )
    txt_x, img_x = to_y(txt_x, 2), to_x(img_x, 2)
    txt_z, img_z, loss_far = to_text_z(txt_z), to_image_z(img_z), to_far_z(loss)
    pairs = float(rows * lax.axis_size("dp") * lax.axis_size("blk"))
    image_grad, text_grad, loss = call(
        functools.partial(finish_kernel, 1.0 / (pairs * pairs)), "finish",
        (loss, loss_far, txt, txt_z, txt_x, img, img_z, img_x, student_image, student_text),
        [((rows, width_s), f32)] * 2 + [((1, 1), f32)],
        keep=False,
    )
    return (image_grad, text_grad, loss.reshape(()))


def solution(mesh):
    spec = P(AXES, None)
    return jax.shard_map(body, mesh=mesh, in_specs=(spec,) * 4, out_specs=(spec, spec, P()), check_vma=False)
```

time: 432 us -> 114 us (0.26)
  waiting for transfers between devices: 283 us -> 47.6 us
  blocking collectives: 71.9 us -> 0 us
  starting transfers between devices: 0.43 us -> 41.8 us
  matrix products: 41.1 us -> 0 us
  Pallas kernels: 0 us -> 22.6 us
  other arithmetic: 17.6 us -> 0.56 us
  between operations: 15.9 us -> 0.88 us
    all_gather x4 -> x0, waiting for transfers between devices: 202 us -> none  [the longest x1 62 us: body(): lax.all_gather(teach_txt, 'dp', axis=0, tiled=True)]
    reduce_scatter x2 -> x0, waiting for transfers between devices: 80.6 us -> none  [the longest x1 80.6 us: body(): grad_txt = lax.psum_scatter(text_acc, 'dp', scatter_dimension=0, tiled=True)]
    psum x1 -> x0, blocking collectives: 71.9 us -> none  [body(): loss_all = lax.psum(loss_sum, ('dp', 'blk'))]
    ppermute x0 -> x32, waiting for transfers between devices: none -> 47.6 us  [permute(): return lax.ppermute(value, AXES, pairs)]
    ppermute x0 -> x32, starting transfers between devices: none -> 41.8 us  [permute(): return lax.ppermute(value, AXES, pairs)]
    dot_general x4 -> x0, matrix products: 41.1 us -> none  [the longest x1 18.1 us: tile_terms(): jnp.dot(rows_t, piece_t.T, preferred_element_type=jnp.float32) * scale_t]
    pallas_call x0 -> x9, Pallas kernels: none -> 22.6 us  [call(): pl.pallas_call(kernel, out_shape=tuple((shape_of(shape, dtype) for shape,...]
    convert_element_type x4 -> x0, other arithmetic: 7.04 us -> none  [the longest x1 1.8 us: body(): teach_img = unit_rows(teacher_image)[0].astype(jnp.bfloat16)]
  transfers between devices with their start and end apart: 6 -> 32, of which waited for: 5 -> 17; matrix products, arithmetic and copies ran while one was open for 7% -> 1% of each run, Pallas kernels for 0% -> 13%
where the time goes in v1:
time: 114 us
  waiting for transfers between devices  47.6 us (42%)
  starting transfers between devices  41.8 us (37%)
  Pallas kernels  22.6 us (20%)
    ppermute x32, waiting for transfers between devices, permute(): return lax.ppermute(value, AXES, pairs)  47.6 us
    ppermute x32, starting transfers between devices, permute(): return lax.ppermute(value, AXES, pairs)  41.8 us
    pallas_call x9, Pallas kernels, call(): pl.pallas_call(kernel, out_shape=tuple((shape_of(shape, dtype) for shape,...  22.6 us
  transfers between devices with their start and end apart: 32, of which 17 were waited for; matrix products, arithmetic and copies ran while one was open for 1% of the time, Pallas kernels for 13%

profile of v1, /device:TPU:0, one launch (start us, length us, event | category | flops | bytes accessed | tf_op | source)
XLA Modules:
  0.0 113.9 jit_solution(16086034208974900030)
XLA Ops:
  0.6 1.6 %units.1 = (bf16[128,1920]{1,0:T(8,128)(2,1)S(1)}, bf16[128,1920]{1,0:T(8,128)(2,1)S(1)}) custom-call(bf16[128,1152]{1,0:T(8,128)(2,1)} %ti.1, bf16[128,768]{1,0:T(8,128)(2,1)} %si.3, bf16[128,1152]{1,0:T(8,128)(2,1)} %tt.1, bf16[128,768]{1,0:T(8,128)(2,1)} %st.3), custom_call_target="tpu_custom_call" | custom-call | bytes 983040 | tf_op jit(solution)/shard_map/units/pallas_call | solution.py:72
  2.2 1.6 %collective-permute-start.3 = (bf16[128,1920]{1,0:T(8,128)(2,1)S(1)}, bf16[128,1920]{1,0:T(8,128)(2,1)S(1)}, u32[]{:S(2)}, u32[]{:S(2)}) collective-permute-start(bf16[128,1920]{1,0:T(8,128)(2,1)S(1)} %get-tuple-element.50.refs_0_), channel_id=1, source_target_pairs={{0,2},{1,3},{2,4},{3,5},{4,6},{5,7},{6,0},{7,1},{8,10},{9,11},{10,... | collective-permute-start | bytes 1474568 | tf_op jit(solution)/shard_map/ppermute | solution.py:31
  3.9 1.9 %collective-permute-start.1 = (bf16[128,1920]{1,0:T(8,128)(2,1)S(1)}, bf16[128,1920]{1,0:T(8,128)(2,1)S(1)}, u32[]{:S(2)}, u32[]{:S(2)}) collective-permute-start(bf16[128,1920]{1,0:T(8,128)(2,1)S(1)} %get-tuple-element.50.refs_0_), channel_id=1, source_target_pairs={{0,1},{1,0},{2,3},{3,2},{4,5},{5,4},{6,7},{7,6},{8,9},{9,8},{10,11... | collective-permute-start | bytes 1474568 | tf_op jit(solution)/shard_map/ppermute | solution.py:31
  5.8 1.6 %collective-permute-start.2 = (bf16[128,1920]{1,0:T(8,128)(2,1)S(1)}, bf16[128,1920]{1,0:T(8,128)(2,1)S(1)}, u32[]{:S(2)}, u32[]{:S(2)}) collective-permute-start(bf16[128,1920]{1,0:T(8,128)(2,1)S(1)} %get-tuple-element.51.refs_3_.refs_5_.refs_6_.refs_0_), channel_id=1, source_target_pairs={{0,16},{1,17},{2,18},{3,19},{4,20},{5,21},{6,22},{7,23},{8,24},{9,... | collective-permute-start | bytes 1474568 | tf_op jit(solution)/shard_map/ppermute | solution.py:31
  7.4 2.5 %collective-permute-start = (bf16[128,1920]{1,0:T(8,128)(2,1)S(1)}, bf16[128,1920]{1,0:T(8,128)(2,1)S(1)}, u32[]{:S(2)}, u32[]{:S(2)}) collective-permute-start(bf16[128,1920]{1,0:T(8,128)(2,1)S(1)} %get-tuple-element.51.refs_3_.refs_5_.refs_6_.refs_0_), channel_id=1, source_target_pairs={{0,65},{1,64},{2,67},{3,66},{4,69},{5,68},{6,71},{7,70},{8,73},{9,... | collective-permute-start | bytes 1474568 | tf_op jit(solution)/shard_map/ppermute | solution.py:31
  9.9 6.5 %collective-permute-done.3.refs_2_ = bf16[128,1920]{1,0:T(8,128)(2,1)S(1)} collective-permute-done((bf16[128,1920]{1,0:T(8,128)(2,1)S(1)}, bf16[128,1920]{1,0:T(8,128)(2,1)S(1)}, u32[]{:S(2)}, u32[]{:S(2)}) %collective-permute-start.3) | collective-permute-done | bytes 491552 | tf_op jit(solution)/shard_map/ppermute | solution.py:31
  16.4 0.4 collective-permute-done.1.refs_1_
  16.7 2.7 %collective-permute-done.2.refs_5_.refs_7_.refs_8_.refs_2_ = bf16[128,1920]{1,0:T(8,128)(2,1)S(1)} collective-permute-done((bf16[128,1920]{1,0:T(8,128)(2,1)S(1)}, bf16[128,1920]{1,0:T(8,128)(2,1)S(1)}, u32[]{:S(2)}, u32[]{:S(2)}) %collective-permute-start.2) | collective-permute-done | bytes 491552 | tf_op jit(solution)/shard_map/ppermute | solution.py:31
  19.5 1.2 %collective-permute-done.refs_4_.refs_6_.refs_7_.refs_1_ = bf16[128,1920]{1,0:T(8,128)(2,1)S(1)} collective-permute-done((bf16[128,1920]{1,0:T(8,128)(2,1)S(1)}, bf16[128,1920]{1,0:T(8,128)(2,1)S(1)}, u32[]{:S(2)}, u32[]{:S(2)}) %collective-permute-start) | collective-permute-done | bytes 491552 | tf_op jit(solution)/shard_map/ppermute | solution.py:31
  20.7 0.1 pad_maximum_fusion.1
  20.8 0.1 collective-permute-start.8
  20.9 0.2 pad_maximum_fusion.5
  21.1 1.6 %collective-permute-start.7 = (bf16[256,1920]{1,0:T(8,128)(2,1)S(1)}, bf16[256,1920]{1,0:T(8,128)(2,1)S(1)}, u32[]{:S(2)}, u32[]{:S(2)}) collective-permute-start(bf16[256,1920]{1,0:T(8,128)(2,1)S(1)} %get-tuple-element.102), channel_id=1, source_target_pairs={{0,2},{1,3},{2,4},{3,5},{4,6},{5,7},{6,0},{7,1},{8,10},{9,11},{10,... | collective-permute-start | bytes 2949128 | tf_op jit(solution)/shard_map/ppermute | solution.py:31
  22.6 1.7 %collective-permute-start.5 = (bf16[256,1920]{1,0:T(8,128)(2,1)S(1)}, bf16[256,1920]{1,0:T(8,128)(2,1)S(1)}, u32[]{:S(2)}, u32[]{:S(2)}) collective-permute-start(bf16[256,1920]{1,0:T(8,128)(2,1)S(1)} %get-tuple-element.103), channel_id=1, source_target_pairs={{0,6},{1,7},{2,0},{3,1},{4,2},{5,3},{6,4},{7,5},{8,14},{9,15},{10,... | collective-permute-start | bytes 2949128 | tf_op jit(solution)/shard_map/ppermute | solution.py:31
  24.4 0.1 pad_maximum_fusion.4
  24.5 1.6 %collective-permute-start.6 = (bf16[256,1920]{1,0:T(8,128)(2,1)S(1)}, bf16[256,1920]{1,0:T(8,128)(2,1)S(1)}, u32[]{:S(2)}, u32[]{:S(2)}) collective-permute-start(bf16[256,1920]{1,0:T(8,128)(2,1)S(1)} %get-tuple-element.104), channel_id=1, source_target_pairs={{0,16},{1,17},{2,18},{3,19},{4,20},{5,21},{6,22},{7,23},{8,24},{9,... | collective-permute-start | bytes 2949128 | tf_op jit(solution)/shard_map/ppermute | solution.py:31
  26.2 1.7 %collective-permute-start.4 = (bf16[256,1920]{1,0:T(8,128)(2,1)S(1)}, bf16[256,1920]{1,0:T(8,128)(2,1)S(1)}, u32[]{:S(2)}, u32[]{:S(2)}) collective-permute-start(bf16[256,1920]{1,0:T(8,128)(2,1)S(1)} %get-tuple-element.105), channel_id=1, source_target_pairs={{0,48},{1,49},{2,50},{3,51},{4,52},{5,53},{6,54},{7,55},{8,56},{9,... | collective-permute-start | bytes 2949128 | tf_op jit(solution)/shard_map/ppermute | solution.py:31
  27.8 0.1 fusion.1
  27.9 2.7 %near_tile.1 = (f32[384,768]{1,0:T(8,128)S(1)}, f32[384,768]{1,0:T(8,128)S(1)}, f32[384,768]{1,0:T(8,128)S(1)}, f32[8,128]{1,0:T(8,128)S(1)}) custom-call(bf16[128,1920]{1,0:T(8,128)(2,1)S(1)} %get-tuple-element.50.refs_0_, bf16[128,1920]{1,0:T(8,128)(2,1)S(1)} %collective-permute-done.1.refs_1_, bf16[128,1920]{1,0:T(8,128)(2,1)S(1)} %collective-permute-done.3.refs_2_, ...), custom_call_target="tpu_custom_call" | custom-call | flops 2038431744 | bytes 4423680 | tf_op jit(solution)/shard_map/near_tile/pallas_call | solution.py:72
  30.6 15.9 %collective-permute-done.7.refs_4_ = bf16[256,1920]{1,0:T(8,128)(2,1)S(1)} collective-permute-done((bf16[256,1920]{1,0:T(8,128)(2,1)S(1)}, bf16[256,1920]{1,0:T(8,128)(2,1)S(1)}, u32[]{:S(2)}, u32[]{:S(2)}) %collective-permute-start.7) | collective-permute-done | bytes 983072 | tf_op jit(solution)/shard_map/ppermute | solution.py:31
  46.5 0.0 collective-permute-done.5.refs_3_
  46.5 2.9 %collective-permute-done.6.refs_9_.refs_10_.refs_4_ = bf16[256,1920]{1,0:T(8,128)(2,1)S(1)} collective-permute-done((bf16[256,1920]{1,0:T(8,128)(2,1)S(1)}, bf16[256,1920]{1,0:T(8,128)(2,1)S(1)}, u32[]{:S(2)}, u32[]{:S(2)}) %collective-permute-start.6) | collective-permute-done | bytes 983072 | tf_op jit(solution)/shard_map/ppermute | solution.py:31
  49.4 0.1 collective-permute-done.4.refs_8_.refs_9_.refs_3_
  49.5 0.1 pad_maximum_fusion
  49.6 0.1 collective-permute-start.13
  49.8 2.9 %collective-permute-start.10 = (bf16[64,1920]{1,0:T(8,128)(2,1)S(1)}, bf16[64,1920]{1,0:T(8,128)(2,1)S(1)}, u32[]{:S(2)}, u32[]{:S(2)}) collective-permute-start(bf16[64,1920]{1,0:T(8,128)(2,1)S(1)} %slice.31), channel_id=1, source_target_pairs={{0,48},{1,49},{2,50},{3,51},{4,52},{5,53},{6,54},{7,55},{8,56},{9,... | collective-permute-start | bytes 737288 | tf_op jit(solution)/shard_map/ppermute | solution.py:31
  52.8 0.3 collective-permute-start.11
  53.1 3.0 %collective-permute-start.12 = (bf16[64,1920]{1,0:T(8,128)(2,1)S(1)}, bf16[64,1920]{1,0:T(8,128)(2,1)S(1)}, u32[]{:S(2)}, u32[]{:S(2)}) collective-permute-start(bf16[64,1920]{1,0:T(8,128)(2,1)S(1)} %slice.33), channel_id=1, source_target_pairs={{0,6},{1,7},{2,0},{3,1},{4,2},{5,3},{6,4},{7,5},{8,14},{9,15},{10,... | collective-permute-start | bytes 737288 | tf_op jit(solution)/shard_map/ppermute | solution.py:31
  56.0 0.1 fusion
  56.2 10.6 %first_tile.1 = (f32[896,768]{1,0:T(8,128)S(1)}, f32[896,768]{1,0:T(8,128)S(1)}, f32[896,768]{1,0:T(8,128)S(1)}, f32[8,128]{1,0:T(8,128)S(1)}) custom-call(bf16[128,1920]{1,0:T(8,128)(2,1)S(1)} %get-tuple-element.50.refs_0_, bf16[128,1920]{1,0:T(8,128)(2,1)S(1)} %collective-permute-done.1.refs_1_, bf16[128,1920]{1,0:T(8,128)(2,1)S(1)} %collective-permute-done.3.refs_2_, ...), custom_call_target="tpu_custom_call" | custom-call | flops 9059696640 | bytes 13864960 | tf_op jit(solution)/shard_map/first_tile/pallas_call | solution.py:72
  66.9 0.3 collective-permute-start.14
  67.2 1.8 %collective-permute-done.14.refs_17_.refs_11_ = bf16[128,1920]{1,0:T(8,128)(2,1)S(1)} collective-permute-done((bf16[128,1920]{1,0:T(8,128)(2,1)S(1)}, bf16[128,1920]{1,0:T(8,128)(2,1)S(1)}, u32[]{:S(2)}, u32[]{:S(2)}) %collective-permute-start.14) | collective-permute-done | bytes 491552 | tf_op jit(solution)/shard_map/ppermute | solution.py:31
  69.0 3.5 %last_coef.1 = (bf16[2048,128]{1,0:T(8,128)(2,1)S(1)}, bf16[896,256]{1,0:T(8,128)(2,1)S(1)}, f32[8,128]{1,0:T(8,128)S(1)}) custom-call(bf16[128,1920]{1,0:T(8,128)(2,1)S(1)} %get-tuple-element.50.refs_0_, bf16[128,1920]{1,0:T(8,128)(2,1)S(1)} %collective-permute-done.1.refs_1_, bf16[128,1920]{1,0:T(8,128)(2,1)S(1)} %collective-permute-done.3.refs_2_, ...), custom_call_target="tpu_custom_call" | custom-call | flops 1761607680 | bytes 11800576 | tf_op jit(solution)/shard_map/last_coef/pallas_call | solution.py:72
  72.5 0.8 other_grad.1
  73.3 0.2 collective-permute-start.15
  73.6 0.4 collective-permute-start.19
  73.9 2.9 %collective-permute-done.19 = f32[8,128]{1,0:T(8,128)S(1)} collective-permute-done((f32[8,128]{1,0:T(8,128)S(1)}, f32[8,128]{1,0:T(8,128)S(1)}, u32[]{:S(2)}, u32[]{:S(2)}) %collective-permute-start.19) | collective-permute-done | bytes 4128 | tf_op jit(solution)/shard_map/ppermute | solution.py:31
  76.8 1.5 %collective-permute-start.22 = (f32[8,128]{1,0:T(8,128)S(1)}, f32[8,128]{1,0:T(8,128)S(1)}, u32[]{:S(2)}, u32[]{:S(2)}) collective-permute-start(f32[8,128]{1,0:T(8,128)S(1)} %add.12), channel_id=1, source_target_pairs={{0,32},{1,33},{2,34},{3,35},{4,36},{5,37},{6,38},{7,39},{8,40},{9,... | collective-permute-start | bytes 12296 | tf_op jit(solution)/shard_map/ppermute | solution.py:31
  78.4 1.7 %collective-permute-start.21 = (f32[8,128]{1,0:T(8,128)S(1)}, f32[8,128]{1,0:T(8,128)S(1)}, u32[]{:S(2)}, u32[]{:S(2)}) collective-permute-start(f32[8,128]{1,0:T(8,128)S(1)} %add.12), channel_id=1, source_target_pairs={{0,48},{1,49},{2,50},{3,51},{4,52},{5,53},{6,54},{7,55},{8,56},{9,... | collective-permute-start | bytes 12296 | tf_op jit(solution)/shard_map/ppermute | solution.py:31
  80.1 0.9 collective-permute-start.20
  80.9 1.0 collective-permute-done.22
  82.0 0.6 collective-permute-done.21
  82.6 2.3 %collective-permute-done.20 = f32[8,128]{1,0:T(8,128)S(1)} collective-permute-done((f32[8,128]{1,0:T(8,128)S(1)}, f32[8,128]{1,0:T(8,128)S(1)}, u32[]{:S(2)}, u32[]{:S(2)}) %collective-permute-start.20) | collective-permute-done | bytes 4128 | tf_op jit(solution)/shard_map/ppermute | solution.py:31
  84.9 0.3 collective-permute-start.26
  85.2 1.0 image_grad.1
  86.2 0.7 collective-permute-start.25
  86.9 1.4 %collective-permute-start.23 = (bf16[272,768]{1,0:T(8,128)(2,1)S(1)}, bf16[272,768]{1,0:T(8,128)(2,1)S(1)}, u32[]{:S(2)}, u32[]{:S(2)}) collective-permute-start(bf16[272,768]{1,0:T(8,128)(2,1)S(1)} %get-tuple-element.83), channel_id=1, source_target_pairs={{0,6},{1,7},{2,0},{3,1},{4,2},{5,3},{6,4},{7,5},{8,14},{9,15},{10,... | collective-permute-start | bytes 1253384 | tf_op jit(solution)/shard_map/ppermute | solution.py:31
  88.3 0.6 collective-permute-start.24
  88.9 0.8 text_grad.1
  89.8 0.4 collective-permute-start.16
  90.2 1.7 %collective-permute-start.17 = (bf16[256,768]{1,0:T(8,128)(2,1)S(1)}, bf16[256,768]{1,0:T(8,128)(2,1)S(1)}, u32[]{:S(2)}, u32[]{:S(2)}) collective-permute-start(bf16[256,768]{1,0:T(8,128)(2,1)S(1)} %get-tuple-element.77), channel_id=1, source_target_pairs={{0,16},{1,17},{2,18},{3,19},{4,20},{5,21},{6,22},{7,23},{8,24},{9,... | collective-permute-start | bytes 1179656 | tf_op jit(solution)/shard_map/ppermute | solution.py:31
  91.9 0.1 collective-permute-done.25.refs_9_
  92.0 2.5 %collective-permute-start.18 = (bf16[128,768]{1,0:T(8,128)(2,1)S(1)}, bf16[128,768]{1,0:T(8,128)(2,1)S(1)}, u32[]{:S(2)}, u32[]{:S(2)}) collective-permute-start(bf16[128,768]{1,0:T(8,128)(2,1)S(1)} %get-tuple-element.79), channel_id=1, source_target_pairs={{0,65},{1,64},{2,67},{3,66},{4,69},{5,68},{6,71},{7,70},{8,73},{9,... | collective-permute-start | bytes 589832 | tf_op jit(solution)/shard_map/ppermute | solution.py:31
  94.5 2.1 %collective-permute-done.23.refs_6_ = bf16[272,768]{1,0:T(8,128)(2,1)S(1)} collective-permute-done((bf16[272,768]{1,0:T(8,128)(2,1)S(1)}, bf16[272,768]{1,0:T(8,128)(2,1)S(1)}, u32[]{:S(2)}, u32[]{:S(2)}) %collective-permute-start.23) | collective-permute-done | bytes 417824 | tf_op jit(solution)/shard_map/ppermute | solution.py:31
  96.6 2.4 %collective-permute-done.24.refs_7_ = bf16[272,768]{1,0:T(8,128)(2,1)S(1)} collective-permute-done((bf16[272,768]{1,0:T(8,128)(2,1)S(1)}, bf16[272,768]{1,0:T(8,128)(2,1)S(1)}, u32[]{:S(2)}, u32[]{:S(2)}) %collective-permute-start.24) | collective-permute-done | bytes 417824 | tf_op jit(solution)/shard_map/ppermute | solution.py:31
  99.0 1.0 collective-permute-done.17.refs_2_
  100.0 0.3 ring_sum.1
  100.4 2.4 %collective-permute-start.28 = (bf16[144,768]{1,0:T(8,128)(2,1)S(1)}, bf16[144,768]{1,0:T(8,128)(2,1)S(1)}, u32[]{:S(2)}, u32[]{:S(2)}) collective-permute-start(bf16[144,768]{1,0:T(8,128)(2,1)S(1)} %get-tuple-element.89), channel_id=1, source_target_pairs={{0,65},{1,64},{2,67},{3,66},{4,69},{5,68},{6,71},{7,70},{8,73},{9,... | collective-permute-start | bytes 663560 | tf_op jit(solution)/shard_map/ppermute | solution.py:31
  102.8 1.0 collective-permute-start.30
  103.8 0.5 collective-permute-start.29
  104.3 3.2 %collective-permute-start.31 = (bf16[128,768]{1,0:T(8,128)(2,1)S(1)}, bf16[128,768]{1,0:T(8,128)(2,1)S(1)}, u32[]{:S(2)}, u32[]{:S(2)}) collective-permute-start(bf16[128,768]{1,0:T(8,128)(2,1)S(1)} %get-tuple-element.93), channel_id=1, source_target_pairs={{0,4},{1,5},{2,6},{3,7},{4,0},{5,1},{6,2},{7,3},{8,12},{9,13},{10,... | collective-permute-start | bytes 589832 | tf_op jit(solution)/shard_map/ppermute | solution.py:31
  107.5 1.4 %collective-permute-start.27 = (f32[8,128]{1,0:T(8,128)S(1)}, f32[8,128]{1,0:T(8,128)S(1)}, u32[]{:S(2)}, u32[]{:S(2)}) collective-permute-start(f32[8,128]{1,0:T(8,128)S(1)} %get-tuple-element.87.loss), channel_id=1, source_target_pairs={{0,64},{1,65},{2,66},{3,67},{4,68},{5,69},{6,70},{7,71},{8,72},{9,... | collective-permute-start | bytes 12296 | tf_op jit(solution)/shard_map/ppermute | solution.py:31
  108.9 3.7 %collective-permute-done.27.loss_far = f32[8,128]{1,0:T(8,128)S(1)} collective-permute-done((f32[8,128]{1,0:T(8,128)S(1)}, f32[8,128]{1,0:T(8,128)S(1)}, u32[]{:S(2)}, u32[]{:S(2)}) %collective-permute-start.27) | collective-permute-done | bytes 4128 | tf_op jit(solution)/shard_map/ppermute | solution.py:31
  112.7 1.3 %finish.1 = (f32[128,768]{1,0:T(8,128)}, f32[128,768]{1,0:T(8,128)}, f32[1,1]{1,0:T(1,128)}) custom-call(f32[8,128]{1,0:T(8,128)S(1)} %get-tuple-element.87.loss, f32[8,128]{1,0:T(8,128)S(1)} %collective-permute-done.27.loss_far, f32[128,768]{1,0:T(8,128)S(1)} %get-tuple-element.88.txt, bf16[144,768]{1,0:T(8,128)(2,1)S(1)} %collective-permute-done.28.txt_z, ...), custom_call_target="tpu_custom_call" | custom-call | bytes 2023424 | tf_op jit(solution)/shard_map/finish/pallas_call | solution.py:72
  (29 shorter events, 0.2 us)
Async XLA Ops:
  2.2 14.1 %collective-permute-start.3 = (bf16[128,1920]{1,0:T(8,128)(2,1)S(1)}, bf16[128,1920]{1,0:T(8,128)(2,1)S(1)}, u32[]{:S(2)}, u32[]{:S(2)}) collective-permute-start(bf16[128,1920]{1,0:T(8,128)(2,1)S(1)} %get-tuple-element.50.refs_0_), channel_id=1, source_target_pairs={{0,2},{1,3},{2,4},{3,5},{4,6},{5,7},{6,0},{7,1},{8,10},{9,11},{10,... | collective-permute-start | bytes 1474568 | tf_op jit(solution)/shard_map/ppermute | solution.py:31
  3.9 12.9 %collective-permute-start.1 = (bf16[128,1920]{1,0:T(8,128)(2,1)S(1)}, bf16[128,1920]{1,0:T(8,128)(2,1)S(1)}, u32[]{:S(2)}, u32[]{:S(2)}) collective-permute-start(bf16[128,1920]{1,0:T(8,128)(2,1)S(1)} %get-tuple-element.50.refs_0_), channel_id=1, source_target_pairs={{0,1},{1,0},{2,3},{3,2},{4,5},{5,4},{6,7},{7,6},{8,9},{9,8},{10,11... | collective-permute-start | bytes 1474568 | tf_op jit(solution)/shard_map/ppermute | solution.py:31
  5.8 13.7 %collective-permute-start.2 = (bf16[128,1920]{1,0:T(8,128)(2,1)S(1)}, bf16[128,1920]{1,0:T(8,128)(2,1)S(1)}, u32[]{:S(2)}, u32[]{:S(2)}) collective-permute-start(bf16[128,1920]{1,0:T(8,128)(2,1)S(1)} %get-tuple-element.51.refs_3_.refs_5_.refs_6_.refs_0_), channel_id=1, source_target_pairs={{0,16},{1,17},{2,18},{3,19},{4,20},{5,21},{6,22},{7,23},{8,24},{9,... | collective-permute-start | bytes 1474568 | tf_op jit(solution)/shard_map/ppermute | solution.py:31
  7.4 13.3 %collective-permute-start = (bf16[128,1920]{1,0:T(8,128)(2,1)S(1)}, bf16[128,1920]{1,0:T(8,128)(2,1)S(1)}, u32[]{:S(2)}, u32[]{:S(2)}) collective-permute-start(bf16[128,1920]{1,0:T(8,128)(2,1)S(1)} %get-tuple-element.51.refs_3_.refs_5_.refs_6_.refs_0_), channel_id=1, source_target_pairs={{0,65},{1,64},{2,67},{3,66},{4,69},{5,68},{6,71},{7,70},{8,73},{9,... | collective-permute-start | bytes 1474568 | tf_op jit(solution)/shard_map/ppermute | solution.py:31
  20.8 7.0 %collective-permute-start.8 = (bf16[384,1920]{1,0:T(8,128)(2,1)S(1)}, bf16[384,1920]{1,0:T(8,128)(2,1)S(1)}, u32[]{:S(2)}, u32[]{:S(2)}) collective-permute-start(bf16[384,1920]{1,0:T(8,128)(2,1)S(1)} %pad_maximum_fusion.1), channel_id=1, source_target_pairs={{0,8},{1,9},{2,10},{3,11},{4,12},{5,13},{6,14},{7,15},{8,0},{9,1},... | collective-permute-start | bytes 4423688 | tf_op jit(solution)/shard_map/ppermute | solution.py:31
  21.1 25.4 %collective-permute-start.7 = (bf16[256,1920]{1,0:T(8,128)(2,1)S(1)}, bf16[256,1920]{1,0:T(8,128)(2,1)S(1)}, u32[]{:S(2)}, u32[]{:S(2)}) collective-permute-start(bf16[256,1920]{1,0:T(8,128)(2,1)S(1)} %get-tuple-element.102), channel_id=1, source_target_pairs={{0,2},{1,3},{2,4},{3,5},{4,6},{5,7},{6,0},{7,1},{8,10},{9,11},{10,... | collective-permute-start | bytes 2949128 | tf_op jit(solution)/shard_map/ppermute | solution.py:31
  22.6 23.9 %collective-permute-start.5 = (bf16[256,1920]{1,0:T(8,128)(2,1)S(1)}, bf16[256,1920]{1,0:T(8,128)(2,1)S(1)}, u32[]{:S(2)}, u32[]{:S(2)}) collective-permute-start(bf16[256,1920]{1,0:T(8,128)(2,1)S(1)} %get-tuple-element.103), channel_id=1, source_target_pairs={{0,6},{1,7},{2,0},{3,1},{4,2},{5,3},{6,4},{7,5},{8,14},{9,15},{10,... | collective-permute-start | bytes 2949128 | tf_op jit(solution)/shard_map/ppermute | solution.py:31
  24.5 24.9 %collective-permute-start.6 = (bf16[256,1920]{1,0:T(8,128)(2,1)S(1)}, bf16[256,1920]{1,0:T(8,128)(2,1)S(1)}, u32[]{:S(2)}, u32[]{:S(2)}) collective-permute-start(bf16[256,1920]{1,0:T(8,128)(2,1)S(1)} %get-tuple-element.104), channel_id=1, source_target_pairs={{0,16},{1,17},{2,18},{3,19},{4,20},{5,21},{6,22},{7,23},{8,24},{9,... | collective-permute-start | bytes 2949128 | tf_op jit(solution)/shard_map/ppermute | solution.py:31
  26.2 23.3 %collective-permute-start.4 = (bf16[256,1920]{1,0:T(8,128)(2,1)S(1)}, bf16[256,1920]{1,0:T(8,128)(2,1)S(1)}, u32[]{:S(2)}, u32[]{:S(2)}) collective-permute-start(bf16[256,1920]{1,0:T(8,128)(2,1)S(1)} %get-tuple-element.105), channel_id=1, source_target_pairs={{0,48},{1,49},{2,50},{3,51},{4,52},{5,53},{6,54},{7,55},{8,56},{9,... | collective-permute-start | bytes 2949128 | tf_op jit(solution)/shard_map/ppermute | solution.py:31
  49.6 6.4 %collective-permute-start.13 = (bf16[512,1920]{1,0:T(8,128)(2,1)S(1)}, bf16[512,1920]{1,0:T(8,128)(2,1)S(1)}, u32[]{:S(2)}, u32[]{:S(2)}) collective-permute-start(bf16[512,1920]{1,0:T(8,128)(2,1)S(1)} %pad_maximum_fusion), channel_id=1, source_target_pairs={{0,8},{1,9},{2,10},{3,11},{4,12},{5,13},{6,14},{7,15},{8,0},{9,1},... | collective-permute-start | bytes 5898248 | tf_op jit(solution)/shard_map/ppermute | solution.py:31
  49.8 16.9 %collective-permute-start.10 = (bf16[64,1920]{1,0:T(8,128)(2,1)S(1)}, bf16[64,1920]{1,0:T(8,128)(2,1)S(1)}, u32[]{:S(2)}, u32[]{:S(2)}) collective-permute-start(bf16[64,1920]{1,0:T(8,128)(2,1)S(1)} %slice.31), channel_id=1, source_target_pairs={{0,48},{1,49},{2,50},{3,51},{4,52},{5,53},{6,54},{7,55},{8,56},{9,... | collective-permute-start | bytes 737288 | tf_op jit(solution)/shard_map/ppermute | solution.py:31
  52.8 14.0 %collective-permute-start.9 = (bf16[64,1920]{1,0:T(8,128)(2,1)S(1)}, bf16[64,1920]{1,0:T(8,128)(2,1)S(1)}, u32[]{:S(2)}, u32[]{:S(2)}) collective-permute-start(bf16[64,1920]{1,0:T(8,128)(2,1)S(1)} %slice.30), channel_id=1, source_target_pairs={{0,16},{1,17},{2,18},{3,19},{4,20},{5,21},{6,22},{7,23},{8,24},{9,... | collective-permute-start | bytes 737288 | tf_op jit(solution)/shard_map/ppermute | solution.py:31
  52.8 14.0 %collective-permute-start.11 = (bf16[64,1920]{1,0:T(8,128)(2,1)S(1)}, bf16[64,1920]{1,0:T(8,128)(2,1)S(1)}, u32[]{:S(2)}, u32[]{:S(2)}) collective-permute-start(bf16[64,1920]{1,0:T(8,128)(2,1)S(1)} %slice.32), channel_id=1, source_target_pairs={{0,2},{1,3},{2,4},{3,5},{4,6},{5,7},{6,0},{7,1},{8,10},{9,11},{10,... | collective-permute-start | bytes 737288 | tf_op jit(solution)/shard_map/ppermute | solution.py:31
  53.1 13.8 %collective-permute-start.12 = (bf16[64,1920]{1,0:T(8,128)(2,1)S(1)}, bf16[64,1920]{1,0:T(8,128)(2,1)S(1)}, u32[]{:S(2)}, u32[]{:S(2)}) collective-permute-start(bf16[64,1920]{1,0:T(8,128)(2,1)S(1)} %slice.33), channel_id=1, source_target_pairs={{0,6},{1,7},{2,0},{3,1},{4,2},{5,3},{6,4},{7,5},{8,14},{9,15},{10,... | collective-permute-start | bytes 737288 | tf_op jit(solution)/shard_map/ppermute | solution.py:31
  66.9 2.2 %collective-permute-start.14 = (bf16[128,1920]{1,0:T(8,128)(2,1)S(1)}, bf16[128,1920]{1,0:T(8,128)(2,1)S(1)}, u32[]{:S(2)}, u32[]{:S(2)}) collective-permute-start(bf16[128,1920]{1,0:T(8,128)(2,1)S(1)} %constant_dynamic-update-slice_fusion.2.refs_11_.refs_5_), channel_id=1, source_target_pairs={{0,8},{1,9},{2,10},{3,11},{4,12},{5,13},{6,14},{7,15},{8,0},{9,1},... | collective-permute-start | bytes 1474568 | tf_op jit(solution)/shard_map/ppermute | solution.py:31
  73.3 15.6 %collective-permute-start.15 = (bf16[1024,768]{1,0:T(8,128)(2,1)S(1)}, bf16[1024,768]{1,0:T(8,128)(2,1)S(1)}, u32[]{:S(2)}, u32[]{:S(2)}) collective-permute-start(bf16[1024,768]{1,0:T(8,128)(2,1)S(1)} %other_grad.1), channel_id=1, source_target_pairs={{0,8},{1,9},{2,10},{3,11},{4,12},{5,13},{6,14},{7,15},{8,0},{9,1},... | collective-permute-start | bytes 4718600 | tf_op jit(solution)/shard_map/ppermute | solution.py:31
  73.6 3.3 %collective-permute-start.19 = (f32[8,128]{1,0:T(8,128)S(1)}, f32[8,128]{1,0:T(8,128)S(1)}, u32[]{:S(2)}, u32[]{:S(2)}) collective-permute-start(f32[8,128]{1,0:T(8,128)S(1)} %get-tuple-element.81), channel_id=1, source_target_pairs={{0,8},{1,9},{2,10},{3,11},{4,12},{5,13},{6,14},{7,15},{8,0},{9,1},... | collective-permute-start | bytes 12296 | tf_op jit(solution)/shard_map/ppermute | solution.py:31
  76.8 5.1 %collective-permute-start.22 = (f32[8,128]{1,0:T(8,128)S(1)}, f32[8,128]{1,0:T(8,128)S(1)}, u32[]{:S(2)}, u32[]{:S(2)}) collective-permute-start(f32[8,128]{1,0:T(8,128)S(1)} %add.12), channel_id=1, source_target_pairs={{0,32},{1,33},{2,34},{3,35},{4,36},{5,37},{6,38},{7,39},{8,40},{9,... | collective-permute-start | bytes 12296 | tf_op jit(solution)/shard_map/ppermute | solution.py:31
  78.4 4.2 %collective-permute-start.21 = (f32[8,128]{1,0:T(8,128)S(1)}, f32[8,128]{1,0:T(8,128)S(1)}, u32[]{:S(2)}, u32[]{:S(2)}) collective-permute-start(f32[8,128]{1,0:T(8,128)S(1)} %add.12), channel_id=1, source_target_pairs={{0,48},{1,49},{2,50},{3,51},{4,52},{5,53},{6,54},{7,55},{8,56},{9,... | collective-permute-start | bytes 12296 | tf_op jit(solution)/shard_map/ppermute | solution.py:31
  80.1 4.8 %collective-permute-start.20 = (f32[8,128]{1,0:T(8,128)S(1)}, f32[8,128]{1,0:T(8,128)S(1)}, u32[]{:S(2)}, u32[]{:S(2)}) collective-permute-start(f32[8,128]{1,0:T(8,128)S(1)} %add.12), channel_id=1, source_target_pairs={{0,16},{1,17},{2,18},{3,19},{4,20},{5,21},{6,22},{7,23},{8,24},{9,... | collective-permute-start | bytes 12296 | tf_op jit(solution)/shard_map/ppermute | solution.py:31
  84.9 5.3 %collective-permute-start.26 = (f32[8,128]{1,0:T(8,128)S(1)}, f32[8,128]{1,0:T(8,128)S(1)}, u32[]{:S(2)}, u32[]{:S(2)}) collective-permute-start(f32[8,128]{1,0:T(8,128)S(1)} %add_add_fusion.refs_15_.refs_10_), channel_id=1, source_target_pairs={{0,4},{1,5},{2,6},{3,7},{4,0},{5,1},{6,2},{7,3},{8,12},{9,13},{10,... | collective-permute-start | bytes 12296 | tf_op jit(solution)/shard_map/ppermute | solution.py:31
  86.2 5.8 %collective-permute-start.25 = (bf16[128,768]{1,0:T(8,128)(2,1)S(1)}, bf16[128,768]{1,0:T(8,128)(2,1)S(1)}, u32[]{:S(2)}, u32[]{:S(2)}) collective-permute-start(bf16[128,768]{1,0:T(8,128)(2,1)S(1)} %get-tuple-element.86), channel_id=1, source_target_pairs={{0,1},{1,0},{2,3},{3,2},{4,5},{5,4},{6,7},{7,6},{8,9},{9,8},{10,11... | collective-permute-start | bytes 589832 | tf_op jit(solution)/shard_map/ppermute | solution.py:31
  86.9 9.7 %collective-permute-start.23 = (bf16[272,768]{1,0:T(8,128)(2,1)S(1)}, bf16[272,768]{1,0:T(8,128)(2,1)S(1)}, u32[]{:S(2)}, u32[]{:S(2)}) collective-permute-start(bf16[272,768]{1,0:T(8,128)(2,1)S(1)} %get-tuple-element.83), channel_id=1, source_target_pairs={{0,6},{1,7},{2,0},{3,1},{4,2},{5,3},{6,4},{7,5},{8,14},{9,15},{10,... | collective-permute-start | bytes 1253384 | tf_op jit(solution)/shard_map/ppermute | solution.py:31
  88.3 10.6 %collective-permute-start.24 = (bf16[272,768]{1,0:T(8,128)(2,1)S(1)}, bf16[272,768]{1,0:T(8,128)(2,1)S(1)}, u32[]{:S(2)}, u32[]{:S(2)}) collective-permute-start(bf16[272,768]{1,0:T(8,128)(2,1)S(1)} %get-tuple-element.84), channel_id=1, source_target_pairs={{0,2},{1,3},{2,4},{3,5},{4,6},{5,7},{6,0},{7,1},{8,10},{9,11},{10,... | collective-permute-start | bytes 1253384 | tf_op jit(solution)/shard_map/ppermute | solution.py:31
  89.8 9.2 %collective-permute-start.16 = (bf16[256,768]{1,0:T(8,128)(2,1)S(1)}, bf16[256,768]{1,0:T(8,128)(2,1)S(1)}, u32[]{:S(2)}, u32[]{:S(2)}) collective-permute-start(bf16[256,768]{1,0:T(8,128)(2,1)S(1)} %get-tuple-element.76), channel_id=1, source_target_pairs={{0,48},{1,49},{2,50},{3,51},{4,52},{5,53},{6,54},{7,55},{8,56},{9,... | collective-permute-start | bytes 1179656 | tf_op jit(solution)/shard_map/ppermute | solution.py:31
  90.2 9.8 %collective-permute-start.17 = (bf16[256,768]{1,0:T(8,128)(2,1)S(1)}, bf16[256,768]{1,0:T(8,128)(2,1)S(1)}, u32[]{:S(2)}, u32[]{:S(2)}) collective-permute-start(bf16[256,768]{1,0:T(8,128)(2,1)S(1)} %get-tuple-element.77), channel_id=1, source_target_pairs={{0,16},{1,17},{2,18},{3,19},{4,20},{5,21},{6,22},{7,23},{8,24},{9,... | collective-permute-start | bytes 1179656 | tf_op jit(solution)/shard_map/ppermute | solution.py:31
  92.0 7.0 %collective-permute-start.18 = (bf16[128,768]{1,0:T(8,128)(2,1)S(1)}, bf16[128,768]{1,0:T(8,128)(2,1)S(1)}, u32[]{:S(2)}, u32[]{:S(2)}) collective-permute-start(bf16[128,768]{1,0:T(8,128)(2,1)S(1)} %get-tuple-element.79), channel_id=1, source_target_pairs={{0,65},{1,64},{2,67},{3,66},{4,69},{5,68},{6,71},{7,70},{8,73},{9,... | collective-permute-start | bytes 589832 | tf_op jit(solution)/shard_map/ppermute | solution.py:31
  100.0 12.6 %copy-start = (bf16[128,768]{1,0:T(8,128)(2,1)S(1)}, bf16[128,768]{1,0:T(8,128)(2,1)}, u32[]{:S(2)}) copy-start(bf16[128,768]{1,0:T(8,128)(2,1)} %si.3) | copy-start | bytes 589828
  100.0 12.6 %copy-start.1 = (bf16[128,768]{1,0:T(8,128)(2,1)S(1)}, bf16[128,768]{1,0:T(8,128)(2,1)}, u32[]{:S(2)}) copy-start(bf16[128,768]{1,0:T(8,128)(2,1)} %st.3) | copy-start | bytes 589828
  100.4 12.3 %collective-permute-start.28 = (bf16[144,768]{1,0:T(8,128)(2,1)S(1)}, bf16[144,768]{1,0:T(8,128)(2,1)S(1)}, u32[]{:S(2)}, u32[]{:S(2)}) collective-permute-start(bf16[144,768]{1,0:T(8,128)(2,1)S(1)} %get-tuple-element.89), channel_id=1, source_target_pairs={{0,65},{1,64},{2,67},{3,66},{4,69},{5,68},{6,71},{7,70},{8,73},{9,... | collective-permute-start | bytes 663560 | tf_op jit(solution)/shard_map/ppermute | solution.py:31
  102.8 9.8 %collective-permute-start.30 = (bf16[144,768]{1,0:T(8,128)(2,1)S(1)}, bf16[144,768]{1,0:T(8,128)(2,1)S(1)}, u32[]{:S(2)}, u32[]{:S(2)}) collective-permute-start(bf16[144,768]{1,0:T(8,128)(2,1)S(1)} %get-tuple-element.92), channel_id=1, source_target_pairs={{0,1},{1,0},{2,3},{3,2},{4,5},{5,4},{6,7},{7,6},{8,9},{9,8},{10,11... | collective-permute-start | bytes 663560 | tf_op jit(solution)/shard_map/ppermute | solution.py:31
  103.8 8.8 %collective-permute-start.29 = (bf16[128,768]{1,0:T(8,128)(2,1)S(1)}, bf16[128,768]{1,0:T(8,128)(2,1)S(1)}, u32[]{:S(2)}, u32[]{:S(2)}) collective-permute-start(bf16[128,768]{1,0:T(8,128)(2,1)S(1)} %get-tuple-element.90), channel_id=1, source_target_pairs={{0,32},{1,33},{2,34},{3,35},{4,36},{5,37},{6,38},{7,39},{8,40},{9,... | collective-permute-start | bytes 589832 | tf_op jit(solution)/shard_map/ppermute | solution.py:31
  104.3 8.3 %collective-permute-start.31 = (bf16[128,768]{1,0:T(8,128)(2,1)S(1)}, bf16[128,768]{1,0:T(8,128)(2,1)S(1)}, u32[]{:S(2)}, u32[]{:S(2)}) collective-permute-start(bf16[128,768]{1,0:T(8,128)(2,1)S(1)} %get-tuple-element.93), channel_id=1, source_target_pairs={{0,4},{1,5},{2,6},{3,7},{4,0},{5,1},{6,2},{7,3},{8,12},{9,13},{10,... | collective-permute-start | bytes 589832 | tf_op jit(solution)/shard_map/ppermute | solution.py:31
  107.5 5.1 %collective-permute-start.27 = (f32[8,128]{1,0:T(8,128)S(1)}, f32[8,128]{1,0:T(8,128)S(1)}, u32[]{:S(2)}, u32[]{:S(2)}) collective-permute-start(f32[8,128]{1,0:T(8,128)S(1)} %get-tuple-element.87.loss), channel_id=1, source_target_pairs={{0,64},{1,65},{2,66},{3,67},{4,68},{5,69},{6,70},{7,71},{8,72},{9,... | collective-permute-start | bytes 12296 | tf_op jit(solution)/shard_map/ppermute | solution.py:31

commit v2 on v1

v2 whole, which is shorter than its diff:
```python
import functools
import itertools

import jax
import jax.numpy as jnp
from jax import lax
from jax.experimental import pallas as pl
from jax.experimental.pallas import tpu as pltpu
from jax.sharding import PartitionSpec as P

eps = 1e-06
scale = 10.0
bias = -2.0
AXES = ("dp", "blk")
f32, bf16 = jnp.float32, jnp.bfloat16

ZH, Y, C, X, ZL = 2, 4, 2, 4, 2
NT = (((1,), (1,)), ((), ()))
TN = (((0,), (0,)), ((), ()))


def place(zh, y, c, x, zl):
    return ((zh * Y + y) * C + c) * (X * ZL) + x * ZL + zl


def permute(value, move):
    pairs = [
        (place(*at), place(*move(*at)))
        for at in itertools.product(range(ZH), range(Y), range(C), range(X), range(ZL))
    ]
    return lax.ppermute(value, AXES, pairs)


def to_x(value, step):
    return permute(value, lambda zh, y, c, x, zl: (zh, y, c, (x + step) % X, zl))


def to_y(value, step):
    return permute(value, lambda zh, y, c, x, zl: (zh, (y + step) % Y, c, x, zl))


def flip_x(value, bits):
    return permute(value, lambda zh, y, c, x, zl: (zh, y, c, x ^ bits, zl))


def flip_y(value, bits):
    return permute(value, lambda zh, y, c, x, zl: (zh, y ^ bits, c, x, zl))


def to_core(value):
    return permute(value, lambda zh, y, c, x, zl: (zh, y, 1 - c, x, zl))


def to_image_z(value):
    return permute(value, lambda zh, y, c, x, zl: (zh, y, c, x, 1 - zl))


def to_text_z(value):
    return permute(value, lambda zh, y, c, x, zl: (1 - zh, y, c, x, 1 - zl))


def to_far_z(value):
    return permute(value, lambda zh, y, c, x, zl: (1 - zh, y, c, x, zl))


def call(kernel, name, args, outs, limit=16, far=(), keep=True, flops=0, scratch=()):
    vmem = pl.BlockSpec(memory_space=pltpu.VMEM)
    near = [
        pltpu.with_memory_space_constraint(v, pltpu.HBM if any(v is w for w in far) else pltpu.VMEM) for v in args
    ]
    shape_of = pltpu.VMEM if keep else jax.ShapeDtypeStruct
    return pl.pallas_call(
        kernel,
        out_shape=tuple(shape_of(shape, dtype) for shape, dtype in outs),
        in_specs=[vmem] * len(args),
        out_specs=(vmem,) * len(outs),
        scratch_shapes=[pltpu.VMEM(shape, dtype) for shape, dtype in scratch],
        compiler_params=pltpu.CompilerParams(vmem_limit_bytes=limit * 2**20),
        cost_estimate=pl.CostEstimate(
            flops=flops, transcendentals=0, bytes_accessed=sum(v.size * v.dtype.itemsize for v in args),
        ),
        name=name,
    )(*near)


def norm_of(wide):
    return jnp.sqrt(jnp.sum(wide * wide, axis=-1, keepdims=True) + eps)


def units_kernel(ti, si, tt, st, img, txt):
    for teach, stud, out in ((ti, si, img), (tt, st, txt)):
        wide = teach[...].astype(f32)
        split = wide.shape[1]
        out[:, :split] = (wide / norm_of(wide)).astype(bf16)
        wide = stud[...].astype(f32)
        out[:, split:] = (wide / norm_of(wide)).astype(bf16)


def tile_terms(cos_t, cos_s):
    half_s = cos_s * (0.5 * scale) + 0.5 * bias
    tanh_t = jnp.tanh(cos_t * (0.5 * scale) + 0.5 * bias)
    tanh_s = jnp.tanh(half_s)
    coef = ((tanh_s - tanh_t) * (0.5 * scale)).astype(bf16)
    left = 1.0 - tanh_s
    for _ in range(3):
        rows = left.shape[0] // 2
        left = left[:rows] * left[rows:]
    line = half_s + half_s * tanh_t
    fold = lambda v: jnp.sum(v.reshape(-1, 8, v.shape[1]), axis=0)
    loss = -(fold(jnp.log(left)) + fold(line))
    return coef, sum(loss[:, k:k + 128] for k in range(0, loss.shape[1], 128))


def stack(refs, cols):
    return jnp.concatenate([r[:, cols] for r in refs], axis=0)


def dot(a, b, dims=(((1,), (0,)), ((), ()))):
    return lax.dot_general(a, b, dims, preferred_element_type=f32)


def near_tile_kernel(width_t, *refs):
    imgs, texts, (g_img, g_txt, g_oth, loss_ref) = refs[:3], refs[3:5], refs[5:]
    cols_t, cols_s = slice(0, width_t), slice(width_t, None)
    img_t, img_s, text_s = stack(imgs, cols_t), stack(imgs, cols_s), stack(texts, cols_s)
    coef, loss = tile_terms(dot(img_t, stack(texts, cols_t), NT), dot(img_s, text_s, NT))
    loss_ref[...] = loss
    g_img[...] = dot(coef, text_s)
    half = g_txt.shape[0]
    g_txt[...] = dot(coef[:, :half], img_s, TN)
    g_oth[...] = dot(coef[:, half:], img_s, TN)


def mid_tile_kernel(width_t, *refs):
    imgs, old, new, refs = refs[:6], refs[6:8], refs[8:10], refs[10:]
    p_img, p_txt, p_oth, p_loss, g_img, g_txt, g_oth, loss_ref = refs
    cols_t, cols_s = slice(0, width_t), slice(width_t, None)
    img_s, add_s = stack(imgs, cols_s), stack(imgs[3:], cols_s)
    old_s, new_s = stack(old, cols_s), stack(new, cols_s)
    coef_i, loss_i = tile_terms(dot(stack(imgs, cols_t), stack(new, cols_t), NT), dot(img_s, new_s, NT))
    coef_t, loss_t = tile_terms(dot(stack(old, cols_t), stack(imgs[3:], cols_t), NT), dot(old_s, add_s, NT))
    loss_ref[...] = p_loss[...] + loss_i + loss_t
    some, half, add = p_img.shape[0], p_txt.shape[0], new[0].shape[0]
    grad = dot(coef_i, new_s)
    g_img[:some, :] = p_img[...] + grad[:some]
    g_img[some:, :] = grad[some:] + dot(coef_t, old_s, TN)
    for n, (part, ref) in enumerate(((p_txt, g_txt), (p_oth, g_oth))):
        ref[:half, :] = part[...] + dot(coef_t[n * half:(n + 1) * half], add_s)
        ref[half:, :] = dot(coef_i[:, n * add:(n + 1) * add], img_s, TN)


def last_coef_kernel(width_t, *refs):
    imgs, texts, last, (p_loss, coef_p, coef_t, loss_ref) = refs[:8], refs[8:12], refs[12], refs[13:]
    cols_t, cols_s = slice(0, width_t), slice(width_t, None)
    late = imgs[6:]
    part, loss_p = tile_terms(
        dot(stack(texts, cols_t), stack(late, cols_t), NT), dot(stack(texts, cols_s), stack(late, cols_s), NT)
    )
    coef_p[...] = part
    part, loss_t = tile_terms(
        dot(stack(imgs, cols_t), last[:, cols_t], NT), dot(stack(imgs, cols_s), last[:, cols_s], NT)
    )
    coef_t[...] = part
    loss_ref[...] = p_loss[...] + loss_p + loss_t


def end_coef_kernel(width_t, *refs):
    imgs, (last, p_loss, coef_u, loss_ref) = refs[:8], refs[8:]
    cols_t, cols_s = slice(0, width_t), slice(width_t, None)
    part, loss = tile_terms(
        dot(stack(imgs, cols_t), last[:, cols_t], NT), dot(stack(imgs, cols_s), last[:, cols_s], NT)
    )
    coef_u[...] = part
    loss_ref[...] = p_loss[...] + loss


def text_grad_kernel(width_t, core, *refs):
    imgs, (coef_p, coef_l, part, out) = refs[:8], refs[8:]
    cols_s = slice(width_t, None)
    most = part.shape[0]
    grad = part[...] + dot(coef_p[core * most:(core + 1) * most, :], stack(imgs[6:], cols_s))
    out[:most, :] = grad.astype(out.dtype)
    out[most:, :] = dot(coef_l[...], stack(imgs, cols_s), TN).astype(out.dtype)


def text_sum_kernel(own, from_core, t0, t1, t2, t3, t4):
    at = lambda low, high: own[low:high, :] + from_core[low:high, :].astype(f32)
    t0[...] = at(0, 256)
    t1[0:128, :] = at(256, 384).astype(bf16)
    t1[128:256, :] = at(640, 768).astype(bf16)
    t2[0:128, :] = at(384, 512).astype(bf16)
    t2[128:256, :] = at(768, 896).astype(bf16)
    t3[...] = at(512, 640)
    t4[...] = at(896, 1024).astype(bf16)


def image_grad_kernel(width_t, *refs):
    texts, last_t, last_u = refs[:4], refs[4], refs[5]
    coef_p, coef_t, coef_u, part, loss, i0, i1, i2, i3, i4 = refs[6:]
    cols_s = slice(width_t, None)
    most = part.shape[0]
    grad = dot(coef_t[...], last_t[:, cols_s]) + dot(coef_u[...], last_u[:, cols_s])
    early = part[...] + grad[:most]
    late = grad[most:] + dot(coef_p[...], stack(texts, cols_s), TN)
    i0[...] = early[0:256]
    i1[0:128, :] = early[256:384].astype(bf16)
    i1[128:256, :] = early[512:640].astype(bf16)
    i2[0:128, :] = early[640:768].astype(bf16)
    i2[128:256, :] = late[0:128].astype(bf16)
    i3[...] = early[384:512]
    i4[...] = late[128:256].astype(bf16)
    for ref in (i1, i2):
        put_pieces(ref, 256, loss[...])


def join(*parts):
    return jnp.concatenate(parts, axis=0)


def put_pieces(ref, row, value):
    ref[row:row + 16, :] = jnp.zeros((16, ref.shape[1]), bf16)
    first = value.astype(bf16)
    second = (value - first.astype(f32)).astype(bf16)
    third = (value - first.astype(f32) - second.astype(f32)).astype(bf16)
    ref[row:row + 16, 0:128] = jnp.concatenate([first, first], axis=0)
    ref[row:row + 16, 128:256] = jnp.concatenate([second, second], axis=0)
    ref[row:row + 16, 256:384] = jnp.concatenate([third, third], axis=0)


def get_pieces(ref, row):
    at = lambda k: ref[row:row + 16, k:k + 128].astype(f32)[:8]
    return at(0) + at(128) + at(256)


def image_sum_kernel(own, one, two, far, from_z, loss, loss_x, near, to_z, to_far, loss_out):
    rows = near.shape[0]
    loss_out[...] = loss[...] + loss_x[...] + get_pieces(one, 2 * rows) + get_pieces(two, 2 * rows)
    ring_sum(own, one, two, far, from_z, loss_out, near, to_z, to_far)


def ring_sum(own, one, two, far, from_z, loss, near, to_z, to_far):
    rows = near.shape[0]
    total = own[...] + one[:2 * rows, :].astype(f32) + two[:2 * rows, :].astype(f32)
    near[...] = total[:rows]
    to_z[:rows, :] = total[rows:].astype(bf16)
    put_pieces(to_z, rows, loss[...])
    to_far[...] = (far[...] + from_z[...].astype(f32)).astype(bf16)


def finish_kernel(
    scale_loss, loss, loss_far, txt, txt_z, txt_x, img, img_z, img_x, si, st, img_out, txt_out, loss_out
):
    rows = txt.shape[0]
    for stud, near, far, ring, out in ((si, img, img_z, img_x, img_out), (st, txt, txt_z, txt_x, txt_out)):
        wide = stud[...].astype(f32)
        norm = norm_of(wide)
        unit = wide / norm
        grad = near[...] + far[:rows, :].astype(f32) + ring[...].astype(f32)
        out[...] = (grad - jnp.sum(grad * unit, axis=-1, keepdims=True) * unit) / norm
    total = (loss[...] + loss_far[...]) + (get_pieces(img_z, rows) + get_pieces(txt_z, rows))
    loss_out[...] = jnp.sum(total, keepdims=True) * scale_loss + jnp.log(2.0)


def body(teacher_image, teacher_text, student_image, student_text):
    rows, width_t = teacher_image.shape
    width_s = student_image.shape[1]
    width = width_t + width_s
    img, txt = call(
        units_kernel, "units", (teacher_image, student_image, teacher_text, student_text),
        [((rows, width), bf16)] * 2,
        far=(teacher_image, student_image, teacher_text, student_text),
    )

    hold = lax.optimization_barrier
    run = functools.partial
    txt_l, img_l, txt_z, img_z = to_y(txt, 1), to_x(img, 1), to_text_z(txt), to_image_z(img)
    txt_r = to_y(txt, -1)
    txt_o, img_o = to_y(txt_l, 1), to_x(img_l, 1)
    txt_zl, img_zl = to_text_z(hold((txt_l, txt_z))[0]), to_image_z(hold((img_l, img_z))[0])
    img_r = to_x(hold((img, img_z))[0], -1)
    txt_zo, img_zo = to_text_z(txt_o), to_image_z(img_o)
    txt_zr, img_zr = to_y(hold((txt_z, txt_zl))[0], -1), to_x(hold((img_z, img_zl))[0], -1)
    txt_o, img_o, txt_zl, img_zl, img_r, txt_z, txt_l, txt_r = hold((txt_o, img_o, txt_zl, img_zl, img_r, txt_z, txt_l, txt_r))
    txt_1 = join(txt, txt_z, txt_l, txt_r)
    oth_1 = to_core(txt_1)
    pair_work = 2 * (width + 2 * width_s)
    grads = lambda *sizes: [((size * rows, width_s), f32) for size in sizes] + [((8, 128), f32)]
    imgs = [img, img_z, img_l]
    p_img, p_txt, p_oth, p_loss = call(
        run(near_tile_kernel, width_t), "near_tile", (*imgs, txt_1, oth_1), grads(3, 4, 4),
        flops=24 * rows * rows * pair_work,
    )
    txt_2 = join(txt_o, txt_zl)
    oth_2 = to_core(txt_2)
    imgs += [img_o, img_zl, img_r]
    p_img, p_txt, p_oth, p_loss = call(
        run(mid_tile_kernel, width_t), "mid_tile", (*imgs, txt_1, oth_1, txt_2, oth_2, p_img, p_txt, p_oth, p_loss),
        grads(6, 6, 6), limit=20, flops=48 * rows * rows * pair_work,
    )
    txt_zr, txt_zo, img_zo, img_zr, p_loss = hold((txt_zr, txt_zo, img_zo, img_zr, p_loss))
    txt_n = join(txt_zr, txt_zo)
    oth_n = to_core(txt_n)
    imgs += [img_zr, img_zo]
    texts = [txt_1, txt_2, oth_1, oth_2]
    coef_p, coef_t, loss = call(
        run(last_coef_kernel, width_t), "last_coef", (*imgs, *texts, txt_n, p_loss),
        [((12 * rows, 2 * rows), bf16), ((8 * rows, 2 * rows), bf16), ((8, 128), f32)], limit=24,
        flops=2 * (24 + 16) * rows * rows * width,
    )
    coef_u, loss = call(
        run(end_coef_kernel, width_t), "end_coef", (*imgs, oth_n, loss),
        [((8 * rows, 2 * rows), bf16), ((8, 128), f32)], flops=2 * 16 * rows * rows * width,
    )
    loss_core = to_core(loss)
    grad_work = 2 * (12 + 16) * rows * rows * width_s
    grad_o = call(
        run(text_grad_kernel, width_t, 1), "other_grad", (*imgs, coef_p, coef_u, p_oth),
        [((8 * rows, width_s), bf16)], flops=grad_work,
    )[0]
    grad_o, loss_core = hold((grad_o, loss_core))
    from_core = to_core(grad_o)
    loss = loss + loss_core
    loss = loss + to_y(loss, 1) + to_y(loss, -1) + to_y(loss, 2)
    pair = 2 * rows
    sums = [((rows, width_s), f32), ((rows, width_s), bf16)]
    grad_t = call(
        run(text_grad_kernel, width_t, 0), "text_grad", (*imgs, coef_p, coef_t, p_txt),
        [((8 * rows, width_s), f32)], flops=grad_work,
    )[0]
    t0, t1, t2, t3, t4 = call(
        text_sum_kernel, "text_sum", (grad_t, from_core),
        [((pair, width_s), f32)] + [((pair, width_s), bf16)] * 2 + sums,
    )
    i0, i1, i2, i3, i4 = call(
        run(image_grad_kernel, width_t), "image_grad", (*texts, txt_n, oth_n, coef_p, coef_t, coef_u, p_img, loss),
        [((pair, width_s), f32)] + [((pair + 16, width_s), bf16)] * 2 + sums, flops=2 * grad_work,
    )
    loss_x = to_x(loss, 2)
    i4, i1, i2 = to_image_z(i4), to_x(i1, -1), to_x(i2, 1)
    t1, t2, t4 = to_y(t1, -1), to_y(t2, 1), to_text_z(t4)
    parts = [((rows, width_s), f32), ((rows + 16, width_s), bf16), ((rows, width_s), bf16)]
    img, img_z, img_x, loss = call(
        image_sum_kernel, "image_sum", (i0, i1, i2, i3, i4, loss, loss_x), parts + [((8, 128), f32)],
    )
    txt, txt_z, txt_x = call(ring_sum, "text_ring_sum", (t0, t1, t2, t3, t4, loss), parts)
    txt_x, img_x = to_y(txt_x, 2), to_x(img_x, 2)
    txt_z, img_z, loss_far = to_text_z(txt_z), to_image_z(img_z), to_far_z(loss)
    pairs = float(rows * lax.axis_size("dp") * lax.axis_size("blk"))
    image_grad, text_grad, loss = call(
        functools.partial(finish_kernel, 1.0 / (pairs * pairs)), "finish",
        (loss, loss_far, txt, txt_z, txt_x, img, img_z, img_x, student_image, student_text),
        [((rows, width_s), f32)] * 2 + [((1, 1), f32)],
        keep=False,
    )
    return (image_grad, text_grad, loss.reshape(()))


def solution(mesh):
    spec = P(AXES, None)
    return jax.shard_map(body, mesh=mesh, in_specs=(spec,) * 4, out_specs=(spec, spec, P()), check_vma=False)
```

time: 114 us -> 102 us (0.89)
  waiting for transfers between devices: 47.6 us -> 34.8 us
  starting transfers between devices: 41.8 us -> 43 us
    ppermute x32 -> x34, waiting for transfers between devices: 47.6 us -> 34.8 us  [permute(): return lax.ppermute(value, AXES, pairs)]
    ppermute x32 -> x34, starting transfers between devices: 41.8 us -> 43 us  [permute(): return lax.ppermute(value, AXES, pairs)]
    pallas_call x9 -> x12, Pallas kernels: 22.6 us -> 22.7 us  [call(): pl.pallas_call(kernel, out_shape=tuple((shape_of(shape, dtype) for shape,...]
  transfers between devices with their start and end apart: 32 -> 34, of which waited for: 17 -> 14; matrix products, arithmetic and copies ran while one was open for 1% -> 0% of each run, Pallas kernels for 13% -> 18%
where the time goes in v2:
time: 102 us
  starting transfers between devices  43 us (42%)
  waiting for transfers between devices  34.8 us (34%)
  Pallas kernels  22.7 us (22%)
    ppermute x34, starting transfers between devices, permute(): return lax.ppermute(value, AXES, pairs)  43 us
    ppermute x34, waiting for transfers between devices, permute(): return lax.ppermute(value, AXES, pairs)  34.8 us
    pallas_call x12, Pallas kernels, call(): pl.pallas_call(kernel, out_shape=tuple((shape_of(shape, dtype) for shape,...  22.7 us
  transfers between devices with their start and end apart: 34, of which 14 were waited for; matrix products, arithmetic and copies ran while one was open for 0% of the time, Pallas kernels for 18%

profile of v2, /device:TPU:0, one launch (start us, length us, event | category | flops | bytes accessed | tf_op | source)
XLA Modules:
  0.0 101.7 jit_solution(2505505240741819859)
XLA Ops:
  0.6 1.6 %units.1 = (bf16[128,1920]{1,0:T(8,128)(2,1)S(1)}, bf16[128,1920]{1,0:T(8,128)(2,1)S(1)}) custom-call(bf16[128,1152]{1,0:T(8,128)(2,1)} %ti.1, bf16[128,768]{1,0:T(8,128)(2,1)} %si.3, bf16[128,1152]{1,0:T(8,128)(2,1)} %tt.1, bf16[128,768]{1,0:T(8,128)(2,1)} %st.3), custom_call_target="tpu_custom_call" | custom-call | bytes 983040 | tf_op jit(solution)/shard_map/units/pallas_call | solution.py:72
  2.2 1.7 %collective-permute-start = (bf16[128,1920]{1,0:T(8,128)(2,1)S(1)}, bf16[128,1920]{1,0:T(8,128)(2,1)S(1)}, u32[]{:S(2)}, u32[]{:S(2)}) collective-permute-start(bf16[128,1920]{1,0:T(8,128)(2,1)S(1)} %get-tuple-element.58), channel_id=1, source_target_pairs={{0,16},{1,17},{2,18},{3,19},{4,20},{5,21},{6,22},{7,23},{8,24},{9,... | collective-permute-start | bytes 1474568 | tf_op jit(solution)/shard_map/ppermute | solution.py:31
  3.9 4.0 %collective-permute-start.4 = (bf16[128,1920]{1,0:T(8,128)(2,1)S(1)}, bf16[128,1920]{1,0:T(8,128)(2,1)S(1)}, u32[]{:S(2)}, u32[]{:S(2)}) collective-permute-start(bf16[128,1920]{1,0:T(8,128)(2,1)S(1)} %get-tuple-element.58), channel_id=1, source_target_pairs={{0,65},{1,64},{2,67},{3,66},{4,69},{5,68},{6,71},{7,70},{8,73},{9,... | collective-permute-start | bytes 1474568 | tf_op jit(solution)/shard_map/ppermute | solution.py:31
  8.0 1.5 %collective-permute-start.2 = (bf16[128,1920]{1,0:T(8,128)(2,1)S(1)}, bf16[128,1920]{1,0:T(8,128)(2,1)S(1)}, u32[]{:S(2)}, u32[]{:S(2)}) collective-permute-start(bf16[128,1920]{1,0:T(8,128)(2,1)S(1)} %get-tuple-element.62.refs_0_), channel_id=1, source_target_pairs={{0,2},{1,3},{2,4},{3,5},{4,6},{5,7},{6,0},{7,1},{8,10},{9,11},{10,... | collective-permute-start | bytes 1474568 | tf_op jit(solution)/shard_map/ppermute | solution.py:31
  9.5 1.7 %collective-permute-start.9 = (bf16[128,1920]{1,0:T(8,128)(2,1)S(1)}, bf16[128,1920]{1,0:T(8,128)(2,1)S(1)}, u32[]{:S(2)}, u32[]{:S(2)}) collective-permute-start(bf16[128,1920]{1,0:T(8,128)(2,1)S(1)} %get-tuple-element.58), channel_id=1, source_target_pairs={{0,48},{1,49},{2,50},{3,51},{4,52},{5,53},{6,54},{7,55},{8,56},{9,... | collective-permute-start | bytes 1474568 | tf_op jit(solution)/shard_map/ppermute | solution.py:31
  11.1 5.5 %collective-permute-done = bf16[128,1920]{1,0:T(8,128)(2,1)S(1)} collective-permute-done((bf16[128,1920]{1,0:T(8,128)(2,1)S(1)}, bf16[128,1920]{1,0:T(8,128)(2,1)S(1)}, u32[]{:S(2)}, u32[]{:S(2)}) %collective-permute-start) | collective-permute-done | bytes 491552 | tf_op jit(solution)/shard_map/ppermute | solution.py:31
  16.6 2.3 %collective-permute-done.4 = bf16[128,1920]{1,0:T(8,128)(2,1)S(1)} collective-permute-done((bf16[128,1920]{1,0:T(8,128)(2,1)S(1)}, bf16[128,1920]{1,0:T(8,128)(2,1)S(1)}, u32[]{:S(2)}, u32[]{:S(2)}) %collective-permute-start.4) | collective-permute-done | bytes 491552 | tf_op jit(solution)/shard_map/ppermute | solution.py:31
  18.9 3.0 %collective-permute-start.5 = (bf16[128,1920]{1,0:T(8,128)(2,1)S(1)}, bf16[128,1920]{1,0:T(8,128)(2,1)S(1)}, u32[]{:S(2)}, u32[]{:S(2)}) collective-permute-start(bf16[128,1920]{1,0:T(8,128)(2,1)S(1)} %collective-permute-done), channel_id=1, source_target_pairs={{0,65},{1,64},{2,67},{3,66},{4,69},{5,68},{6,71},{7,70},{8,73},{9,... | collective-permute-start | bytes 1474568 | tf_op jit(solution)/shard_map/ppermute | solution.py:31
  21.9 0.0 collective-permute-done.2.refs_2_
  21.9 0.0 collective-permute-done.6.refs_1_
  21.9 0.0 collective-permute-start.7
  21.9 1.6 %collective-permute-start.1 = (bf16[128,1920]{1,0:T(8,128)(2,1)S(1)}, bf16[128,1920]{1,0:T(8,128)(2,1)S(1)}, u32[]{:S(2)}, u32[]{:S(2)}) collective-permute-start(bf16[128,1920]{1,0:T(8,128)(2,1)S(1)} %collective-permute-done), channel_id=1, source_target_pairs={{0,16},{1,17},{2,18},{3,19},{4,20},{5,21},{6,22},{7,23},{8,24},{9,... | collective-permute-start | bytes 1474568 | tf_op jit(solution)/shard_map/ppermute | solution.py:31
  23.5 1.5 %collective-permute-start.3 = (bf16[128,1920]{1,0:T(8,128)(2,1)S(1)}, bf16[128,1920]{1,0:T(8,128)(2,1)S(1)}, u32[]{:S(2)}, u32[]{:S(2)}) collective-permute-start(bf16[128,1920]{1,0:T(8,128)(2,1)S(1)} %collective-permute-done.2.refs_2_), channel_id=1, source_target_pairs={{0,2},{1,3},{2,4},{3,5},{4,6},{5,7},{6,0},{7,1},{8,10},{9,11},{10,... | collective-permute-start | bytes 1474568 | tf_op jit(solution)/shard_map/ppermute | solution.py:31
  25.0 1.7 %collective-permute-start.8 = (bf16[128,1920]{1,0:T(8,128)(2,1)S(1)}, bf16[128,1920]{1,0:T(8,128)(2,1)S(1)}, u32[]{:S(2)}, u32[]{:S(2)}) collective-permute-start(bf16[128,1920]{1,0:T(8,128)(2,1)S(1)} %get-tuple-element.62.refs_0_), channel_id=1, source_target_pairs={{0,6},{1,7},{2,0},{3,1},{4,2},{5,3},{6,4},{7,5},{8,14},{9,15},{10,... | collective-permute-start | bytes 1474568 | tf_op jit(solution)/shard_map/ppermute | solution.py:31
  26.8 7.8 %collective-permute-done.1 = bf16[128,1920]{1,0:T(8,128)(2,1)S(1)} collective-permute-done((bf16[128,1920]{1,0:T(8,128)(2,1)S(1)}, bf16[128,1920]{1,0:T(8,128)(2,1)S(1)}, u32[]{:S(2)}, u32[]{:S(2)}) %collective-permute-start.1) | collective-permute-done | bytes 491552 | tf_op jit(solution)/shard_map/ppermute | solution.py:31
  34.7 1.3 %collective-permute-done.3.refs_3_ = bf16[128,1920]{1,0:T(8,128)(2,1)S(1)} collective-permute-done((bf16[128,1920]{1,0:T(8,128)(2,1)S(1)}, bf16[128,1920]{1,0:T(8,128)(2,1)S(1)}, u32[]{:S(2)}, u32[]{:S(2)}) %collective-permute-start.3) | collective-permute-done | bytes 491552 | tf_op jit(solution)/shard_map/ppermute | solution.py:31
  36.0 0.0 collective-permute-done.5
  36.0 0.0 collective-permute-done.7.refs_4_
  36.0 0.0 collective-permute-done.8.refs_5_
  36.1 0.1 collective-permute-start.10
  36.3 0.6 collective-permute-start.11
  36.9 1.7 %collective-permute-start.12 = (bf16[128,1920]{1,0:T(8,128)(2,1)S(1)}, bf16[128,1920]{1,0:T(8,128)(2,1)S(1)}, u32[]{:S(2)}, u32[]{:S(2)}) collective-permute-start(bf16[128,1920]{1,0:T(8,128)(2,1)S(1)} %collective-permute-done.4), channel_id=1, source_target_pairs={{0,48},{1,49},{2,50},{3,51},{4,52},{5,53},{6,54},{7,55},{8,56},{9,... | collective-permute-start | bytes 1474568 | tf_op jit(solution)/shard_map/ppermute | solution.py:31
  38.6 2.9 %collective-permute-start.15 = (bf16[128,1920]{1,0:T(8,128)(2,1)S(1)}, bf16[128,1920]{1,0:T(8,128)(2,1)S(1)}, u32[]{:S(2)}, u32[]{:S(2)}) collective-permute-start(bf16[128,1920]{1,0:T(8,128)(2,1)S(1)} %collective-permute-done.6.refs_1_), channel_id=1, source_target_pairs={{0,6},{1,7},{2,0},{3,1},{4,2},{5,3},{6,4},{7,5},{8,14},{9,15},{10,... | collective-permute-start | bytes 1474568 | tf_op jit(solution)/shard_map/ppermute | solution.py:31
  41.5 0.6 collective-permute-start.13
  42.1 0.0 collective-permute-done.10.refs_4_.refs_7_.refs_10_.refs_2_
  42.1 1.1 %collective-permute-start.14 = (bf16[128,1920]{1,0:T(8,128)(2,1)S(1)}, bf16[128,1920]{1,0:T(8,128)(2,1)S(1)}, u32[]{:S(2)}, u32[]{:S(2)}) collective-permute-start(bf16[128,1920]{1,0:T(8,128)(2,1)S(1)} %collective-permute-done.3.refs_3_), channel_id=1, source_target_pairs={{0,1},{1,0},{2,3},{3,2},{4,5},{5,4},{6,7},{7,6},{8,9},{9,8},{10,11... | collective-permute-start | bytes 1474568 | tf_op jit(solution)/shard_map/ppermute | solution.py:31
  43.2 3.5 %near_tile.1 = (f32[384,768]{1,0:T(8,128)S(1)}, f32[512,768]{1,0:T(8,128)S(1)}, f32[512,768]{1,0:T(8,128)S(1)}, f32[8,128]{1,0:T(8,128)S(1)}) custom-call(bf16[128,1920]{1,0:T(8,128)(2,1)S(1)} %get-tuple-element.62.refs_0_, bf16[128,1920]{1,0:T(8,128)(2,1)S(1)} %collective-permute-done.6.refs_1_, bf16[128,1920]{1,0:T(8,128)(2,1)S(1)} %collective-permute-done.2.refs_2_, ...), custom_call_target="tpu_custom_call" | custom-call | flops 2717908992 | bytes 5406720 | tf_op jit(solution)/shard_map/near_tile/pallas_call | solution.py:72
  46.7 7.1 %mid_tile.1 = (f32[768,768]{1,0:T(8,128)S(1)}, f32[768,768]{1,0:T(8,128)S(1)}, f32[768,768]{1,0:T(8,128)S(1)}, f32[8,128]{1,0:T(8,128)S(1)}) custom-call(bf16[128,1920]{1,0:T(8,128)(2,1)S(1)} %get-tuple-element.62.refs_0_, bf16[128,1920]{1,0:T(8,128)(2,1)S(1)} %collective-permute-done.6.refs_1_, bf16[128,1920]{1,0:T(8,128)(2,1)S(1)} %collective-permute-done.2.refs_2_, ...), custom_call_target="tpu_custom_call" | custom-call | flops 5435817984 | bytes 13176832 | tf_op jit(solution)/shard_map/mid_tile/pallas_call | solution.py:72
  53.8 1.6 %collective-permute-done.13 = bf16[128,1920]{1,0:T(8,128)(2,1)S(1)} collective-permute-done((bf16[128,1920]{1,0:T(8,128)(2,1)S(1)}, bf16[128,1920]{1,0:T(8,128)(2,1)S(1)}, u32[]{:S(2)}, u32[]{:S(2)}) %collective-permute-start.13) | collective-permute-done | bytes 491552 | tf_op jit(solution)/shard_map/ppermute | solution.py:31
  55.5 0.3 collective-permute-start.16
  55.8 3.4 %last_coef.1 = (bf16[1536,256]{1,0:T(8,128)(2,1)S(1)}, bf16[1024,256]{1,0:T(8,128)(2,1)S(1)}, f32[8,128]{1,0:T(8,128)S(1)}) custom-call(bf16[128,1920]{1,0:T(8,128)(2,1)S(1)} %get-tuple-element.62.refs_0_, bf16[128,1920]{1,0:T(8,128)(2,1)S(1)} %collective-permute-done.6.refs_1_, bf16[128,1920]{1,0:T(8,128)(2,1)S(1)} %collective-permute-done.2.refs_2_, ...), custom_call_target="tpu_custom_call" | custom-call | flops 2516582400 | bytes 10817536 | tf_op jit(solution)/shard_map/last_coef/pallas_call | solution.py:72
  59.2 1.5 %end_coef.1 = (bf16[1024,256]{1,0:T(8,128)(2,1)S(1)}, f32[8,128]{1,0:T(8,128)S(1)}) custom-call(bf16[128,1920]{1,0:T(8,128)(2,1)S(1)} %get-tuple-element.62.refs_0_, bf16[128,1920]{1,0:T(8,128)(2,1)S(1)} %collective-permute-done.6.refs_1_, bf16[128,1920]{1,0:T(8,128)(2,1)S(1)} %collective-permute-done.2.refs_2_, ...), custom_call_target="tpu_custom_call" | custom-call | flops 1006632960 | bytes 4919296 | tf_op jit(solution)/shard_map/end_coef/pallas_call | solution.py:72
  60.8 0.6 collective-permute-start.17
  61.3 0.9 other_grad.1
  62.3 0.2 collective-permute-start.26
  62.5 1.7 %collective-permute-start.20 = (f32[8,128]{1,0:T(8,128)S(1)}, f32[8,128]{1,0:T(8,128)S(1)}, u32[]{:S(2)}, u32[]{:S(2)}) collective-permute-start(f32[8,128]{1,0:T(8,128)S(1)} %add.12), channel_id=1, source_target_pairs={{0,32},{1,33},{2,34},{3,35},{4,36},{5,37},{6,38},{7,39},{8,40},{9,... | collective-permute-start | bytes 12296 | tf_op jit(solution)/shard_map/ppermute | solution.py:31
  64.2 1.3 %collective-permute-start.19 = (f32[8,128]{1,0:T(8,128)S(1)}, f32[8,128]{1,0:T(8,128)S(1)}, u32[]{:S(2)}, u32[]{:S(2)}) collective-permute-start(f32[8,128]{1,0:T(8,128)S(1)} %add.12), channel_id=1, source_target_pairs={{0,48},{1,49},{2,50},{3,51},{4,52},{5,53},{6,54},{7,55},{8,56},{9,... | collective-permute-start | bytes 12296 | tf_op jit(solution)/shard_map/ppermute | solution.py:31
  65.6 0.7 collective-permute-start.18
  66.2 1.4 %collective-permute-done.20 = f32[8,128]{1,0:T(8,128)S(1)} collective-permute-done((f32[8,128]{1,0:T(8,128)S(1)}, f32[8,128]{1,0:T(8,128)S(1)}, u32[]{:S(2)}, u32[]{:S(2)}) %collective-permute-start.20) | collective-permute-done | bytes 4128 | tf_op jit(solution)/shard_map/ppermute | solution.py:31
  67.6 0.2 collective-permute-done.19
  67.8 2.6 %collective-permute-done.18 = f32[8,128]{1,0:T(8,128)S(1)} collective-permute-done((f32[8,128]{1,0:T(8,128)S(1)}, f32[8,128]{1,0:T(8,128)S(1)}, u32[]{:S(2)}, u32[]{:S(2)}) %collective-permute-start.18) | collective-permute-done | bytes 4128 | tf_op jit(solution)/shard_map/ppermute | solution.py:31
  70.4 1.7 %collective-permute-start.24 = (f32[8,128]{1,0:T(8,128)S(1)}, f32[8,128]{1,0:T(8,128)S(1)}, u32[]{:S(2)}, u32[]{:S(2)}) collective-permute-start(f32[8,128]{1,0:T(8,128)S(1)} %add_add_fusion.refs_10_.loss), channel_id=1, source_target_pairs={{0,4},{1,5},{2,6},{3,7},{4,0},{5,1},{6,2},{7,3},{8,12},{9,13},{10,... | collective-permute-start | bytes 12296 | tf_op jit(solution)/shard_map/ppermute | solution.py:31
  72.1 1.7 %image_grad.1 = (f32[256,768]{1,0:T(8,128)S(1)}, bf16[272,768]{1,0:T(8,128)(2,1)S(1)}, bf16[272,768]{1,0:T(8,128)(2,1)S(1)}, f32[128,768]{1,0:T(8,128)S(1)}, bf16[128,768]{1,0:T(8,128)(2,1)S(1)}) custom-call(bf16[512,1920]{1,0:T(8,128)(2,1)S(1)} %constant_dynamic-update-slice_fusion.refs_3_.refs_6_.refs_8_.refs_0_, ...), custom_call_target="tpu_custom_call" | custom-call | flops 1409286144 | bytes 12062720 | tf_op jit(solution)/shard_map/image_grad/pallas_call | solution.py:72
  73.8 1.5 %collective-permute-start.21 = (bf16[272,768]{1,0:T(8,128)(2,1)S(1)}, bf16[272,768]{1,0:T(8,128)(2,1)S(1)}, u32[]{:S(2)}, u32[]{:S(2)}) collective-permute-start(bf16[272,768]{1,0:T(8,128)(2,1)S(1)} %get-tuple-element.92), channel_id=1, source_target_pairs={{0,6},{1,7},{2,0},{3,1},{4,2},{5,3},{6,4},{7,5},{8,14},{9,15},{10,... | collective-permute-start | bytes 1253384 | tf_op jit(solution)/shard_map/ppermute | solution.py:31
  75.3 0.6 collective-permute-start.22
  75.9 0.9 text_grad.1.own
  76.8 1.7 %collective-permute-start.23 = (bf16[128,768]{1,0:T(8,128)(2,1)S(1)}, bf16[128,768]{1,0:T(8,128)(2,1)S(1)}, u32[]{:S(2)}, u32[]{:S(2)}) collective-permute-start(bf16[128,768]{1,0:T(8,128)(2,1)S(1)} %get-tuple-element.95), channel_id=1, source_target_pairs={{0,1},{1,0},{2,3},{3,2},{4,5},{5,4},{6,7},{7,6},{8,9},{9,8},{10,11... | collective-permute-start | bytes 589832 | tf_op jit(solution)/shard_map/ppermute | solution.py:31
  78.6 0.4 text_sum.1
  79.0 0.2 collective-permute-start.27
  79.1 1.9 %collective-permute-start.28 = (bf16[256,768]{1,0:T(8,128)(2,1)S(1)}, bf16[256,768]{1,0:T(8,128)(2,1)S(1)}, u32[]{:S(2)}, u32[]{:S(2)}) collective-permute-start(bf16[256,768]{1,0:T(8,128)(2,1)S(1)} %get-tuple-element.101), channel_id=1, source_target_pairs={{0,16},{1,17},{2,18},{3,19},{4,20},{5,21},{6,22},{7,23},{8,24},{9,... | collective-permute-start | bytes 1179656 | tf_op jit(solution)/shard_map/ppermute | solution.py:31
  81.0 1.5 %collective-permute-done.23.from_z = bf16[128,768]{1,0:T(8,128)(2,1)S(1)} collective-permute-done((bf16[128,768]{1,0:T(8,128)(2,1)S(1)}, bf16[128,768]{1,0:T(8,128)(2,1)S(1)}, u32[]{:S(2)}, u32[]{:S(2)}) %collective-permute-start.23) | collective-permute-done | bytes 196640 | tf_op jit(solution)/shard_map/ppermute | solution.py:31
  82.6 0.6 collective-permute-start.29
  83.2 0.6 collective-permute-done.21.one
  83.8 2.4 %collective-permute-done.22.two = bf16[272,768]{1,0:T(8,128)(2,1)S(1)} collective-permute-done((bf16[272,768]{1,0:T(8,128)(2,1)S(1)}, bf16[272,768]{1,0:T(8,128)(2,1)S(1)}, u32[]{:S(2)}, u32[]{:S(2)}) %collective-permute-start.22) | collective-permute-done | bytes 417824 | tf_op jit(solution)/shard_map/ppermute | solution.py:31
  86.2 0.2 image_sum.1
  86.4 1.7 %collective-permute-start.32 = (bf16[144,768]{1,0:T(8,128)(2,1)S(1)}, bf16[144,768]{1,0:T(8,128)(2,1)S(1)}, u32[]{:S(2)}, u32[]{:S(2)}) collective-permute-start(bf16[144,768]{1,0:T(8,128)(2,1)S(1)} %get-tuple-element.108), channel_id=1, source_target_pairs={{0,1},{1,0},{2,3},{3,2},{4,5},{5,4},{6,7},{7,6},{8,9},{9,8},{10,11... | collective-permute-start | bytes 663560 | tf_op jit(solution)/shard_map/ppermute | solution.py:31
  88.2 1.3 %collective-permute-done.29.from_z = bf16[128,768]{1,0:T(8,128)(2,1)S(1)} collective-permute-done((bf16[128,768]{1,0:T(8,128)(2,1)S(1)}, bf16[128,768]{1,0:T(8,128)(2,1)S(1)}, u32[]{:S(2)}, u32[]{:S(2)}) %collective-permute-start.29) | collective-permute-done | bytes 196640 | tf_op jit(solution)/shard_map/ppermute | solution.py:31
  89.5 0.1 text_ring_sum.1
  89.6 0.7 collective-permute-start.30
  90.3 2.9 %collective-permute-start.33 = (bf16[128,768]{1,0:T(8,128)(2,1)S(1)}, bf16[128,768]{1,0:T(8,128)(2,1)S(1)}, u32[]{:S(2)}, u32[]{:S(2)}) collective-permute-start(bf16[128,768]{1,0:T(8,128)(2,1)S(1)} %get-tuple-element.109), channel_id=1, source_target_pairs={{0,4},{1,5},{2,6},{3,7},{4,0},{5,1},{6,2},{7,3},{8,12},{9,13},{10,... | collective-permute-start | bytes 589832 | tf_op jit(solution)/shard_map/ppermute | solution.py:31
  93.3 0.8 collective-permute-start.25
  94.1 4.3 %collective-permute-done.25.loss_far = f32[8,128]{1,0:T(8,128)S(1)} collective-permute-done((f32[8,128]{1,0:T(8,128)S(1)}, f32[8,128]{1,0:T(8,128)S(1)}, u32[]{:S(2)}, u32[]{:S(2)}) %collective-permute-start.25) | collective-permute-done | bytes 4128 | tf_op jit(solution)/shard_map/ppermute | solution.py:31
  98.4 2.1 %collective-permute-done.31.txt_x = bf16[128,768]{1,0:T(8,128)(2,1)S(1)} collective-permute-done((bf16[128,768]{1,0:T(8,128)(2,1)S(1)}, bf16[128,768]{1,0:T(8,128)(2,1)S(1)}, u32[]{:S(2)}, u32[]{:S(2)}) %collective-permute-start.31) | collective-permute-done | bytes 196640 | tf_op jit(solution)/shard_map/ppermute | solution.py:31
  100.4 1.3 %finish.1 = (f32[128,768]{1,0:T(8,128)}, f32[128,768]{1,0:T(8,128)}, f32[1,1]{1,0:T(1,128)}) custom-call(f32[8,128]{1,0:T(8,128)S(1)} %get-tuple-element.96.loss, f32[8,128]{1,0:T(8,128)S(1)} %collective-permute-done.25.loss_far, f32[128,768]{1,0:T(8,128)S(1)} %get-tuple-element.104.txt, bf16[144,768]{1,0:T(8,128)(2,1)S(1)} %collective-permute-done.30.txt_z, ...), custom_call_target="tpu_custom_call" | custom-call | bytes 2023424 | tf_op jit(solution)/shard_map/finish/pallas_call | solution.py:72
  (30 shorter events, 0.4 us)
Async XLA Ops:
  2.2 14.4 %collective-permute-start = (bf16[128,1920]{1,0:T(8,128)(2,1)S(1)}, bf16[128,1920]{1,0:T(8,128)(2,1)S(1)}, u32[]{:S(2)}, u32[]{:S(2)}) collective-permute-start(bf16[128,1920]{1,0:T(8,128)(2,1)S(1)} %get-tuple-element.58), channel_id=1, source_target_pairs={{0,16},{1,17},{2,18},{3,19},{4,20},{5,21},{6,22},{7,23},{8,24},{9,... | collective-permute-start | bytes 1474568 | tf_op jit(solution)/shard_map/ppermute | solution.py:31
  3.9 15.0 %collective-permute-start.4 = (bf16[128,1920]{1,0:T(8,128)(2,1)S(1)}, bf16[128,1920]{1,0:T(8,128)(2,1)S(1)}, u32[]{:S(2)}, u32[]{:S(2)}) collective-permute-start(bf16[128,1920]{1,0:T(8,128)(2,1)S(1)} %get-tuple-element.58), channel_id=1, source_target_pairs={{0,65},{1,64},{2,67},{3,66},{4,69},{5,68},{6,71},{7,70},{8,73},{9,... | collective-permute-start | bytes 1474568 | tf_op jit(solution)/shard_map/ppermute | solution.py:31
  8.0 13.9 %collective-permute-start.2 = (bf16[128,1920]{1,0:T(8,128)(2,1)S(1)}, bf16[128,1920]{1,0:T(8,128)(2,1)S(1)}, u32[]{:S(2)}, u32[]{:S(2)}) collective-permute-start(bf16[128,1920]{1,0:T(8,128)(2,1)S(1)} %get-tuple-element.62.refs_0_), channel_id=1, source_target_pairs={{0,2},{1,3},{2,4},{3,5},{4,6},{5,7},{6,0},{7,1},{8,10},{9,11},{10,... | collective-permute-start | bytes 1474568 | tf_op jit(solution)/shard_map/ppermute | solution.py:31
  9.5 12.4 %collective-permute-start.6 = (bf16[128,1920]{1,0:T(8,128)(2,1)S(1)}, bf16[128,1920]{1,0:T(8,128)(2,1)S(1)}, u32[]{:S(2)}, u32[]{:S(2)}) collective-permute-start(bf16[128,1920]{1,0:T(8,128)(2,1)S(1)} %get-tuple-element.62.refs_0_), channel_id=1, source_target_pairs={{0,1},{1,0},{2,3},{3,2},{4,5},{5,4},{6,7},{7,6},{8,9},{9,8},{10,11... | collective-permute-start | bytes 1474568 | tf_op jit(solution)/shard_map/ppermute | solution.py:31
  9.5 15.6 %collective-permute-start.9 = (bf16[128,1920]{1,0:T(8,128)(2,1)S(1)}, bf16[128,1920]{1,0:T(8,128)(2,1)S(1)}, u32[]{:S(2)}, u32[]{:S(2)}) collective-permute-start(bf16[128,1920]{1,0:T(8,128)(2,1)S(1)} %get-tuple-element.58), channel_id=1, source_target_pairs={{0,48},{1,49},{2,50},{3,51},{4,52},{5,53},{6,54},{7,55},{8,56},{9,... | collective-permute-start | bytes 1474568 | tf_op jit(solution)/shard_map/ppermute | solution.py:31
  18.9 17.0 %collective-permute-start.5 = (bf16[128,1920]{1,0:T(8,128)(2,1)S(1)}, bf16[128,1920]{1,0:T(8,128)(2,1)S(1)}, u32[]{:S(2)}, u32[]{:S(2)}) collective-permute-start(bf16[128,1920]{1,0:T(8,128)(2,1)S(1)} %collective-permute-done), channel_id=1, source_target_pairs={{0,65},{1,64},{2,67},{3,66},{4,69},{5,68},{6,71},{7,70},{8,73},{9,... | collective-permute-start | bytes 1474568 | tf_op jit(solution)/shard_map/ppermute | solution.py:31
  21.9 14.1 %collective-permute-start.7 = (bf16[128,1920]{1,0:T(8,128)(2,1)S(1)}, bf16[128,1920]{1,0:T(8,128)(2,1)S(1)}, u32[]{:S(2)}, u32[]{:S(2)}) collective-permute-start(bf16[128,1920]{1,0:T(8,128)(2,1)S(1)} %collective-permute-done.2.refs_2_), channel_id=1, source_target_pairs={{0,1},{1,0},{2,3},{3,2},{4,5},{5,4},{6,7},{7,6},{8,9},{9,8},{10,11... | collective-permute-start | bytes 1474568 | tf_op jit(solution)/shard_map/ppermute | solution.py:31
  21.9 12.8 %collective-permute-start.1 = (bf16[128,1920]{1,0:T(8,128)(2,1)S(1)}, bf16[128,1920]{1,0:T(8,128)(2,1)S(1)}, u32[]{:S(2)}, u32[]{:S(2)}) collective-permute-start(bf16[128,1920]{1,0:T(8,128)(2,1)S(1)} %collective-permute-done), channel_id=1, source_target_pairs={{0,16},{1,17},{2,18},{3,19},{4,20},{5,21},{6,22},{7,23},{8,24},{9,... | collective-permute-start | bytes 1474568 | tf_op jit(solution)/shard_map/ppermute | solution.py:31
  23.5 12.4 %collective-permute-start.3 = (bf16[128,1920]{1,0:T(8,128)(2,1)S(1)}, bf16[128,1920]{1,0:T(8,128)(2,1)S(1)}, u32[]{:S(2)}, u32[]{:S(2)}) collective-permute-start(bf16[128,1920]{1,0:T(8,128)(2,1)S(1)} %collective-permute-done.2.refs_2_), channel_id=1, source_target_pairs={{0,2},{1,3},{2,4},{3,5},{4,6},{5,7},{6,0},{7,1},{8,10},{9,11},{10,... | collective-permute-start | bytes 1474568 | tf_op jit(solution)/shard_map/ppermute | solution.py:31
  25.0 10.9 %collective-permute-start.8 = (bf16[128,1920]{1,0:T(8,128)(2,1)S(1)}, bf16[128,1920]{1,0:T(8,128)(2,1)S(1)}, u32[]{:S(2)}, u32[]{:S(2)}) collective-permute-start(bf16[128,1920]{1,0:T(8,128)(2,1)S(1)} %get-tuple-element.62.refs_0_), channel_id=1, source_target_pairs={{0,6},{1,7},{2,0},{3,1},{4,2},{5,3},{6,4},{7,5},{8,14},{9,15},{10,... | collective-permute-start | bytes 1474568 | tf_op jit(solution)/shard_map/ppermute | solution.py:31
  36.1 6.0 %collective-permute-start.10 = (bf16[512,1920]{1,0:T(8,128)(2,1)S(1)}, bf16[512,1920]{1,0:T(8,128)(2,1)S(1)}, u32[]{:S(2)}, u32[]{:S(2)}) collective-permute-start(bf16[512,1920]{1,0:T(8,128)(2,1)S(1)} %constant_dynamic-update-slice_fusion.refs_3_.refs_6_.refs_8_.refs_0_), channel_id=1, source_target_pairs={{0,8},{1,9},{2,10},{3,11},{4,12},{5,13},{6,14},{7,15},{8,0},{9,1},... | collective-permute-start | bytes 5898248 | tf_op jit(solution)/shard_map/ppermute | solution.py:31
  36.3 10.3 %collective-permute-start.11 = (bf16[256,1920]{1,0:T(8,128)(2,1)S(1)}, bf16[256,1920]{1,0:T(8,128)(2,1)S(1)}, u32[]{:S(2)}, u32[]{:S(2)}) collective-permute-start(bf16[256,1920]{1,0:T(8,128)(2,1)S(1)} %constant_dynamic-update-slice_fusion.4.refs_8_.refs_9_.refs_1_), channel_id=1, source_target_pairs={{0,8},{1,9},{2,10},{3,11},{4,12},{5,13},{6,14},{7,15},{8,0},{9,1},... | collective-permute-start | bytes 2949128 | tf_op jit(solution)/shard_map/ppermute | solution.py:31
  36.9 16.9 %collective-permute-start.12 = (bf16[128,1920]{1,0:T(8,128)(2,1)S(1)}, bf16[128,1920]{1,0:T(8,128)(2,1)S(1)}, u32[]{:S(2)}, u32[]{:S(2)}) collective-permute-start(bf16[128,1920]{1,0:T(8,128)(2,1)S(1)} %collective-permute-done.4), channel_id=1, source_target_pairs={{0,48},{1,49},{2,50},{3,51},{4,52},{5,53},{6,54},{7,55},{8,56},{9,... | collective-permute-start | bytes 1474568 | tf_op jit(solution)/shard_map/ppermute | solution.py:31
  38.6 16.8 %collective-permute-start.15 = (bf16[128,1920]{1,0:T(8,128)(2,1)S(1)}, bf16[128,1920]{1,0:T(8,128)(2,1)S(1)}, u32[]{:S(2)}, u32[]{:S(2)}) collective-permute-start(bf16[128,1920]{1,0:T(8,128)(2,1)S(1)} %collective-permute-done.6.refs_1_), channel_id=1, source_target_pairs={{0,6},{1,7},{2,0},{3,1},{4,2},{5,3},{6,4},{7,5},{8,14},{9,15},{10,... | collective-permute-start | bytes 1474568 | tf_op jit(solution)/shard_map/ppermute | solution.py:31
  41.5 13.9 %collective-permute-start.13 = (bf16[128,1920]{1,0:T(8,128)(2,1)S(1)}, bf16[128,1920]{1,0:T(8,128)(2,1)S(1)}, u32[]{:S(2)}, u32[]{:S(2)}) collective-permute-start(bf16[128,1920]{1,0:T(8,128)(2,1)S(1)} %collective-permute-done.1), channel_id=1, source_target_pairs={{0,65},{1,64},{2,67},{3,66},{4,69},{5,68},{6,71},{7,70},{8,73},{9,... | collective-permute-start | bytes 1474568 | tf_op jit(solution)/shard_map/ppermute | solution.py:31
  42.1 13.3 %collective-permute-start.14 = (bf16[128,1920]{1,0:T(8,128)(2,1)S(1)}, bf16[128,1920]{1,0:T(8,128)(2,1)S(1)}, u32[]{:S(2)}, u32[]{:S(2)}) collective-permute-start(bf16[128,1920]{1,0:T(8,128)(2,1)S(1)} %collective-permute-done.3.refs_3_), channel_id=1, source_target_pairs={{0,1},{1,0},{2,3},{3,2},{4,5},{5,4},{6,7},{7,6},{8,9},{9,8},{10,11... | collective-permute-start | bytes 1474568 | tf_op jit(solution)/shard_map/ppermute | solution.py:31
  55.5 3.7 %collective-permute-start.16 = (bf16[256,1920]{1,0:T(8,128)(2,1)S(1)}, bf16[256,1920]{1,0:T(8,128)(2,1)S(1)}, u32[]{:S(2)}, u32[]{:S(2)}) collective-permute-start(bf16[256,1920]{1,0:T(8,128)(2,1)S(1)} %constant_dynamic-update-slice_fusion.6.refs_12_.refs_4_), channel_id=1, source_target_pairs={{0,8},{1,9},{2,10},{3,11},{4,12},{5,13},{6,14},{7,15},{8,0},{9,1},... | collective-permute-start | bytes 2949128 | tf_op jit(solution)/shard_map/ppermute | solution.py:31
  60.8 1.5 %collective-permute-start.17 = (f32[8,128]{1,0:T(8,128)S(1)}, f32[8,128]{1,0:T(8,128)S(1)}, u32[]{:S(2)}, u32[]{:S(2)}) collective-permute-start(f32[8,128]{1,0:T(8,128)S(1)} %get-tuple-element.88), channel_id=1, source_target_pairs={{0,8},{1,9},{2,10},{3,11},{4,12},{5,13},{6,14},{7,15},{8,0},{9,1},... | collective-permute-start | bytes 12296 | tf_op jit(solution)/shard_map/ppermute | solution.py:31
  62.3 16.3 %collective-permute-start.26 = (bf16[1024,768]{1,0:T(8,128)(2,1)S(1)}, bf16[1024,768]{1,0:T(8,128)(2,1)S(1)}, u32[]{:S(2)}, u32[]{:S(2)}) collective-permute-start(bf16[1024,768]{1,0:T(8,128)(2,1)S(1)} %other_grad.1), channel_id=1, source_target_pairs={{0,8},{1,9},{2,10},{3,11},{4,12},{5,13},{6,14},{7,15},{8,0},{9,1},... | collective-permute-start | bytes 4718600 | tf_op jit(solution)/shard_map/ppermute | solution.py:31
  62.5 5.1 %collective-permute-start.20 = (f32[8,128]{1,0:T(8,128)S(1)}, f32[8,128]{1,0:T(8,128)S(1)}, u32[]{:S(2)}, u32[]{:S(2)}) collective-permute-start(f32[8,128]{1,0:T(8,128)S(1)} %add.12), channel_id=1, source_target_pairs={{0,32},{1,33},{2,34},{3,35},{4,36},{5,37},{6,38},{7,39},{8,40},{9,... | collective-permute-start | bytes 12296 | tf_op jit(solution)/shard_map/ppermute | solution.py:31
  64.2 3.6 %collective-permute-start.19 = (f32[8,128]{1,0:T(8,128)S(1)}, f32[8,128]{1,0:T(8,128)S(1)}, u32[]{:S(2)}, u32[]{:S(2)}) collective-permute-start(f32[8,128]{1,0:T(8,128)S(1)} %add.12), channel_id=1, source_target_pairs={{0,48},{1,49},{2,50},{3,51},{4,52},{5,53},{6,54},{7,55},{8,56},{9,... | collective-permute-start | bytes 12296 | tf_op jit(solution)/shard_map/ppermute | solution.py:31
  65.6 4.8 %collective-permute-start.18 = (f32[8,128]{1,0:T(8,128)S(1)}, f32[8,128]{1,0:T(8,128)S(1)}, u32[]{:S(2)}, u32[]{:S(2)}) collective-permute-start(f32[8,128]{1,0:T(8,128)S(1)} %add.12), channel_id=1, source_target_pairs={{0,16},{1,17},{2,18},{3,19},{4,20},{5,21},{6,22},{7,23},{8,24},{9,... | collective-permute-start | bytes 12296 | tf_op jit(solution)/shard_map/ppermute | solution.py:31
  70.4 8.7 %collective-permute-start.24 = (f32[8,128]{1,0:T(8,128)S(1)}, f32[8,128]{1,0:T(8,128)S(1)}, u32[]{:S(2)}, u32[]{:S(2)}) collective-permute-start(f32[8,128]{1,0:T(8,128)S(1)} %add_add_fusion.refs_10_.loss), channel_id=1, source_target_pairs={{0,4},{1,5},{2,6},{3,7},{4,0},{5,1},{6,2},{7,3},{8,12},{9,13},{10,... | collective-permute-start | bytes 12296 | tf_op jit(solution)/shard_map/ppermute | solution.py:31
  73.8 10.0 %collective-permute-start.21 = (bf16[272,768]{1,0:T(8,128)(2,1)S(1)}, bf16[272,768]{1,0:T(8,128)(2,1)S(1)}, u32[]{:S(2)}, u32[]{:S(2)}) collective-permute-start(bf16[272,768]{1,0:T(8,128)(2,1)S(1)} %get-tuple-element.92), channel_id=1, source_target_pairs={{0,6},{1,7},{2,0},{3,1},{4,2},{5,3},{6,4},{7,5},{8,14},{9,15},{10,... | collective-permute-start | bytes 1253384 | tf_op jit(solution)/shard_map/ppermute | solution.py:31
  75.3 10.8 %collective-permute-start.22 = (bf16[272,768]{1,0:T(8,128)(2,1)S(1)}, bf16[272,768]{1,0:T(8,128)(2,1)S(1)}, u32[]{:S(2)}, u32[]{:S(2)}) collective-permute-start(bf16[272,768]{1,0:T(8,128)(2,1)S(1)} %get-tuple-element.93), channel_id=1, source_target_pairs={{0,2},{1,3},{2,4},{3,5},{4,6},{5,7},{6,0},{7,1},{8,10},{9,11},{10,... | collective-permute-start | bytes 1253384 | tf_op jit(solution)/shard_map/ppermute | solution.py:31
  76.8 5.8 %collective-permute-start.23 = (bf16[128,768]{1,0:T(8,128)(2,1)S(1)}, bf16[128,768]{1,0:T(8,128)(2,1)S(1)}, u32[]{:S(2)}, u32[]{:S(2)}) collective-permute-start(bf16[128,768]{1,0:T(8,128)(2,1)S(1)} %get-tuple-element.95), channel_id=1, source_target_pairs={{0,1},{1,0},{2,3},{3,2},{4,5},{5,4},{6,7},{7,6},{8,9},{9,8},{10,11... | collective-permute-start | bytes 589832 | tf_op jit(solution)/shard_map/ppermute | solution.py:31
  79.0 10.5 %collective-permute-start.27 = (bf16[256,768]{1,0:T(8,128)(2,1)S(1)}, bf16[256,768]{1,0:T(8,128)(2,1)S(1)}, u32[]{:S(2)}, u32[]{:S(2)}) collective-permute-start(bf16[256,768]{1,0:T(8,128)(2,1)S(1)} %get-tuple-element.100), channel_id=1, source_target_pairs={{0,48},{1,49},{2,50},{3,51},{4,52},{5,53},{6,54},{7,55},{8,56},{9,... | collective-permute-start | bytes 1179656 | tf_op jit(solution)/shard_map/ppermute | solution.py:31
  79.1 10.4 %collective-permute-start.28 = (bf16[256,768]{1,0:T(8,128)(2,1)S(1)}, bf16[256,768]{1,0:T(8,128)(2,1)S(1)}, u32[]{:S(2)}, u32[]{:S(2)}) collective-permute-start(bf16[256,768]{1,0:T(8,128)(2,1)S(1)} %get-tuple-element.101), channel_id=1, source_target_pairs={{0,16},{1,17},{2,18},{3,19},{4,20},{5,21},{6,22},{7,23},{8,24},{9,... | collective-permute-start | bytes 1179656 | tf_op jit(solution)/shard_map/ppermute | solution.py:31
  82.6 6.9 %collective-permute-start.29 = (bf16[128,768]{1,0:T(8,128)(2,1)S(1)}, bf16[128,768]{1,0:T(8,128)(2,1)S(1)}, u32[]{:S(2)}, u32[]{:S(2)}) collective-permute-start(bf16[128,768]{1,0:T(8,128)(2,1)S(1)} %get-tuple-element.103), channel_id=1, source_target_pairs={{0,65},{1,64},{2,67},{3,66},{4,69},{5,68},{6,71},{7,70},{8,73},{9,... | collective-permute-start | bytes 589832 | tf_op jit(solution)/shard_map/ppermute | solution.py:31
  86.2 14.3 %copy-start = (bf16[128,768]{1,0:T(8,128)(2,1)S(1)}, bf16[128,768]{1,0:T(8,128)(2,1)}, u32[]{:S(2)}) copy-start(bf16[128,768]{1,0:T(8,128)(2,1)} %si.3) | copy-start | bytes 589828
  86.2 14.3 %copy-start.1 = (bf16[128,768]{1,0:T(8,128)(2,1)S(1)}, bf16[128,768]{1,0:T(8,128)(2,1)}, u32[]{:S(2)}) copy-start(bf16[128,768]{1,0:T(8,128)(2,1)} %st.3) | copy-start | bytes 589828
  86.4 12.0 %collective-permute-start.32 = (bf16[144,768]{1,0:T(8,128)(2,1)S(1)}, bf16[144,768]{1,0:T(8,128)(2,1)S(1)}, u32[]{:S(2)}, u32[]{:S(2)}) collective-permute-start(bf16[144,768]{1,0:T(8,128)(2,1)S(1)} %get-tuple-element.108), channel_id=1, source_target_pairs={{0,1},{1,0},{2,3},{3,2},{4,5},{5,4},{6,7},{7,6},{8,9},{9,8},{10,11... | collective-permute-start | bytes 663560 | tf_op jit(solution)/shard_map/ppermute | solution.py:31
  89.6 10.8 %collective-permute-start.30 = (bf16[144,768]{1,0:T(8,128)(2,1)S(1)}, bf16[144,768]{1,0:T(8,128)(2,1)S(1)}, u32[]{:S(2)}, u32[]{:S(2)}) collective-permute-start(bf16[144,768]{1,0:T(8,128)(2,1)S(1)} %get-tuple-element.105), channel_id=1, source_target_pairs={{0,65},{1,64},{2,67},{3,66},{4,69},{5,68},{6,71},{7,70},{8,73},{9,... | collective-permute-start | bytes 663560 | tf_op jit(solution)/shard_map/ppermute | solution.py:31
  90.3 8.0 %collective-permute-start.33 = (bf16[128,768]{1,0:T(8,128)(2,1)S(1)}, bf16[128,768]{1,0:T(8,128)(2,1)S(1)}, u32[]{:S(2)}, u32[]{:S(2)}) collective-permute-start(bf16[128,768]{1,0:T(8,128)(2,1)S(1)} %get-tuple-element.109), channel_id=1, source_target_pairs={{0,4},{1,5},{2,6},{3,7},{4,0},{5,1},{6,2},{7,3},{8,12},{9,13},{10,... | collective-permute-start | bytes 589832 | tf_op jit(solution)/shard_map/ppermute | solution.py:31
  93.3 7.2 %collective-permute-start.31 = (bf16[128,768]{1,0:T(8,128)(2,1)S(1)}, bf16[128,768]{1,0:T(8,128)(2,1)S(1)}, u32[]{:S(2)}, u32[]{:S(2)}) collective-permute-start(bf16[128,768]{1,0:T(8,128)(2,1)S(1)} %get-tuple-element.106), channel_id=1, source_target_pairs={{0,32},{1,33},{2,34},{3,35},{4,36},{5,37},{6,38},{7,39},{8,40},{9,... | collective-permute-start | bytes 589832 | tf_op jit(solution)/shard_map/ppermute | solution.py:31
  93.3 5.1 %collective-permute-start.25 = (f32[8,128]{1,0:T(8,128)S(1)}, f32[8,128]{1,0:T(8,128)S(1)}, u32[]{:S(2)}, u32[]{:S(2)}) collective-permute-start(f32[8,128]{1,0:T(8,128)S(1)} %get-tuple-element.96.loss), channel_id=1, source_target_pairs={{0,64},{1,65},{2,66},{3,67},{4,68},{5,69},{6,70},{7,71},{8,72},{9,... | collective-permute-start | bytes 12296 | tf_op jit(solution)/shard_map/ppermute | solution.py:31

commit v3 on v2

--- a/solution.py
+++ b/solution.py
@@ -183,7 +183,7 @@
     out[most:, :] = dot(coef_l[...], stack(imgs, cols_s), TN).astype(out.dtype)
 
 
-def text_sum_kernel(own, from_core, t0, t1, t2, t3, t4):
+def text_sum_kernel(own, from_core, loss, t0, t1, t2, t3, t4):
     at = lambda low, high: own[low:high, :] + from_core[low:high, :].astype(f32)
     t0[...] = at(0, 256)
     t1[0:128, :] = at(256, 384).astype(bf16)
@@ -192,11 +192,13 @@
     t2[128:256, :] = at(768, 896).astype(bf16)
     t3[...] = at(512, 640)
     t4[...] = at(896, 1024).astype(bf16)
+    for ref in (t1, t2):
+        put_pieces(ref, 256, loss[...])
 
 
 def image_grad_kernel(width_t, *refs):
     texts, last_t, last_u = refs[:4], refs[4], refs[5]
-    coef_p, coef_t, coef_u, part, loss, i0, i1, i2, i3, i4 = refs[6:]
+    coef_p, coef_t, coef_u, part, i0, i1, i2, i3, i4 = refs[6:]
     cols_s = slice(width_t, None)
     most = part.shape[0]
     grad = dot(coef_t[...], last_t[:, cols_s]) + dot(coef_u[...], last_u[:, cols_s])
@@ -209,8 +211,6 @@
     i2[128:256, :] = late[0:128].astype(bf16)
     i3[...] = early[384:512]
     i4[...] = late[128:256].astype(bf16)
-    for ref in (i1, i2):
-        put_pieces(ref, 256, loss[...])
 
 
 def join(*parts):
@@ -232,19 +232,21 @@
     return at(0) + at(128) + at(256)
 
 
-def image_sum_kernel(own, one, two, far, from_z, loss, loss_x, near, to_z, to_far, loss_out):
-    rows = near.shape[0]
-    loss_out[...] = loss[...] + loss_x[...] + get_pieces(one, 2 * rows) + get_pieces(two, 2 * rows)
-    ring_sum(own, one, two, far, from_z, loss_out, near, to_z, to_far)
-
-
-def ring_sum(own, one, two, far, from_z, loss, near, to_z, to_far):
+def ring_sum(own, one, two, far, from_z, near, to_z, to_far):
     rows = near.shape[0]
     total = own[...] + one[:2 * rows, :].astype(f32) + two[:2 * rows, :].astype(f32)
     near[...] = total[:rows]
     to_z[:rows, :] = total[rows:].astype(bf16)
-    put_pieces(to_z, rows, loss[...])
     to_far[...] = (far[...] + from_z[...].astype(f32)).astype(bf16)
+
+
+def text_ring_kernel(own, one, two, far, from_z, loss, loss_far, img_z, near, to_z, to_far, img_out, loss_out):
+    rows = near.shape[0]
+    loss_out[...] = loss[...] + loss_far[...] + get_pieces(one, 2 * rows) + get_pieces(two, 2 * rows)
+    ring_sum(own, one, two, far, from_z, near, to_z, to_far)
+    img_out[:rows, :] = img_z[...]
+    for ref in (to_z, img_out):
+        put_pieces(ref, rows, loss_out[...])
 
 
 def finish_kernel(
@@ -320,29 +322,32 @@
     grad_o, loss_core = hold((grad_o, loss_core))
     from_core = to_core(grad_o)
     loss = loss + loss_core
-    loss = loss + to_y(loss, 1) + to_y(loss, -1) + to_y(loss, 2)
+    loss_x = [to_x(loss, 1), to_x(loss, -1), to_x(loss, 2)]
     pair = 2 * rows
     sums = [((rows, width_s), f32), ((rows, width_s), bf16)]
     grad_t = call(
         run(text_grad_kernel, width_t, 0), "text_grad", (*imgs, coef_p, coef_t, p_txt),
         [((8 * rows, width_s), f32)], flops=grad_work,
     )[0]
+    i0, i1, i2, i3, i4 = call(
+        run(image_grad_kernel, width_t), "image_grad", (*texts, txt_n, oth_n, coef_p, coef_t, coef_u, p_img),
+        [((pair, width_s), f32)] + [((pair, width_s), bf16)] * 2 + sums, flops=2 * grad_work,
+    )
+    loss_x, i0 = hold((loss_x, i0))
+    loss = loss + loss_x[0] + loss_x[1] + loss_x[2]
     t0, t1, t2, t3, t4 = call(
-        text_sum_kernel, "text_sum", (grad_t, from_core),
-        [((pair, width_s), f32)] + [((pair, width_s), bf16)] * 2 + sums,
-    )
-    i0, i1, i2, i3, i4 = call(
-        run(image_grad_kernel, width_t), "image_grad", (*texts, txt_n, oth_n, coef_p, coef_t, coef_u, p_img, loss),
-        [((pair, width_s), f32)] + [((pair + 16, width_s), bf16)] * 2 + sums, flops=2 * grad_work,
-    )
-    loss_x = to_x(loss, 2)
+        text_sum_kernel, "text_sum", (grad_t, from_core, loss),
+        [((pair, width_s), f32)] + [((pair + 16, width_s), bf16)] * 2 + sums,
+    )
     i4, i1, i2 = to_image_z(i4), to_x(i1, -1), to_x(i2, 1)
+    loss_2 = to_y(loss, 2)
     t1, t2, t4 = to_y(t1, -1), to_y(t2, 1), to_text_z(t4)
-    parts = [((rows, width_s), f32), ((rows + 16, width_s), bf16), ((rows, width_s), bf16)]
-    img, img_z, img_x, loss = call(
-        image_sum_kernel, "image_sum", (i0, i1, i2, i3, i4, loss, loss_x), parts + [((8, 128), f32)],
-    )
-    txt, txt_z, txt_x = call(ring_sum, "text_ring_sum", (t0, t1, t2, t3, t4, loss), parts)
+    near, to_z, to_far = ((rows, width_s), f32), ((rows + 16, width_s), bf16), ((rows, width_s), bf16)
+    img, img_z, img_x = call(ring_sum, "image_ring", (i0, i1, i2, i3, i4), [near, to_far, to_far])
+    txt, txt_z, txt_x, img_z, loss = call(
+        text_ring_kernel, "text_ring", (t0, t1, t2, t3, t4, loss, loss_2, img_z),
+        [near, to_z, to_far, to_z, ((8, 128), f32)],
+    )
     txt_x, img_x = to_y(txt_x, 2), to_x(img_x, 2)
     txt_z, img_z, loss_far = to_text_z(txt_z), to_image_z(img_z), to_far_z(loss)
     pairs = float(rows * lax.axis_size("dp") * lax.axis_size("blk"))

time: 102 us -> 101 us (level); the launches traced: 102 us -> 99.6 us
  waiting for transfers between devices: 34.8 us -> 33.6 us
    ppermute x34, waiting for transfers between devices: 34.8 us -> 33.6 us  [permute(): return lax.ppermute(value, AXES, pairs)]
  transfers between devices with their start and end apart: 34 -> 34, of which waited for: 14 -> 15; matrix products, arithmetic and copies ran while one was open for 0% -> 0% of each run, Pallas kernels for 18% -> 18%
where the time goes in v3:
time: 101 us; the launch traced here: 99.6 us
  starting transfers between devices  42.3 us (42%)
  waiting for transfers between devices  33.6 us (33%)
  Pallas kernels  22.6 us (22%)
    ppermute x34, starting transfers between devices, permute(): return lax.ppermute(value, AXES, pairs)  42.3 us
    ppermute x34, waiting for transfers between devices, permute(): return lax.ppermute(value, AXES, pairs)  33.6 us
    pallas_call x12, Pallas kernels, call(): pl.pallas_call(kernel, out_shape=tuple((shape_of(shape, dtype) for shape,...  22.6 us
  transfers between devices with their start and end apart: 34, of which 15 were waited for; matrix products, arithmetic and copies ran while one was open for 0% of the time, Pallas kernels for 18%

profile of v3, /device:TPU:0, one launch (start us, length us, event | category | flops | bytes accessed | tf_op | source)
XLA Modules:
  0.0 99.6 jit_solution(10129918587076329685)
XLA Ops:
  0.6 1.6 %units.1 = (bf16[128,1920]{1,0:T(8,128)(2,1)S(1)}, bf16[128,1920]{1,0:T(8,128)(2,1)S(1)}) custom-call(bf16[128,1152]{1,0:T(8,128)(2,1)} %ti.1, bf16[128,768]{1,0:T(8,128)(2,1)} %si.3, bf16[128,1152]{1,0:T(8,128)(2,1)} %tt.1, bf16[128,768]{1,0:T(8,128)(2,1)} %st.3), custom_call_target="tpu_custom_call" | custom-call | bytes 983040 | tf_op jit(solution)/shard_map/units/pallas_call | solution.py:72
  2.2 4.2 %collective-permute-start.5 = (bf16[128,1920]{1,0:T(8,128)(2,1)S(1)}, bf16[128,1920]{1,0:T(8,128)(2,1)S(1)}, u32[]{:S(2)}, u32[]{:S(2)}) collective-permute-start(bf16[128,1920]{1,0:T(8,128)(2,1)S(1)} %get-tuple-element.64), channel_id=1, source_target_pairs={{0,65},{1,64},{2,67},{3,66},{4,69},{5,68},{6,71},{7,70},{8,73},{9,... | collective-permute-start | bytes 1474568 | tf_op jit(solution)/shard_map/ppermute | solution.py:31
  6.4 1.6 %collective-permute-start.2 = (bf16[128,1920]{1,0:T(8,128)(2,1)S(1)}, bf16[128,1920]{1,0:T(8,128)(2,1)S(1)}, u32[]{:S(2)}, u32[]{:S(2)}) collective-permute-start(bf16[128,1920]{1,0:T(8,128)(2,1)S(1)} %get-tuple-element.64), channel_id=1, source_target_pairs={{0,16},{1,17},{2,18},{3,19},{4,20},{5,21},{6,22},{7,23},{8,24},{9,... | collective-permute-start | bytes 1474568 | tf_op jit(solution)/shard_map/ppermute | solution.py:31
  8.0 0.0 collective-permute-start
  8.0 1.5 %collective-permute-start.1 = (bf16[128,1920]{1,0:T(8,128)(2,1)S(1)}, bf16[128,1920]{1,0:T(8,128)(2,1)S(1)}, u32[]{:S(2)}, u32[]{:S(2)}) collective-permute-start(bf16[128,1920]{1,0:T(8,128)(2,1)S(1)} %get-tuple-element.67.refs_0_), channel_id=1, source_target_pairs={{0,2},{1,3},{2,4},{3,5},{4,6},{5,7},{6,0},{7,1},{8,10},{9,11},{10,... | collective-permute-start | bytes 1474568 | tf_op jit(solution)/shard_map/ppermute | solution.py:31
  9.5 1.7 %collective-permute-start.9 = (bf16[128,1920]{1,0:T(8,128)(2,1)S(1)}, bf16[128,1920]{1,0:T(8,128)(2,1)S(1)}, u32[]{:S(2)}, u32[]{:S(2)}) collective-permute-start(bf16[128,1920]{1,0:T(8,128)(2,1)S(1)} %get-tuple-element.64), channel_id=1, source_target_pairs={{0,48},{1,49},{2,50},{3,51},{4,52},{5,53},{6,54},{7,55},{8,56},{9,... | collective-permute-start | bytes 1474568 | tf_op jit(solution)/shard_map/ppermute | solution.py:31
  11.2 6.5 %collective-permute-done.5 = bf16[128,1920]{1,0:T(8,128)(2,1)S(1)} collective-permute-done((bf16[128,1920]{1,0:T(8,128)(2,1)S(1)}, bf16[128,1920]{1,0:T(8,128)(2,1)S(1)}, u32[]{:S(2)}, u32[]{:S(2)}) %collective-permute-start.5) | collective-permute-done | bytes 491552 | tf_op jit(solution)/shard_map/ppermute | solution.py:31
  17.6 2.7 %collective-permute-done.2 = bf16[128,1920]{1,0:T(8,128)(2,1)S(1)} collective-permute-done((bf16[128,1920]{1,0:T(8,128)(2,1)S(1)}, bf16[128,1920]{1,0:T(8,128)(2,1)S(1)}, u32[]{:S(2)}, u32[]{:S(2)}) %collective-permute-start.2) | collective-permute-done | bytes 491552 | tf_op jit(solution)/shard_map/ppermute | solution.py:31
  20.4 0.4 collective-permute-start.6
  20.7 0.0 collective-permute-done.refs_1_
  20.7 0.9 collective-permute-done.1.refs_2_
  21.6 1.7 %collective-permute-start.7 = (bf16[128,1920]{1,0:T(8,128)(2,1)S(1)}, bf16[128,1920]{1,0:T(8,128)(2,1)S(1)}, u32[]{:S(2)}, u32[]{:S(2)}) collective-permute-start(bf16[128,1920]{1,0:T(8,128)(2,1)S(1)} %collective-permute-done.1.refs_2_), channel_id=1, source_target_pairs={{0,1},{1,0},{2,3},{3,2},{4,5},{5,4},{6,7},{7,6},{8,9},{9,8},{10,11... | collective-permute-start | bytes 1474568 | tf_op jit(solution)/shard_map/ppermute | solution.py:31
  23.4 1.6 %collective-permute-start.3 = (bf16[128,1920]{1,0:T(8,128)(2,1)S(1)}, bf16[128,1920]{1,0:T(8,128)(2,1)S(1)}, u32[]{:S(2)}, u32[]{:S(2)}) collective-permute-start(bf16[128,1920]{1,0:T(8,128)(2,1)S(1)} %collective-permute-done.2), channel_id=1, source_target_pairs={{0,16},{1,17},{2,18},{3,19},{4,20},{5,21},{6,22},{7,23},{8,24},{9,... | collective-permute-start | bytes 1474568 | tf_op jit(solution)/shard_map/ppermute | solution.py:31
  24.9 0.3 collective-permute-start.4
  25.2 0.0 collective-permute-done.9
  25.2 3.0 %collective-permute-start.8 = (bf16[128,1920]{1,0:T(8,128)(2,1)S(1)}, bf16[128,1920]{1,0:T(8,128)(2,1)S(1)}, u32[]{:S(2)}, u32[]{:S(2)}) collective-permute-start(bf16[128,1920]{1,0:T(8,128)(2,1)S(1)} %get-tuple-element.67.refs_0_), channel_id=1, source_target_pairs={{0,6},{1,7},{2,0},{3,1},{4,2},{5,3},{6,4},{7,5},{8,14},{9,15},{10,... | collective-permute-start | bytes 1474568 | tf_op jit(solution)/shard_map/ppermute | solution.py:31
  28.2 5.2 %collective-permute-done.6 = bf16[128,1920]{1,0:T(8,128)(2,1)S(1)} collective-permute-done((bf16[128,1920]{1,0:T(8,128)(2,1)S(1)}, bf16[128,1920]{1,0:T(8,128)(2,1)S(1)}, u32[]{:S(2)}, u32[]{:S(2)}) %collective-permute-start.6) | collective-permute-done | bytes 491552 | tf_op jit(solution)/shard_map/ppermute | solution.py:31
  33.4 2.1 %collective-permute-done.3 = bf16[128,1920]{1,0:T(8,128)(2,1)S(1)} collective-permute-done((bf16[128,1920]{1,0:T(8,128)(2,1)S(1)}, bf16[128,1920]{1,0:T(8,128)(2,1)S(1)}, u32[]{:S(2)}, u32[]{:S(2)}) %collective-permute-start.3) | collective-permute-done | bytes 491552 | tf_op jit(solution)/shard_map/ppermute | solution.py:31
  35.5 1.3 %collective-permute-done.4.refs_3_ = bf16[128,1920]{1,0:T(8,128)(2,1)S(1)} collective-permute-done((bf16[128,1920]{1,0:T(8,128)(2,1)S(1)}, bf16[128,1920]{1,0:T(8,128)(2,1)S(1)}, u32[]{:S(2)}, u32[]{:S(2)}) %collective-permute-start.4) | collective-permute-done | bytes 491552 | tf_op jit(solution)/shard_map/ppermute | solution.py:31
  36.9 0.1 collective-permute-start.14
  37.1 0.6 collective-permute-start.15
  37.7 1.7 %collective-permute-start.10 = (bf16[128,1920]{1,0:T(8,128)(2,1)S(1)}, bf16[128,1920]{1,0:T(8,128)(2,1)S(1)}, u32[]{:S(2)}, u32[]{:S(2)}) collective-permute-start(bf16[128,1920]{1,0:T(8,128)(2,1)S(1)} %collective-permute-done.5), channel_id=1, source_target_pairs={{0,48},{1,49},{2,50},{3,51},{4,52},{5,53},{6,54},{7,55},{8,56},{9,... | collective-permute-start | bytes 1474568 | tf_op jit(solution)/shard_map/ppermute | solution.py:31
  39.4 3.0 %collective-permute-start.13 = (bf16[128,1920]{1,0:T(8,128)(2,1)S(1)}, bf16[128,1920]{1,0:T(8,128)(2,1)S(1)}, u32[]{:S(2)}, u32[]{:S(2)}) collective-permute-start(bf16[128,1920]{1,0:T(8,128)(2,1)S(1)} %collective-permute-done.refs_1_), channel_id=1, source_target_pairs={{0,6},{1,7},{2,0},{3,1},{4,2},{5,3},{6,4},{7,5},{8,14},{9,15},{10,... | collective-permute-start | bytes 1474568 | tf_op jit(solution)/shard_map/ppermute | solution.py:31
  42.3 1.0 collective-permute-start.11
  43.3 1.1 %collective-permute-start.12 = (bf16[128,1920]{1,0:T(8,128)(2,1)S(1)}, bf16[128,1920]{1,0:T(8,128)(2,1)S(1)}, u32[]{:S(2)}, u32[]{:S(2)}) collective-permute-start(bf16[128,1920]{1,0:T(8,128)(2,1)S(1)} %collective-permute-done.4.refs_3_), channel_id=1, source_target_pairs={{0,1},{1,0},{2,3},{3,2},{4,5},{5,4},{6,7},{7,6},{8,9},{9,8},{10,11... | collective-permute-start | bytes 1474568 | tf_op jit(solution)/shard_map/ppermute | solution.py:31
  44.4 3.5 %near_tile.1 = (f32[384,768]{1,0:T(8,128)S(1)}, f32[512,768]{1,0:T(8,128)S(1)}, f32[512,768]{1,0:T(8,128)S(1)}, f32[8,128]{1,0:T(8,128)S(1)}) custom-call(bf16[128,1920]{1,0:T(8,128)(2,1)S(1)} %get-tuple-element.67.refs_0_, bf16[128,1920]{1,0:T(8,128)(2,1)S(1)} %collective-permute-done.refs_1_, bf16[128,1920]{1,0:T(8,128)(2,1)S(1)} %collective-permute-done.1.refs_2_, ...), custom_call_target="tpu_custom_call" | custom-call | flops 2717908992 | bytes 5406720 | tf_op jit(solution)/shard_map/near_tile/pallas_call | solution.py:72
  47.9 7.1 %mid_tile.1 = (f32[768,768]{1,0:T(8,128)S(1)}, f32[768,768]{1,0:T(8,128)S(1)}, f32[768,768]{1,0:T(8,128)S(1)}, f32[8,128]{1,0:T(8,128)S(1)}) custom-call(bf16[128,1920]{1,0:T(8,128)(2,1)S(1)} %get-tuple-element.67.refs_0_, bf16[128,1920]{1,0:T(8,128)(2,1)S(1)} %collective-permute-done.refs_1_, bf16[128,1920]{1,0:T(8,128)(2,1)S(1)} %collective-permute-done.1.refs_2_, ...), custom_call_target="tpu_custom_call" | custom-call | flops 5435817984 | bytes 13176832 | tf_op jit(solution)/shard_map/mid_tile/pallas_call | solution.py:72
  55.0 1.2 %collective-permute-done.11 = bf16[128,1920]{1,0:T(8,128)(2,1)S(1)} collective-permute-done((bf16[128,1920]{1,0:T(8,128)(2,1)S(1)}, bf16[128,1920]{1,0:T(8,128)(2,1)S(1)}, u32[]{:S(2)}, u32[]{:S(2)}) %collective-permute-start.11) | collective-permute-done | bytes 491552 | tf_op jit(solution)/shard_map/ppermute | solution.py:31
  56.3 0.3 collective-permute-start.16
  56.6 3.4 %last_coef.1 = (bf16[1536,256]{1,0:T(8,128)(2,1)S(1)}, bf16[1024,256]{1,0:T(8,128)(2,1)S(1)}, f32[8,128]{1,0:T(8,128)S(1)}) custom-call(bf16[128,1920]{1,0:T(8,128)(2,1)S(1)} %get-tuple-element.67.refs_0_, bf16[128,1920]{1,0:T(8,128)(2,1)S(1)} %collective-permute-done.refs_1_, bf16[128,1920]{1,0:T(8,128)(2,1)S(1)} %collective-permute-done.1.refs_2_, ...), custom_call_target="tpu_custom_call" | custom-call | flops 2516582400 | bytes 10817536 | tf_op jit(solution)/shard_map/last_coef/pallas_call | solution.py:72
  60.0 1.5 %end_coef.1 = (bf16[1024,256]{1,0:T(8,128)(2,1)S(1)}, f32[8,128]{1,0:T(8,128)S(1)}) custom-call(bf16[128,1920]{1,0:T(8,128)(2,1)S(1)} %get-tuple-element.67.refs_0_, bf16[128,1920]{1,0:T(8,128)(2,1)S(1)} %collective-permute-done.refs_1_, bf16[128,1920]{1,0:T(8,128)(2,1)S(1)} %collective-permute-done.1.refs_2_, ...), custom_call_target="tpu_custom_call" | custom-call | flops 1006632960 | bytes 4919296 | tf_op jit(solution)/shard_map/end_coef/pallas_call | solution.py:72
  61.6 0.6 collective-permute-start.17
  62.1 0.9 other_grad.1
  63.1 0.2 collective-permute-start.18
  63.3 0.9 text_grad.1.own
  64.2 0.2 collective-permute-start.21
  64.4 1.7 %collective-permute-start.20 = (f32[8,128]{1,0:T(8,128)S(1)}, f32[8,128]{1,0:T(8,128)S(1)}, u32[]{:S(2)}, u32[]{:S(2)}) collective-permute-start(f32[8,128]{1,0:T(8,128)S(1)} %add.12), channel_id=1, source_target_pairs={{0,6},{1,7},{2,0},{3,1},{4,2},{5,3},{6,4},{7,5},{8,14},{9,15},{10,... | collective-permute-start | bytes 12296 | tf_op jit(solution)/shard_map/ppermute | solution.py:31
  66.0 0.4 collective-permute-start.19
  66.4 1.7 %image_grad.1 = (f32[256,768]{1,0:T(8,128)S(1)}, bf16[256,768]{1,0:T(8,128)(2,1)S(1)}, bf16[256,768]{1,0:T(8,128)(2,1)S(1)}, f32[128,768]{1,0:T(8,128)S(1)}, bf16[128,768]{1,0:T(8,128)(2,1)S(1)}) custom-call(bf16[512,1920]{1,0:T(8,128)(2,1)S(1)} %constant_dynamic-update-slice_fusion.refs_3_.refs_6_.refs_8_.refs_0_, ...), custom_call_target="tpu_custom_call" | custom-call | flops 1409286144 | bytes 12058624 | tf_op jit(solution)/shard_map/image_grad/pallas_call | solution.py:72
  68.1 1.3 %collective-permute-done.21 = f32[8,128]{1,0:T(8,128)S(1)} collective-permute-done((f32[8,128]{1,0:T(8,128)S(1)}, f32[8,128]{1,0:T(8,128)S(1)}, u32[]{:S(2)}, u32[]{:S(2)}) %collective-permute-start.21) | collective-permute-done | bytes 4128 | tf_op jit(solution)/shard_map/ppermute | solution.py:31
  69.4 1.4 %collective-permute-done.19 = f32[8,128]{1,0:T(8,128)S(1)} collective-permute-done((f32[8,128]{1,0:T(8,128)S(1)}, f32[8,128]{1,0:T(8,128)S(1)}, u32[]{:S(2)}, u32[]{:S(2)}) %collective-permute-start.19) | collective-permute-done | bytes 4128 | tf_op jit(solution)/shard_map/ppermute | solution.py:31
  70.9 0.3 text_sum.1
  71.1 1.1 %collective-permute-start.22 = (bf16[272,768]{1,0:T(8,128)(2,1)S(1)}, bf16[272,768]{1,0:T(8,128)(2,1)S(1)}, u32[]{:S(2)}, u32[]{:S(2)}) collective-permute-start(bf16[272,768]{1,0:T(8,128)(2,1)S(1)} %get-tuple-element.103), channel_id=1, source_target_pairs={{0,48},{1,49},{2,50},{3,51},{4,52},{5,53},{6,54},{7,55},{8,56},{9,... | collective-permute-start | bytes 1253384 | tf_op jit(solution)/shard_map/ppermute | solution.py:31
  72.2 1.0 %collective-permute-start.23 = (bf16[272,768]{1,0:T(8,128)(2,1)S(1)}, bf16[272,768]{1,0:T(8,128)(2,1)S(1)}, u32[]{:S(2)}, u32[]{:S(2)}) collective-permute-start(bf16[272,768]{1,0:T(8,128)(2,1)S(1)} %get-tuple-element.104), channel_id=1, source_target_pairs={{0,16},{1,17},{2,18},{3,19},{4,20},{5,21},{6,22},{7,23},{8,24},{9,... | collective-permute-start | bytes 1253384 | tf_op jit(solution)/shard_map/ppermute | solution.py:31
  73.2 1.1 %collective-permute-start.26 = (bf16[256,768]{1,0:T(8,128)(2,1)S(1)}, bf16[256,768]{1,0:T(8,128)(2,1)S(1)}, u32[]{:S(2)}, u32[]{:S(2)}) collective-permute-start(bf16[256,768]{1,0:T(8,128)(2,1)S(1)} %get-tuple-element.108), channel_id=1, source_target_pairs={{0,6},{1,7},{2,0},{3,1},{4,2},{5,3},{6,4},{7,5},{8,14},{9,15},{10,... | collective-permute-start | bytes 1179656 | tf_op jit(solution)/shard_map/ppermute | solution.py:31
  74.4 0.9 collective-permute-start.27
  75.3 0.6 collective-permute-start.28
  75.8 5.1 %collective-permute-done.28.from_z = bf16[128,768]{1,0:T(8,128)(2,1)S(1)} collective-permute-done((bf16[128,768]{1,0:T(8,128)(2,1)S(1)}, bf16[128,768]{1,0:T(8,128)(2,1)S(1)}, u32[]{:S(2)}, u32[]{:S(2)}) %collective-permute-start.28) | collective-permute-done | bytes 196640 | tf_op jit(solution)/shard_map/ppermute | solution.py:31
  80.9 1.7 %collective-permute-start.24 = (bf16[128,768]{1,0:T(8,128)(2,1)S(1)}, bf16[128,768]{1,0:T(8,128)(2,1)S(1)}, u32[]{:S(2)}, u32[]{:S(2)}) collective-permute-start(bf16[128,768]{1,0:T(8,128)(2,1)S(1)} %get-tuple-element.106), channel_id=1, source_target_pairs={{0,65},{1,64},{2,67},{3,66},{4,69},{5,68},{6,71},{7,70},{8,73},{9,... | collective-permute-start | bytes 589832 | tf_op jit(solution)/shard_map/ppermute | solution.py:31
  82.7 1.7 %collective-permute-start.25 = (f32[8,128]{1,0:T(8,128)S(1)}, f32[8,128]{1,0:T(8,128)S(1)}, u32[]{:S(2)}, u32[]{:S(2)}) collective-permute-start(f32[8,128]{1,0:T(8,128)S(1)} %add_add_fusion.loss), channel_id=1, source_target_pairs={{0,32},{1,33},{2,34},{3,35},{4,36},{5,37},{6,38},{7,39},{8,40},{9,... | collective-permute-start | bytes 12296 | tf_op jit(solution)/shard_map/ppermute | solution.py:31
  84.4 0.3 collective-permute-done.27.two
  84.7 0.1 image_ring.1
  84.9 2.9 %collective-permute-done.25.loss_far = f32[8,128]{1,0:T(8,128)S(1)} collective-permute-done((f32[8,128]{1,0:T(8,128)S(1)}, f32[8,128]{1,0:T(8,128)S(1)}, u32[]{:S(2)}, u32[]{:S(2)}) %collective-permute-start.25) | collective-permute-done | bytes 4128 | tf_op jit(solution)/shard_map/ppermute | solution.py:31
  87.8 0.0 collective-permute-done.24.from_z
  87.8 0.3 text_ring.1
  88.1 1.8 %collective-permute-start.30 = (bf16[144,768]{1,0:T(8,128)(2,1)S(1)}, bf16[144,768]{1,0:T(8,128)(2,1)S(1)}, u32[]{:S(2)}, u32[]{:S(2)}) collective-permute-start(bf16[144,768]{1,0:T(8,128)(2,1)S(1)} %get-tuple-element.115), channel_id=1, source_target_pairs={{0,65},{1,64},{2,67},{3,66},{4,69},{5,68},{6,71},{7,70},{8,73},{9,... | collective-permute-start | bytes 663560 | tf_op jit(solution)/shard_map/ppermute | solution.py:31
  89.9 0.4 collective-permute-start.32
  90.3 0.9 collective-permute-start.33
  91.2 1.7 %collective-permute-start.31 = (bf16[128,768]{1,0:T(8,128)(2,1)S(1)}, bf16[128,768]{1,0:T(8,128)(2,1)S(1)}, u32[]{:S(2)}, u32[]{:S(2)}) collective-permute-start(bf16[128,768]{1,0:T(8,128)(2,1)S(1)} %get-tuple-element.116), channel_id=1, source_target_pairs={{0,32},{1,33},{2,34},{3,35},{4,36},{5,37},{6,38},{7,39},{8,40},{9,... | collective-permute-start | bytes 589832 | tf_op jit(solution)/shard_map/ppermute | solution.py:31
  92.9 3.0 %collective-permute-start.29 = (f32[8,128]{1,0:T(8,128)S(1)}, f32[8,128]{1,0:T(8,128)S(1)}, u32[]{:S(2)}, u32[]{:S(2)}) collective-permute-start(f32[8,128]{1,0:T(8,128)S(1)} %get-tuple-element.113.loss), channel_id=1, source_target_pairs={{0,64},{1,65},{2,66},{3,67},{4,68},{5,69},{6,70},{7,71},{8,72},{9,... | collective-permute-start | bytes 12296 | tf_op jit(solution)/shard_map/ppermute | solution.py:31
  95.8 1.6 %collective-permute-done.33.img_x = bf16[128,768]{1,0:T(8,128)(2,1)S(1)} collective-permute-done((bf16[128,768]{1,0:T(8,128)(2,1)S(1)}, bf16[128,768]{1,0:T(8,128)(2,1)S(1)}, u32[]{:S(2)}, u32[]{:S(2)}) %collective-permute-start.33) | collective-permute-done | bytes 196640 | tf_op jit(solution)/shard_map/ppermute | solution.py:31
  97.5 0.5 collective-permute-done.29.loss_far
  98.0 0.4 collective-permute-done.31.txt_x
  98.4 1.3 %finish.1 = (f32[128,768]{1,0:T(8,128)}, f32[128,768]{1,0:T(8,128)}, f32[1,1]{1,0:T(1,128)}) custom-call(f32[8,128]{1,0:T(8,128)S(1)} %get-tuple-element.113.loss, f32[8,128]{1,0:T(8,128)S(1)} %collective-permute-done.29.loss_far, f32[128,768]{1,0:T(8,128)S(1)} %get-tuple-element.114.txt, bf16[144,768]{1,0:T(8,128)(2,1)S(1)} %collective-permute-done.30.txt_z, ...), custom_call_target="tpu_custom_call" | custom-call | bytes 2023424 | tf_op jit(solution)/shard_map/finish/pallas_call | solution.py:72
  (30 shorter events, 0.4 us)
Async XLA Ops:
  2.2 15.4 %collective-permute-start.5 = (bf16[128,1920]{1,0:T(8,128)(2,1)S(1)}, bf16[128,1920]{1,0:T(8,128)(2,1)S(1)}, u32[]{:S(2)}, u32[]{:S(2)}) collective-permute-start(bf16[128,1920]{1,0:T(8,128)(2,1)S(1)} %get-tuple-element.64), channel_id=1, source_target_pairs={{0,65},{1,64},{2,67},{3,66},{4,69},{5,68},{6,71},{7,70},{8,73},{9,... | collective-permute-start | bytes 1474568 | tf_op jit(solution)/shard_map/ppermute | solution.py:31
  6.4 14.0 %collective-permute-start.2 = (bf16[128,1920]{1,0:T(8,128)(2,1)S(1)}, bf16[128,1920]{1,0:T(8,128)(2,1)S(1)}, u32[]{:S(2)}, u32[]{:S(2)}) collective-permute-start(bf16[128,1920]{1,0:T(8,128)(2,1)S(1)} %get-tuple-element.64), channel_id=1, source_target_pairs={{0,16},{1,17},{2,18},{3,19},{4,20},{5,21},{6,22},{7,23},{8,24},{9,... | collective-permute-start | bytes 1474568 | tf_op jit(solution)/shard_map/ppermute | solution.py:31
  8.0 12.7 %collective-permute-start = (bf16[128,1920]{1,0:T(8,128)(2,1)S(1)}, bf16[128,1920]{1,0:T(8,128)(2,1)S(1)}, u32[]{:S(2)}, u32[]{:S(2)}) collective-permute-start(bf16[128,1920]{1,0:T(8,128)(2,1)S(1)} %get-tuple-element.67.refs_0_), channel_id=1, source_target_pairs={{0,1},{1,0},{2,3},{3,2},{4,5},{5,4},{6,7},{7,6},{8,9},{9,8},{10,11... | collective-permute-start | bytes 1474568 | tf_op jit(solution)/shard_map/ppermute | solution.py:31
  8.0 13.6 %collective-permute-start.1 = (bf16[128,1920]{1,0:T(8,128)(2,1)S(1)}, bf16[128,1920]{1,0:T(8,128)(2,1)S(1)}, u32[]{:S(2)}, u32[]{:S(2)}) collective-permute-start(bf16[128,1920]{1,0:T(8,128)(2,1)S(1)} %get-tuple-element.67.refs_0_), channel_id=1, source_target_pairs={{0,2},{1,3},{2,4},{3,5},{4,6},{5,7},{6,0},{7,1},{8,10},{9,11},{10,... | collective-permute-start | bytes 1474568 | tf_op jit(solution)/shard_map/ppermute | solution.py:31
  9.5 15.7 %collective-permute-start.9 = (bf16[128,1920]{1,0:T(8,128)(2,1)S(1)}, bf16[128,1920]{1,0:T(8,128)(2,1)S(1)}, u32[]{:S(2)}, u32[]{:S(2)}) collective-permute-start(bf16[128,1920]{1,0:T(8,128)(2,1)S(1)} %get-tuple-element.64), channel_id=1, source_target_pairs={{0,48},{1,49},{2,50},{3,51},{4,52},{5,53},{6,54},{7,55},{8,56},{9,... | collective-permute-start | bytes 1474568 | tf_op jit(solution)/shard_map/ppermute | solution.py:31
  20.4 13.0 %collective-permute-start.6 = (bf16[128,1920]{1,0:T(8,128)(2,1)S(1)}, bf16[128,1920]{1,0:T(8,128)(2,1)S(1)}, u32[]{:S(2)}, u32[]{:S(2)}) collective-permute-start(bf16[128,1920]{1,0:T(8,128)(2,1)S(1)} %collective-permute-done.2), channel_id=1, source_target_pairs={{0,65},{1,64},{2,67},{3,66},{4,69},{5,68},{6,71},{7,70},{8,73},{9,... | collective-permute-start | bytes 1474568 | tf_op jit(solution)/shard_map/ppermute | solution.py:31
  21.6 15.2 %collective-permute-start.7 = (bf16[128,1920]{1,0:T(8,128)(2,1)S(1)}, bf16[128,1920]{1,0:T(8,128)(2,1)S(1)}, u32[]{:S(2)}, u32[]{:S(2)}) collective-permute-start(bf16[128,1920]{1,0:T(8,128)(2,1)S(1)} %collective-permute-done.1.refs_2_), channel_id=1, source_target_pairs={{0,1},{1,0},{2,3},{3,2},{4,5},{5,4},{6,7},{7,6},{8,9},{9,8},{10,11... | collective-permute-start | bytes 1474568 | tf_op jit(solution)/shard_map/ppermute | solution.py:31
  23.4 12.1 %collective-permute-start.3 = (bf16[128,1920]{1,0:T(8,128)(2,1)S(1)}, bf16[128,1920]{1,0:T(8,128)(2,1)S(1)}, u32[]{:S(2)}, u32[]{:S(2)}) collective-permute-start(bf16[128,1920]{1,0:T(8,128)(2,1)S(1)} %collective-permute-done.2), channel_id=1, source_target_pairs={{0,16},{1,17},{2,18},{3,19},{4,20},{5,21},{6,22},{7,23},{8,24},{9,... | collective-permute-start | bytes 1474568 | tf_op jit(solution)/shard_map/ppermute | solution.py:31
  24.9 11.8 %collective-permute-start.4 = (bf16[128,1920]{1,0:T(8,128)(2,1)S(1)}, bf16[128,1920]{1,0:T(8,128)(2,1)S(1)}, u32[]{:S(2)}, u32[]{:S(2)}) collective-permute-start(bf16[128,1920]{1,0:T(8,128)(2,1)S(1)} %collective-permute-done.1.refs_2_), channel_id=1, source_target_pairs={{0,2},{1,3},{2,4},{3,5},{4,6},{5,7},{6,0},{7,1},{8,10},{9,11},{10,... | collective-permute-start | bytes 1474568 | tf_op jit(solution)/shard_map/ppermute | solution.py:31
  25.2 11.6 %collective-permute-start.8 = (bf16[128,1920]{1,0:T(8,128)(2,1)S(1)}, bf16[128,1920]{1,0:T(8,128)(2,1)S(1)}, u32[]{:S(2)}, u32[]{:S(2)}) collective-permute-start(bf16[128,1920]{1,0:T(8,128)(2,1)S(1)} %get-tuple-element.67.refs_0_), channel_id=1, source_target_pairs={{0,6},{1,7},{2,0},{3,1},{4,2},{5,3},{6,4},{7,5},{8,14},{9,15},{10,... | collective-permute-start | bytes 1474568 | tf_op jit(solution)/shard_map/ppermute | solution.py:31
  36.9 6.4 %collective-permute-start.14 = (bf16[512,1920]{1,0:T(8,128)(2,1)S(1)}, bf16[512,1920]{1,0:T(8,128)(2,1)S(1)}, u32[]{:S(2)}, u32[]{:S(2)}) collective-permute-start(bf16[512,1920]{1,0:T(8,128)(2,1)S(1)} %constant_dynamic-update-slice_fusion.refs_3_.refs_6_.refs_8_.refs_0_), channel_id=1, source_target_pairs={{0,8},{1,9},{2,10},{3,11},{4,12},{5,13},{6,14},{7,15},{8,0},{9,1},... | collective-permute-start | bytes 5898248 | tf_op jit(solution)/shard_map/ppermute | solution.py:31
  37.1 10.7 %collective-permute-start.15 = (bf16[256,1920]{1,0:T(8,128)(2,1)S(1)}, bf16[256,1920]{1,0:T(8,128)(2,1)S(1)}, u32[]{:S(2)}, u32[]{:S(2)}) collective-permute-start(bf16[256,1920]{1,0:T(8,128)(2,1)S(1)} %constant_dynamic-update-slice_fusion.4.refs_8_.refs_9_.refs_1_), channel_id=1, source_target_pairs={{0,8},{1,9},{2,10},{3,11},{4,12},{5,13},{6,14},{7,15},{8,0},{9,1},... | collective-permute-start | bytes 2949128 | tf_op jit(solution)/shard_map/ppermute | solution.py:31
  37.7 17.3 %collective-permute-start.10 = (bf16[128,1920]{1,0:T(8,128)(2,1)S(1)}, bf16[128,1920]{1,0:T(8,128)(2,1)S(1)}, u32[]{:S(2)}, u32[]{:S(2)}) collective-permute-start(bf16[128,1920]{1,0:T(8,128)(2,1)S(1)} %collective-permute-done.5), channel_id=1, source_target_pairs={{0,48},{1,49},{2,50},{3,51},{4,52},{5,53},{6,54},{7,55},{8,56},{9,... | collective-permute-start | bytes 1474568 | tf_op jit(solution)/shard_map/ppermute | solution.py:31
  39.4 16.8 %collective-permute-start.13 = (bf16[128,1920]{1,0:T(8,128)(2,1)S(1)}, bf16[128,1920]{1,0:T(8,128)(2,1)S(1)}, u32[]{:S(2)}, u32[]{:S(2)}) collective-permute-start(bf16[128,1920]{1,0:T(8,128)(2,1)S(1)} %collective-permute-done.refs_1_), channel_id=1, source_target_pairs={{0,6},{1,7},{2,0},{3,1},{4,2},{5,3},{6,4},{7,5},{8,14},{9,15},{10,... | collective-permute-start | bytes 1474568 | tf_op jit(solution)/shard_map/ppermute | solution.py:31
  42.3 13.9 %collective-permute-start.11 = (bf16[128,1920]{1,0:T(8,128)(2,1)S(1)}, bf16[128,1920]{1,0:T(8,128)(2,1)S(1)}, u32[]{:S(2)}, u32[]{:S(2)}) collective-permute-start(bf16[128,1920]{1,0:T(8,128)(2,1)S(1)} %collective-permute-done.3), channel_id=1, source_target_pairs={{0,65},{1,64},{2,67},{3,66},{4,69},{5,68},{6,71},{7,70},{8,73},{9,... | collective-permute-start | bytes 1474568 | tf_op jit(solution)/shard_map/ppermute | solution.py:31
  43.3 12.9 %collective-permute-start.12 = (bf16[128,1920]{1,0:T(8,128)(2,1)S(1)}, bf16[128,1920]{1,0:T(8,128)(2,1)S(1)}, u32[]{:S(2)}, u32[]{:S(2)}) collective-permute-start(bf16[128,1920]{1,0:T(8,128)(2,1)S(1)} %collective-permute-done.4.refs_3_), channel_id=1, source_target_pairs={{0,1},{1,0},{2,3},{3,2},{4,5},{5,4},{6,7},{7,6},{8,9},{9,8},{10,11... | collective-permute-start | bytes 1474568 | tf_op jit(solution)/shard_map/ppermute | solution.py:31
  56.3 3.7 %collective-permute-start.16 = (bf16[256,1920]{1,0:T(8,128)(2,1)S(1)}, bf16[256,1920]{1,0:T(8,128)(2,1)S(1)}, u32[]{:S(2)}, u32[]{:S(2)}) collective-permute-start(bf16[256,1920]{1,0:T(8,128)(2,1)S(1)} %constant_dynamic-update-slice_fusion.6.refs_12_.refs_4_), channel_id=1, source_target_pairs={{0,8},{1,9},{2,10},{3,11},{4,12},{5,13},{6,14},{7,15},{8,0},{9,1},... | collective-permute-start | bytes 2949128 | tf_op jit(solution)/shard_map/ppermute | solution.py:31
  61.6 1.5 %collective-permute-start.17 = (f32[8,128]{1,0:T(8,128)S(1)}, f32[8,128]{1,0:T(8,128)S(1)}, u32[]{:S(2)}, u32[]{:S(2)}) collective-permute-start(f32[8,128]{1,0:T(8,128)S(1)} %get-tuple-element.94), channel_id=1, source_target_pairs={{0,8},{1,9},{2,10},{3,11},{4,12},{5,13},{6,14},{7,15},{8,0},{9,1},... | collective-permute-start | bytes 12296 | tf_op jit(solution)/shard_map/ppermute | solution.py:31
  63.1 7.8 %collective-permute-start.18 = (bf16[1024,768]{1,0:T(8,128)(2,1)S(1)}, bf16[1024,768]{1,0:T(8,128)(2,1)S(1)}, u32[]{:S(2)}, u32[]{:S(2)}) collective-permute-start(bf16[1024,768]{1,0:T(8,128)(2,1)S(1)} %other_grad.1), channel_id=1, source_target_pairs={{0,8},{1,9},{2,10},{3,11},{4,12},{5,13},{6,14},{7,15},{8,0},{9,1},... | collective-permute-start | bytes 4718600 | tf_op jit(solution)/shard_map/ppermute | solution.py:31
  64.2 5.2 %collective-permute-start.21 = (f32[8,128]{1,0:T(8,128)S(1)}, f32[8,128]{1,0:T(8,128)S(1)}, u32[]{:S(2)}, u32[]{:S(2)}) collective-permute-start(f32[8,128]{1,0:T(8,128)S(1)} %add.12), channel_id=1, source_target_pairs={{0,4},{1,5},{2,6},{3,7},{4,0},{5,1},{6,2},{7,3},{8,12},{9,13},{10,... | collective-permute-start | bytes 12296 | tf_op jit(solution)/shard_map/ppermute | solution.py:31
  64.4 5.0 %collective-permute-start.20 = (f32[8,128]{1,0:T(8,128)S(1)}, f32[8,128]{1,0:T(8,128)S(1)}, u32[]{:S(2)}, u32[]{:S(2)}) collective-permute-start(f32[8,128]{1,0:T(8,128)S(1)} %add.12), channel_id=1, source_target_pairs={{0,6},{1,7},{2,0},{3,1},{4,2},{5,3},{6,4},{7,5},{8,14},{9,15},{10,... | collective-permute-start | bytes 12296 | tf_op jit(solution)/shard_map/ppermute | solution.py:31
  66.0 4.8 %collective-permute-start.19 = (f32[8,128]{1,0:T(8,128)S(1)}, f32[8,128]{1,0:T(8,128)S(1)}, u32[]{:S(2)}, u32[]{:S(2)}) collective-permute-start(f32[8,128]{1,0:T(8,128)S(1)} %add.12), channel_id=1, source_target_pairs={{0,2},{1,3},{2,4},{3,5},{4,6},{5,7},{6,0},{7,1},{8,10},{9,11},{10,... | collective-permute-start | bytes 12296 | tf_op jit(solution)/shard_map/ppermute | solution.py:31
  71.1 16.7 %collective-permute-start.22 = (bf16[272,768]{1,0:T(8,128)(2,1)S(1)}, bf16[272,768]{1,0:T(8,128)(2,1)S(1)}, u32[]{:S(2)}, u32[]{:S(2)}) collective-permute-start(bf16[272,768]{1,0:T(8,128)(2,1)S(1)} %get-tuple-element.103), channel_id=1, source_target_pairs={{0,48},{1,49},{2,50},{3,51},{4,52},{5,53},{6,54},{7,55},{8,56},{9,... | collective-permute-start | bytes 1253384 | tf_op jit(solution)/shard_map/ppermute | solution.py:31
  72.2 15.6 %collective-permute-start.23 = (bf16[272,768]{1,0:T(8,128)(2,1)S(1)}, bf16[272,768]{1,0:T(8,128)(2,1)S(1)}, u32[]{:S(2)}, u32[]{:S(2)}) collective-permute-start(bf16[272,768]{1,0:T(8,128)(2,1)S(1)} %get-tuple-element.104), channel_id=1, source_target_pairs={{0,16},{1,17},{2,18},{3,19},{4,20},{5,21},{6,22},{7,23},{8,24},{9,... | collective-permute-start | bytes 1253384 | tf_op jit(solution)/shard_map/ppermute | solution.py:31
  73.2 9.4 %collective-permute-start.26 = (bf16[256,768]{1,0:T(8,128)(2,1)S(1)}, bf16[256,768]{1,0:T(8,128)(2,1)S(1)}, u32[]{:S(2)}, u32[]{:S(2)}) collective-permute-start(bf16[256,768]{1,0:T(8,128)(2,1)S(1)} %get-tuple-element.108), channel_id=1, source_target_pairs={{0,6},{1,7},{2,0},{3,1},{4,2},{5,3},{6,4},{7,5},{8,14},{9,15},{10,... | collective-permute-start | bytes 1179656 | tf_op jit(solution)/shard_map/ppermute | solution.py:31
  74.4 10.3 %collective-permute-start.27 = (bf16[256,768]{1,0:T(8,128)(2,1)S(1)}, bf16[256,768]{1,0:T(8,128)(2,1)S(1)}, u32[]{:S(2)}, u32[]{:S(2)}) collective-permute-start(bf16[256,768]{1,0:T(8,128)(2,1)S(1)} %get-tuple-element.109), channel_id=1, source_target_pairs={{0,2},{1,3},{2,4},{3,5},{4,6},{5,7},{6,0},{7,1},{8,10},{9,11},{10,... | collective-permute-start | bytes 1179656 | tf_op jit(solution)/shard_map/ppermute | solution.py:31
  75.3 5.7 %collective-permute-start.28 = (bf16[128,768]{1,0:T(8,128)(2,1)S(1)}, bf16[128,768]{1,0:T(8,128)(2,1)S(1)}, u32[]{:S(2)}, u32[]{:S(2)}) collective-permute-start(bf16[128,768]{1,0:T(8,128)(2,1)S(1)} %get-tuple-element.111), channel_id=1, source_target_pairs={{0,1},{1,0},{2,3},{3,2},{4,5},{5,4},{6,7},{7,6},{8,9},{9,8},{10,11... | collective-permute-start | bytes 589832 | tf_op jit(solution)/shard_map/ppermute | solution.py:31
  80.9 6.9 %collective-permute-start.24 = (bf16[128,768]{1,0:T(8,128)(2,1)S(1)}, bf16[128,768]{1,0:T(8,128)(2,1)S(1)}, u32[]{:S(2)}, u32[]{:S(2)}) collective-permute-start(bf16[128,768]{1,0:T(8,128)(2,1)S(1)} %get-tuple-element.106), channel_id=1, source_target_pairs={{0,65},{1,64},{2,67},{3,66},{4,69},{5,68},{6,71},{7,70},{8,73},{9,... | collective-permute-start | bytes 589832 | tf_op jit(solution)/shard_map/ppermute | solution.py:31
  82.7 5.1 %collective-permute-start.25 = (f32[8,128]{1,0:T(8,128)S(1)}, f32[8,128]{1,0:T(8,128)S(1)}, u32[]{:S(2)}, u32[]{:S(2)}) collective-permute-start(f32[8,128]{1,0:T(8,128)S(1)} %add_add_fusion.loss), channel_id=1, source_target_pairs={{0,32},{1,33},{2,34},{3,35},{4,36},{5,37},{6,38},{7,39},{8,40},{9,... | collective-permute-start | bytes 12296 | tf_op jit(solution)/shard_map/ppermute | solution.py:31
  84.7 13.6 %copy-start = (bf16[128,768]{1,0:T(8,128)(2,1)S(1)}, bf16[128,768]{1,0:T(8,128)(2,1)}, u32[]{:S(2)}) copy-start(bf16[128,768]{1,0:T(8,128)(2,1)} %si.3) | copy-start | bytes 589828
  84.7 13.6 %copy-start.1 = (bf16[128,768]{1,0:T(8,128)(2,1)S(1)}, bf16[128,768]{1,0:T(8,128)(2,1)}, u32[]{:S(2)}) copy-start(bf16[128,768]{1,0:T(8,128)(2,1)} %st.3) | copy-start | bytes 589828
  88.1 10.3 %collective-permute-start.30 = (bf16[144,768]{1,0:T(8,128)(2,1)S(1)}, bf16[144,768]{1,0:T(8,128)(2,1)S(1)}, u32[]{:S(2)}, u32[]{:S(2)}) collective-permute-start(bf16[144,768]{1,0:T(8,128)(2,1)S(1)} %get-tuple-element.115), channel_id=1, source_target_pairs={{0,65},{1,64},{2,67},{3,66},{4,69},{5,68},{6,71},{7,70},{8,73},{9,... | collective-permute-start | bytes 663560 | tf_op jit(solution)/shard_map/ppermute | solution.py:31
  89.9 8.4 %collective-permute-start.32 = (bf16[144,768]{1,0:T(8,128)(2,1)S(1)}, bf16[144,768]{1,0:T(8,128)(2,1)S(1)}, u32[]{:S(2)}, u32[]{:S(2)}) collective-permute-start(bf16[144,768]{1,0:T(8,128)(2,1)S(1)} %get-tuple-element.118), channel_id=1, source_target_pairs={{0,1},{1,0},{2,3},{3,2},{4,5},{5,4},{6,7},{7,6},{8,9},{9,8},{10,11... | collective-permute-start | bytes 663560 | tf_op jit(solution)/shard_map/ppermute | solution.py:31
  90.3 7.2 %collective-permute-start.33 = (bf16[128,768]{1,0:T(8,128)(2,1)S(1)}, bf16[128,768]{1,0:T(8,128)(2,1)S(1)}, u32[]{:S(2)}, u32[]{:S(2)}) collective-permute-start(bf16[128,768]{1,0:T(8,128)(2,1)S(1)} %get-tuple-element.119), channel_id=1, source_target_pairs={{0,4},{1,5},{2,6},{3,7},{4,0},{5,1},{6,2},{7,3},{8,12},{9,13},{10,... | collective-permute-start | bytes 589832 | tf_op jit(solution)/shard_map/ppermute | solution.py:31
  91.2 7.2 %collective-permute-start.31 = (bf16[128,768]{1,0:T(8,128)(2,1)S(1)}, bf16[128,768]{1,0:T(8,128)(2,1)S(1)}, u32[]{:S(2)}, u32[]{:S(2)}) collective-permute-start(bf16[128,768]{1,0:T(8,128)(2,1)S(1)} %get-tuple-element.116), channel_id=1, source_target_pairs={{0,32},{1,33},{2,34},{3,35},{4,36},{5,37},{6,38},{7,39},{8,40},{9,... | collective-permute-start | bytes 589832 | tf_op jit(solution)/shard_map/ppermute | solution.py:31
  92.9 5.1 %collective-permute-start.29 = (f32[8,128]{1,0:T(8,128)S(1)}, f32[8,128]{1,0:T(8,128)S(1)}, u32[]{:S(2)}, u32[]{:S(2)}) collective-permute-start(f32[8,128]{1,0:T(8,128)S(1)} %get-tuple-element.113.loss), channel_id=1, source_target_pairs={{0,64},{1,65},{2,66},{3,67},{4,68},{5,69},{6,70},{7,71},{8,72},{9,... | collective-permute-start | bytes 12296 | tf_op jit(solution)/shard_map/ppermute | solution.py:31

commit v4 on v3

--- a/solution.py
+++ b/solution.py
@@ -184,7 +184,7 @@
 
 
 def text_sum_kernel(own, from_core, loss, t0, t1, t2, t3, t4):
-    at = lambda low, high: own[low:high, :] + from_core[low:high, :].astype(f32)
+    at = lambda low, high: own[low:high, :] + from_core[low:high, :]
     t0[...] = at(0, 256)
     t1[0:128, :] = at(256, 384).astype(bf16)
     t1[128:256, :] = at(640, 768).astype(bf16)
@@ -317,7 +317,7 @@
     grad_work = 2 * (12 + 16) * rows * rows * width_s
     grad_o = call(
         run(text_grad_kernel, width_t, 1), "other_grad", (*imgs, coef_p, coef_u, p_oth),
-        [((8 * rows, width_s), bf16)], flops=grad_work,
+        [((8 * rows, width_s), f32)], flops=grad_work,
     )[0]
     grad_o, loss_core = hold((grad_o, loss_core))
     from_core = to_core(grad_o)

time: 101 us -> 101 us (level)
  no operation moved by 1% of the time
where the time goes in v4:
time: 101 us; the launch traced here: 99.9 us
  starting transfers between devices  42.3 us (42%)
  waiting for transfers between devices  33.6 us (33%)
  Pallas kernels  22.8 us (23%)
    ppermute x34, starting transfers between devices, permute(): return lax.ppermute(value, AXES, pairs)  42.3 us
    ppermute x34, waiting for transfers between devices, permute(): return lax.ppermute(value, AXES, pairs)  33.6 us
    pallas_call x12, Pallas kernels, call(): pl.pallas_call(kernel, out_shape=tuple((shape_of(shape, dtype) for shape,...  22.8 us
  transfers between devices with their start and end apart: 34, of which 15 were waited for; matrix products, arithmetic and copies ran while one was open for 0% of the time, Pallas kernels for 18%

profile of v4, /device:TPU:0, one launch (start us, length us, event | category | flops | bytes accessed | tf_op | source)
XLA Modules:
  0.0 99.9 jit_solution(14745124803498441204)
XLA Ops:
  0.6 1.6 %units.1 = (bf16[128,1920]{1,0:T(8,128)(2,1)S(1)}, bf16[128,1920]{1,0:T(8,128)(2,1)S(1)}) custom-call(bf16[128,1152]{1,0:T(8,128)(2,1)} %ti.1, bf16[128,768]{1,0:T(8,128)(2,1)} %si.3, bf16[128,1152]{1,0:T(8,128)(2,1)} %tt.1, bf16[128,768]{1,0:T(8,128)(2,1)} %st.3), custom_call_target="tpu_custom_call" | custom-call | bytes 983040 | tf_op jit(solution)/shard_map/units/pallas_call | solution.py:72
  2.2 4.2 %collective-permute-start.5 = (bf16[128,1920]{1,0:T(8,128)(2,1)S(1)}, bf16[128,1920]{1,0:T(8,128)(2,1)S(1)}, u32[]{:S(2)}, u32[]{:S(2)}) collective-permute-start(bf16[128,1920]{1,0:T(8,128)(2,1)S(1)} %get-tuple-element.64), channel_id=1, source_target_pairs={{0,65},{1,64},{2,67},{3,66},{4,69},{5,68},{6,71},{7,70},{8,73},{9,... | collective-permute-start | bytes 1474568 | tf_op jit(solution)/shard_map/ppermute | solution.py:31
  6.4 1.6 %collective-permute-start.2 = (bf16[128,1920]{1,0:T(8,128)(2,1)S(1)}, bf16[128,1920]{1,0:T(8,128)(2,1)S(1)}, u32[]{:S(2)}, u32[]{:S(2)}) collective-permute-start(bf16[128,1920]{1,0:T(8,128)(2,1)S(1)} %get-tuple-element.64), channel_id=1, source_target_pairs={{0,16},{1,17},{2,18},{3,19},{4,20},{5,21},{6,22},{7,23},{8,24},{9,... | collective-permute-start | bytes 1474568 | tf_op jit(solution)/shard_map/ppermute | solution.py:31
  8.0 0.0 collective-permute-start
  8.0 1.5 %collective-permute-start.1 = (bf16[128,1920]{1,0:T(8,128)(2,1)S(1)}, bf16[128,1920]{1,0:T(8,128)(2,1)S(1)}, u32[]{:S(2)}, u32[]{:S(2)}) collective-permute-start(bf16[128,1920]{1,0:T(8,128)(2,1)S(1)} %get-tuple-element.67.refs_0_), channel_id=1, source_target_pairs={{0,2},{1,3},{2,4},{3,5},{4,6},{5,7},{6,0},{7,1},{8,10},{9,11},{10,... | collective-permute-start | bytes 1474568 | tf_op jit(solution)/shard_map/ppermute | solution.py:31
  9.5 1.7 %collective-permute-start.9 = (bf16[128,1920]{1,0:T(8,128)(2,1)S(1)}, bf16[128,1920]{1,0:T(8,128)(2,1)S(1)}, u32[]{:S(2)}, u32[]{:S(2)}) collective-permute-start(bf16[128,1920]{1,0:T(8,128)(2,1)S(1)} %get-tuple-element.64), channel_id=1, source_target_pairs={{0,48},{1,49},{2,50},{3,51},{4,52},{5,53},{6,54},{7,55},{8,56},{9,... | collective-permute-start | bytes 1474568 | tf_op jit(solution)/shard_map/ppermute | solution.py:31
  11.2 6.5 %collective-permute-done.5 = bf16[128,1920]{1,0:T(8,128)(2,1)S(1)} collective-permute-done((bf16[128,1920]{1,0:T(8,128)(2,1)S(1)}, bf16[128,1920]{1,0:T(8,128)(2,1)S(1)}, u32[]{:S(2)}, u32[]{:S(2)}) %collective-permute-start.5) | collective-permute-done | bytes 491552 | tf_op jit(solution)/shard_map/ppermute | solution.py:31
  17.6 2.7 %collective-permute-done.2 = bf16[128,1920]{1,0:T(8,128)(2,1)S(1)} collective-permute-done((bf16[128,1920]{1,0:T(8,128)(2,1)S(1)}, bf16[128,1920]{1,0:T(8,128)(2,1)S(1)}, u32[]{:S(2)}, u32[]{:S(2)}) %collective-permute-start.2) | collective-permute-done | bytes 491552 | tf_op jit(solution)/shard_map/ppermute | solution.py:31
  20.4 0.4 collective-permute-start.6
  20.7 0.0 collective-permute-done.refs_1_
  20.7 0.9 collective-permute-done.1.refs_2_
  21.6 1.7 %collective-permute-start.7 = (bf16[128,1920]{1,0:T(8,128)(2,1)S(1)}, bf16[128,1920]{1,0:T(8,128)(2,1)S(1)}, u32[]{:S(2)}, u32[]{:S(2)}) collective-permute-start(bf16[128,1920]{1,0:T(8,128)(2,1)S(1)} %collective-permute-done.1.refs_2_), channel_id=1, source_target_pairs={{0,1},{1,0},{2,3},{3,2},{4,5},{5,4},{6,7},{7,6},{8,9},{9,8},{10,11... | collective-permute-start | bytes 1474568 | tf_op jit(solution)/shard_map/ppermute | solution.py:31
  23.4 1.6 %collective-permute-start.3 = (bf16[128,1920]{1,0:T(8,128)(2,1)S(1)}, bf16[128,1920]{1,0:T(8,128)(2,1)S(1)}, u32[]{:S(2)}, u32[]{:S(2)}) collective-permute-start(bf16[128,1920]{1,0:T(8,128)(2,1)S(1)} %collective-permute-done.2), channel_id=1, source_target_pairs={{0,16},{1,17},{2,18},{3,19},{4,20},{5,21},{6,22},{7,23},{8,24},{9,... | collective-permute-start | bytes 1474568 | tf_op jit(solution)/shard_map/ppermute | solution.py:31
  24.9 0.3 collective-permute-start.4
  25.2 3.0 %collective-permute-start.8 = (bf16[128,1920]{1,0:T(8,128)(2,1)S(1)}, bf16[128,1920]{1,0:T(8,128)(2,1)S(1)}, u32[]{:S(2)}, u32[]{:S(2)}) collective-permute-start(bf16[128,1920]{1,0:T(8,128)(2,1)S(1)} %get-tuple-element.67.refs_0_), channel_id=1, source_target_pairs={{0,6},{1,7},{2,0},{3,1},{4,2},{5,3},{6,4},{7,5},{8,14},{9,15},{10,... | collective-permute-start | bytes 1474568 | tf_op jit(solution)/shard_map/ppermute | solution.py:31
  28.2 5.2 %collective-permute-done.6 = bf16[128,1920]{1,0:T(8,128)(2,1)S(1)} collective-permute-done((bf16[128,1920]{1,0:T(8,128)(2,1)S(1)}, bf16[128,1920]{1,0:T(8,128)(2,1)S(1)}, u32[]{:S(2)}, u32[]{:S(2)}) %collective-permute-start.6) | collective-permute-done | bytes 491552 | tf_op jit(solution)/shard_map/ppermute | solution.py:31
  33.4 2.1 %collective-permute-done.3 = bf16[128,1920]{1,0:T(8,128)(2,1)S(1)} collective-permute-done((bf16[128,1920]{1,0:T(8,128)(2,1)S(1)}, bf16[128,1920]{1,0:T(8,128)(2,1)S(1)}, u32[]{:S(2)}, u32[]{:S(2)}) %collective-permute-start.3) | collective-permute-done | bytes 491552 | tf_op jit(solution)/shard_map/ppermute | solution.py:31
  35.5 1.3 %collective-permute-done.4.refs_3_ = bf16[128,1920]{1,0:T(8,128)(2,1)S(1)} collective-permute-done((bf16[128,1920]{1,0:T(8,128)(2,1)S(1)}, bf16[128,1920]{1,0:T(8,128)(2,1)S(1)}, u32[]{:S(2)}, u32[]{:S(2)}) %collective-permute-start.4) | collective-permute-done | bytes 491552 | tf_op jit(solution)/shard_map/ppermute | solution.py:31
  36.8 0.0 collective-permute-done.7.refs_4_
  36.9 0.1 collective-permute-start.14
  37.1 0.6 collective-permute-start.15
  37.7 1.7 %collective-permute-start.10 = (bf16[128,1920]{1,0:T(8,128)(2,1)S(1)}, bf16[128,1920]{1,0:T(8,128)(2,1)S(1)}, u32[]{:S(2)}, u32[]{:S(2)}) collective-permute-start(bf16[128,1920]{1,0:T(8,128)(2,1)S(1)} %collective-permute-done.5), channel_id=1, source_target_pairs={{0,48},{1,49},{2,50},{3,51},{4,52},{5,53},{6,54},{7,55},{8,56},{9,... | collective-permute-start | bytes 1474568 | tf_op jit(solution)/shard_map/ppermute | solution.py:31
  39.4 3.0 %collective-permute-start.13 = (bf16[128,1920]{1,0:T(8,128)(2,1)S(1)}, bf16[128,1920]{1,0:T(8,128)(2,1)S(1)}, u32[]{:S(2)}, u32[]{:S(2)}) collective-permute-start(bf16[128,1920]{1,0:T(8,128)(2,1)S(1)} %collective-permute-done.refs_1_), channel_id=1, source_target_pairs={{0,6},{1,7},{2,0},{3,1},{4,2},{5,3},{6,4},{7,5},{8,14},{9,15},{10,... | collective-permute-start | bytes 1474568 | tf_op jit(solution)/shard_map/ppermute | solution.py:31
  42.3 1.0 collective-permute-start.11
  43.3 1.1 %collective-permute-start.12 = (bf16[128,1920]{1,0:T(8,128)(2,1)S(1)}, bf16[128,1920]{1,0:T(8,128)(2,1)S(1)}, u32[]{:S(2)}, u32[]{:S(2)}) collective-permute-start(bf16[128,1920]{1,0:T(8,128)(2,1)S(1)} %collective-permute-done.4.refs_3_), channel_id=1, source_target_pairs={{0,1},{1,0},{2,3},{3,2},{4,5},{5,4},{6,7},{7,6},{8,9},{9,8},{10,11... | collective-permute-start | bytes 1474568 | tf_op jit(solution)/shard_map/ppermute | solution.py:31
  44.4 3.5 %near_tile.1 = (f32[384,768]{1,0:T(8,128)S(1)}, f32[512,768]{1,0:T(8,128)S(1)}, f32[512,768]{1,0:T(8,128)S(1)}, f32[8,128]{1,0:T(8,128)S(1)}) custom-call(bf16[128,1920]{1,0:T(8,128)(2,1)S(1)} %get-tuple-element.67.refs_0_, bf16[128,1920]{1,0:T(8,128)(2,1)S(1)} %collective-permute-done.refs_1_, bf16[128,1920]{1,0:T(8,128)(2,1)S(1)} %collective-permute-done.1.refs_2_, ...), custom_call_target="tpu_custom_call" | custom-call | flops 2717908992 | bytes 5406720 | tf_op jit(solution)/shard_map/near_tile/pallas_call | solution.py:72
  47.9 7.1 %mid_tile.1 = (f32[768,768]{1,0:T(8,128)S(1)}, f32[768,768]{1,0:T(8,128)S(1)}, f32[768,768]{1,0:T(8,128)S(1)}, f32[8,128]{1,0:T(8,128)S(1)}) custom-call(bf16[128,1920]{1,0:T(8,128)(2,1)S(1)} %get-tuple-element.67.refs_0_, bf16[128,1920]{1,0:T(8,128)(2,1)S(1)} %collective-permute-done.refs_1_, bf16[128,1920]{1,0:T(8,128)(2,1)S(1)} %collective-permute-done.1.refs_2_, ...), custom_call_target="tpu_custom_call" | custom-call | flops 5435817984 | bytes 13176832 | tf_op jit(solution)/shard_map/mid_tile/pallas_call | solution.py:72
  55.0 1.2 %collective-permute-done.11 = bf16[128,1920]{1,0:T(8,128)(2,1)S(1)} collective-permute-done((bf16[128,1920]{1,0:T(8,128)(2,1)S(1)}, bf16[128,1920]{1,0:T(8,128)(2,1)S(1)}, u32[]{:S(2)}, u32[]{:S(2)}) %collective-permute-start.11) | collective-permute-done | bytes 491552 | tf_op jit(solution)/shard_map/ppermute | solution.py:31
  56.3 0.3 collective-permute-start.16
  56.6 3.4 %last_coef.1 = (bf16[1536,256]{1,0:T(8,128)(2,1)S(1)}, bf16[1024,256]{1,0:T(8,128)(2,1)S(1)}, f32[8,128]{1,0:T(8,128)S(1)}) custom-call(bf16[128,1920]{1,0:T(8,128)(2,1)S(1)} %get-tuple-element.67.refs_0_, bf16[128,1920]{1,0:T(8,128)(2,1)S(1)} %collective-permute-done.refs_1_, bf16[128,1920]{1,0:T(8,128)(2,1)S(1)} %collective-permute-done.1.refs_2_, ...), custom_call_target="tpu_custom_call" | custom-call | flops 2516582400 | bytes 10817536 | tf_op jit(solution)/shard_map/last_coef/pallas_call | solution.py:72
  60.0 1.5 %end_coef.1 = (bf16[1024,256]{1,0:T(8,128)(2,1)S(1)}, f32[8,128]{1,0:T(8,128)S(1)}) custom-call(bf16[128,1920]{1,0:T(8,128)(2,1)S(1)} %get-tuple-element.67.refs_0_, bf16[128,1920]{1,0:T(8,128)(2,1)S(1)} %collective-permute-done.refs_1_, bf16[128,1920]{1,0:T(8,128)(2,1)S(1)} %collective-permute-done.1.refs_2_, ...), custom_call_target="tpu_custom_call" | custom-call | flops 1006632960 | bytes 4919296 | tf_op jit(solution)/shard_map/end_coef/pallas_call | solution.py:72
  61.6 0.6 collective-permute-start.17
  62.1 0.9 other_grad.1
  63.0 0.3 collective-permute-start.18
  63.3 0.9 text_grad.1.own
  64.2 0.2 collective-permute-start.21
  64.4 1.7 %collective-permute-start.20 = (f32[8,128]{1,0:T(8,128)S(1)}, f32[8,128]{1,0:T(8,128)S(1)}, u32[]{:S(2)}, u32[]{:S(2)}) collective-permute-start(f32[8,128]{1,0:T(8,128)S(1)} %add.12), channel_id=1, source_target_pairs={{0,6},{1,7},{2,0},{3,1},{4,2},{5,3},{6,4},{7,5},{8,14},{9,15},{10,... | collective-permute-start | bytes 12296 | tf_op jit(solution)/shard_map/ppermute | solution.py:31
  66.1 0.4 collective-permute-start.19
  66.4 1.7 %image_grad.1 = (f32[256,768]{1,0:T(8,128)S(1)}, bf16[256,768]{1,0:T(8,128)(2,1)S(1)}, bf16[256,768]{1,0:T(8,128)(2,1)S(1)}, f32[128,768]{1,0:T(8,128)S(1)}, bf16[128,768]{1,0:T(8,128)(2,1)S(1)}) custom-call(bf16[512,1920]{1,0:T(8,128)(2,1)S(1)} %constant_dynamic-update-slice_fusion.refs_3_.refs_6_.refs_8_.refs_0_, ...), custom_call_target="tpu_custom_call" | custom-call | flops 1409286144 | bytes 12058624 | tf_op jit(solution)/shard_map/image_grad/pallas_call | solution.py:72
  68.1 1.3 %collective-permute-done.21 = f32[8,128]{1,0:T(8,128)S(1)} collective-permute-done((f32[8,128]{1,0:T(8,128)S(1)}, f32[8,128]{1,0:T(8,128)S(1)}, u32[]{:S(2)}, u32[]{:S(2)}) %collective-permute-start.21) | collective-permute-done | bytes 4128 | tf_op jit(solution)/shard_map/ppermute | solution.py:31
  69.4 1.4 %collective-permute-done.19 = f32[8,128]{1,0:T(8,128)S(1)} collective-permute-done((f32[8,128]{1,0:T(8,128)S(1)}, f32[8,128]{1,0:T(8,128)S(1)}, u32[]{:S(2)}, u32[]{:S(2)}) %collective-permute-start.19) | collective-permute-done | bytes 4128 | tf_op jit(solution)/shard_map/ppermute | solution.py:31
  70.9 0.5 text_sum.1
  71.4 1.1 %collective-permute-start.22 = (bf16[272,768]{1,0:T(8,128)(2,1)S(1)}, bf16[272,768]{1,0:T(8,128)(2,1)S(1)}, u32[]{:S(2)}, u32[]{:S(2)}) collective-permute-start(bf16[272,768]{1,0:T(8,128)(2,1)S(1)} %get-tuple-element.103), channel_id=1, source_target_pairs={{0,48},{1,49},{2,50},{3,51},{4,52},{5,53},{6,54},{7,55},{8,56},{9,... | collective-permute-start | bytes 1253384 | tf_op jit(solution)/shard_map/ppermute | solution.py:31
  72.5 1.0 %collective-permute-start.23 = (bf16[272,768]{1,0:T(8,128)(2,1)S(1)}, bf16[272,768]{1,0:T(8,128)(2,1)S(1)}, u32[]{:S(2)}, u32[]{:S(2)}) collective-permute-start(bf16[272,768]{1,0:T(8,128)(2,1)S(1)} %get-tuple-element.104), channel_id=1, source_target_pairs={{0,16},{1,17},{2,18},{3,19},{4,20},{5,21},{6,22},{7,23},{8,24},{9,... | collective-permute-start | bytes 1253384 | tf_op jit(solution)/shard_map/ppermute | solution.py:31
  73.5 1.1 %collective-permute-start.26 = (bf16[256,768]{1,0:T(8,128)(2,1)S(1)}, bf16[256,768]{1,0:T(8,128)(2,1)S(1)}, u32[]{:S(2)}, u32[]{:S(2)}) collective-permute-start(bf16[256,768]{1,0:T(8,128)(2,1)S(1)} %get-tuple-element.108), channel_id=1, source_target_pairs={{0,6},{1,7},{2,0},{3,1},{4,2},{5,3},{6,4},{7,5},{8,14},{9,15},{10,... | collective-permute-start | bytes 1179656 | tf_op jit(solution)/shard_map/ppermute | solution.py:31
  74.6 0.9 collective-permute-start.27
  75.5 0.6 collective-permute-start.28
  76.1 5.1 %collective-permute-done.28.from_z = bf16[128,768]{1,0:T(8,128)(2,1)S(1)} collective-permute-done((bf16[128,768]{1,0:T(8,128)(2,1)S(1)}, bf16[128,768]{1,0:T(8,128)(2,1)S(1)}, u32[]{:S(2)}, u32[]{:S(2)}) %collective-permute-start.28) | collective-permute-done | bytes 196640 | tf_op jit(solution)/shard_map/ppermute | solution.py:31
  81.2 1.7 %collective-permute-start.24 = (bf16[128,768]{1,0:T(8,128)(2,1)S(1)}, bf16[128,768]{1,0:T(8,128)(2,1)S(1)}, u32[]{:S(2)}, u32[]{:S(2)}) collective-permute-start(bf16[128,768]{1,0:T(8,128)(2,1)S(1)} %get-tuple-element.106), channel_id=1, source_target_pairs={{0,65},{1,64},{2,67},{3,66},{4,69},{5,68},{6,71},{7,70},{8,73},{9,... | collective-permute-start | bytes 589832 | tf_op jit(solution)/shard_map/ppermute | solution.py:31
  82.9 1.7 %collective-permute-start.25 = (f32[8,128]{1,0:T(8,128)S(1)}, f32[8,128]{1,0:T(8,128)S(1)}, u32[]{:S(2)}, u32[]{:S(2)}) collective-permute-start(f32[8,128]{1,0:T(8,128)S(1)} %add_add_fusion.loss), channel_id=1, source_target_pairs={{0,32},{1,33},{2,34},{3,35},{4,36},{5,37},{6,38},{7,39},{8,40},{9,... | collective-permute-start | bytes 12296 | tf_op jit(solution)/shard_map/ppermute | solution.py:31
  84.6 0.3 collective-permute-done.27.two
  84.9 0.1 image_ring.1
  85.1 3.0 %collective-permute-done.25.loss_far = f32[8,128]{1,0:T(8,128)S(1)} collective-permute-done((f32[8,128]{1,0:T(8,128)S(1)}, f32[8,128]{1,0:T(8,128)S(1)}, u32[]{:S(2)}, u32[]{:S(2)}) %collective-permute-start.25) | collective-permute-done | bytes 4128 | tf_op jit(solution)/shard_map/ppermute | solution.py:31
  88.0 0.0 collective-permute-done.24.from_z
  88.1 0.3 text_ring.1
  88.3 1.8 %collective-permute-start.30 = (bf16[144,768]{1,0:T(8,128)(2,1)S(1)}, bf16[144,768]{1,0:T(8,128)(2,1)S(1)}, u32[]{:S(2)}, u32[]{:S(2)}) collective-permute-start(bf16[144,768]{1,0:T(8,128)(2,1)S(1)} %get-tuple-element.115), channel_id=1, source_target_pairs={{0,65},{1,64},{2,67},{3,66},{4,69},{5,68},{6,71},{7,70},{8,73},{9,... | collective-permute-start | bytes 663560 | tf_op jit(solution)/shard_map/ppermute | solution.py:31
  90.2 0.3 collective-permute-start.32
  90.5 0.9 collective-permute-start.33
  91.4 1.7 %collective-permute-start.31 = (bf16[128,768]{1,0:T(8,128)(2,1)S(1)}, bf16[128,768]{1,0:T(8,128)(2,1)S(1)}, u32[]{:S(2)}, u32[]{:S(2)}) collective-permute-start(bf16[128,768]{1,0:T(8,128)(2,1)S(1)} %get-tuple-element.116), channel_id=1, source_target_pairs={{0,32},{1,33},{2,34},{3,35},{4,36},{5,37},{6,38},{7,39},{8,40},{9,... | collective-permute-start | bytes 589832 | tf_op jit(solution)/shard_map/ppermute | solution.py:31
  93.1 3.0 %collective-permute-start.29 = (f32[8,128]{1,0:T(8,128)S(1)}, f32[8,128]{1,0:T(8,128)S(1)}, u32[]{:S(2)}, u32[]{:S(2)}) collective-permute-start(f32[8,128]{1,0:T(8,128)S(1)} %get-tuple-element.113.loss), channel_id=1, source_target_pairs={{0,64},{1,65},{2,66},{3,67},{4,68},{5,69},{6,70},{7,71},{8,72},{9,... | collective-permute-start | bytes 12296 | tf_op jit(solution)/shard_map/ppermute | solution.py:31
  96.0 1.6 %collective-permute-done.33.img_x = bf16[128,768]{1,0:T(8,128)(2,1)S(1)} collective-permute-done((bf16[128,768]{1,0:T(8,128)(2,1)S(1)}, bf16[128,768]{1,0:T(8,128)(2,1)S(1)}, u32[]{:S(2)}, u32[]{:S(2)}) %collective-permute-start.33) | collective-permute-done | bytes 196640 | tf_op jit(solution)/shard_map/ppermute | solution.py:31
  97.7 0.5 collective-permute-done.29.loss_far
  98.2 0.4 collective-permute-done.31.txt_x
  98.6 1.3 %finish.1 = (f32[128,768]{1,0:T(8,128)}, f32[128,768]{1,0:T(8,128)}, f32[1,1]{1,0:T(1,128)}) custom-call(f32[8,128]{1,0:T(8,128)S(1)} %get-tuple-element.113.loss, f32[8,128]{1,0:T(8,128)S(1)} %collective-permute-done.29.loss_far, f32[128,768]{1,0:T(8,128)S(1)} %get-tuple-element.114.txt, bf16[144,768]{1,0:T(8,128)(2,1)S(1)} %collective-permute-done.30.txt_z, ...), custom_call_target="tpu_custom_call" | custom-call | bytes 2023424 | tf_op jit(solution)/shard_map/finish/pallas_call | solution.py:72
  (30 shorter events, 0.4 us)
Async XLA Ops:
  2.2 15.4 %collective-permute-start.5 = (bf16[128,1920]{1,0:T(8,128)(2,1)S(1)}, bf16[128,1920]{1,0:T(8,128)(2,1)S(1)}, u32[]{:S(2)}, u32[]{:S(2)}) collective-permute-start(bf16[128,1920]{1,0:T(8,128)(2,1)S(1)} %get-tuple-element.64), channel_id=1, source_target_pairs={{0,65},{1,64},{2,67},{3,66},{4,69},{5,68},{6,71},{7,70},{8,73},{9,... | collective-permute-start | bytes 1474568 | tf_op jit(solution)/shard_map/ppermute | solution.py:31
  6.4 14.0 %collective-permute-start.2 = (bf16[128,1920]{1,0:T(8,128)(2,1)S(1)}, bf16[128,1920]{1,0:T(8,128)(2,1)S(1)}, u32[]{:S(2)}, u32[]{:S(2)}) collective-permute-start(bf16[128,1920]{1,0:T(8,128)(2,1)S(1)} %get-tuple-element.64), channel_id=1, source_target_pairs={{0,16},{1,17},{2,18},{3,19},{4,20},{5,21},{6,22},{7,23},{8,24},{9,... | collective-permute-start | bytes 1474568 | tf_op jit(solution)/shard_map/ppermute | solution.py:31
  8.0 12.7 %collective-permute-start = (bf16[128,1920]{1,0:T(8,128)(2,1)S(1)}, bf16[128,1920]{1,0:T(8,128)(2,1)S(1)}, u32[]{:S(2)}, u32[]{:S(2)}) collective-permute-start(bf16[128,1920]{1,0:T(8,128)(2,1)S(1)} %get-tuple-element.67.refs_0_), channel_id=1, source_target_pairs={{0,1},{1,0},{2,3},{3,2},{4,5},{5,4},{6,7},{7,6},{8,9},{9,8},{10,11... | collective-permute-start | bytes 1474568 | tf_op jit(solution)/shard_map/ppermute | solution.py:31
  8.0 13.6 %collective-permute-start.1 = (bf16[128,1920]{1,0:T(8,128)(2,1)S(1)}, bf16[128,1920]{1,0:T(8,128)(2,1)S(1)}, u32[]{:S(2)}, u32[]{:S(2)}) collective-permute-start(bf16[128,1920]{1,0:T(8,128)(2,1)S(1)} %get-tuple-element.67.refs_0_), channel_id=1, source_target_pairs={{0,2},{1,3},{2,4},{3,5},{4,6},{5,7},{6,0},{7,1},{8,10},{9,11},{10,... | collective-permute-start | bytes 1474568 | tf_op jit(solution)/shard_map/ppermute | solution.py:31
  9.5 15.7 %collective-permute-start.9 = (bf16[128,1920]{1,0:T(8,128)(2,1)S(1)}, bf16[128,1920]{1,0:T(8,128)(2,1)S(1)}, u32[]{:S(2)}, u32[]{:S(2)}) collective-permute-start(bf16[128,1920]{1,0:T(8,128)(2,1)S(1)} %get-tuple-element.64), channel_id=1, source_target_pairs={{0,48},{1,49},{2,50},{3,51},{4,52},{5,53},{6,54},{7,55},{8,56},{9,... | collective-permute-start | bytes 1474568 | tf_op jit(solution)/shard_map/ppermute | solution.py:31
  20.4 13.0 %collective-permute-start.6 = (bf16[128,1920]{1,0:T(8,128)(2,1)S(1)}, bf16[128,1920]{1,0:T(8,128)(2,1)S(1)}, u32[]{:S(2)}, u32[]{:S(2)}) collective-permute-start(bf16[128,1920]{1,0:T(8,128)(2,1)S(1)} %collective-permute-done.2), channel_id=1, source_target_pairs={{0,65},{1,64},{2,67},{3,66},{4,69},{5,68},{6,71},{7,70},{8,73},{9,... | collective-permute-start | bytes 1474568 | tf_op jit(solution)/shard_map/ppermute | solution.py:31
  21.6 15.2 %collective-permute-start.7 = (bf16[128,1920]{1,0:T(8,128)(2,1)S(1)}, bf16[128,1920]{1,0:T(8,128)(2,1)S(1)}, u32[]{:S(2)}, u32[]{:S(2)}) collective-permute-start(bf16[128,1920]{1,0:T(8,128)(2,1)S(1)} %collective-permute-done.1.refs_2_), channel_id=1, source_target_pairs={{0,1},{1,0},{2,3},{3,2},{4,5},{5,4},{6,7},{7,6},{8,9},{9,8},{10,11... | collective-permute-start | bytes 1474568 | tf_op jit(solution)/shard_map/ppermute | solution.py:31
  23.4 12.1 %collective-permute-start.3 = (bf16[128,1920]{1,0:T(8,128)(2,1)S(1)}, bf16[128,1920]{1,0:T(8,128)(2,1)S(1)}, u32[]{:S(2)}, u32[]{:S(2)}) collective-permute-start(bf16[128,1920]{1,0:T(8,128)(2,1)S(1)} %collective-permute-done.2), channel_id=1, source_target_pairs={{0,16},{1,17},{2,18},{3,19},{4,20},{5,21},{6,22},{7,23},{8,24},{9,... | collective-permute-start | bytes 1474568 | tf_op jit(solution)/shard_map/ppermute | solution.py:31
  24.9 11.8 %collective-permute-start.4 = (bf16[128,1920]{1,0:T(8,128)(2,1)S(1)}, bf16[128,1920]{1,0:T(8,128)(2,1)S(1)}, u32[]{:S(2)}, u32[]{:S(2)}) collective-permute-start(bf16[128,1920]{1,0:T(8,128)(2,1)S(1)} %collective-permute-done.1.refs_2_), channel_id=1, source_target_pairs={{0,2},{1,3},{2,4},{3,5},{4,6},{5,7},{6,0},{7,1},{8,10},{9,11},{10,... | collective-permute-start | bytes 1474568 | tf_op jit(solution)/shard_map/ppermute | solution.py:31
  25.2 11.6 %collective-permute-start.8 = (bf16[128,1920]{1,0:T(8,128)(2,1)S(1)}, bf16[128,1920]{1,0:T(8,128)(2,1)S(1)}, u32[]{:S(2)}, u32[]{:S(2)}) collective-permute-start(bf16[128,1920]{1,0:T(8,128)(2,1)S(1)} %get-tuple-element.67.refs_0_), channel_id=1, source_target_pairs={{0,6},{1,7},{2,0},{3,1},{4,2},{5,3},{6,4},{7,5},{8,14},{9,15},{10,... | collective-permute-start | bytes 1474568 | tf_op jit(solution)/shard_map/ppermute | solution.py:31
  36.9 6.4 %collective-permute-start.14 = (bf16[512,1920]{1,0:T(8,128)(2,1)S(1)}, bf16[512,1920]{1,0:T(8,128)(2,1)S(1)}, u32[]{:S(2)}, u32[]{:S(2)}) collective-permute-start(bf16[512,1920]{1,0:T(8,128)(2,1)S(1)} %constant_dynamic-update-slice_fusion.refs_3_.refs_6_.refs_8_.refs_0_), channel_id=1, source_target_pairs={{0,8},{1,9},{2,10},{3,11},{4,12},{5,13},{6,14},{7,15},{8,0},{9,1},... | collective-permute-start | bytes 5898248 | tf_op jit(solution)/shard_map/ppermute | solution.py:31
  37.1 10.7 %collective-permute-start.15 = (bf16[256,1920]{1,0:T(8,128)(2,1)S(1)}, bf16[256,1920]{1,0:T(8,128)(2,1)S(1)}, u32[]{:S(2)}, u32[]{:S(2)}) collective-permute-start(bf16[256,1920]{1,0:T(8,128)(2,1)S(1)} %constant_dynamic-update-slice_fusion.4.refs_8_.refs_9_.refs_1_), channel_id=1, source_target_pairs={{0,8},{1,9},{2,10},{3,11},{4,12},{5,13},{6,14},{7,15},{8,0},{9,1},... | collective-permute-start | bytes 2949128 | tf_op jit(solution)/shard_map/ppermute | solution.py:31
  37.7 17.3 %collective-permute-start.10 = (bf16[128,1920]{1,0:T(8,128)(2,1)S(1)}, bf16[128,1920]{1,0:T(8,128)(2,1)S(1)}, u32[]{:S(2)}, u32[]{:S(2)}) collective-permute-start(bf16[128,1920]{1,0:T(8,128)(2,1)S(1)} %collective-permute-done.5), channel_id=1, source_target_pairs={{0,48},{1,49},{2,50},{3,51},{4,52},{5,53},{6,54},{7,55},{8,56},{9,... | collective-permute-start | bytes 1474568 | tf_op jit(solution)/shard_map/ppermute | solution.py:31
  39.4 16.8 %collective-permute-start.13 = (bf16[128,1920]{1,0:T(8,128)(2,1)S(1)}, bf16[128,1920]{1,0:T(8,128)(2,1)S(1)}, u32[]{:S(2)}, u32[]{:S(2)}) collective-permute-start(bf16[128,1920]{1,0:T(8,128)(2,1)S(1)} %collective-permute-done.refs_1_), channel_id=1, source_target_pairs={{0,6},{1,7},{2,0},{3,1},{4,2},{5,3},{6,4},{7,5},{8,14},{9,15},{10,... | collective-permute-start | bytes 1474568 | tf_op jit(solution)/shard_map/ppermute | solution.py:31
  42.3 13.9 %collective-permute-start.11 = (bf16[128,1920]{1,0:T(8,128)(2,1)S(1)}, bf16[128,1920]{1,0:T(8,128)(2,1)S(1)}, u32[]{:S(2)}, u32[]{:S(2)}) collective-permute-start(bf16[128,1920]{1,0:T(8,128)(2,1)S(1)} %collective-permute-done.3), channel_id=1, source_target_pairs={{0,65},{1,64},{2,67},{3,66},{4,69},{5,68},{6,71},{7,70},{8,73},{9,... | collective-permute-start | bytes 1474568 | tf_op jit(solution)/shard_map/ppermute | solution.py:31
  43.3 12.9 %collective-permute-start.12 = (bf16[128,1920]{1,0:T(8,128)(2,1)S(1)}, bf16[128,1920]{1,0:T(8,128)(2,1)S(1)}, u32[]{:S(2)}, u32[]{:S(2)}) collective-permute-start(bf16[128,1920]{1,0:T(8,128)(2,1)S(1)} %collective-permute-done.4.refs_3_), channel_id=1, source_target_pairs={{0,1},{1,0},{2,3},{3,2},{4,5},{5,4},{6,7},{7,6},{8,9},{9,8},{10,11... | collective-permute-start | bytes 1474568 | tf_op jit(solution)/shard_map/ppermute | solution.py:31
  56.3 3.7 %collective-permute-start.16 = (bf16[256,1920]{1,0:T(8,128)(2,1)S(1)}, bf16[256,1920]{1,0:T(8,128)(2,1)S(1)}, u32[]{:S(2)}, u32[]{:S(2)}) collective-permute-start(bf16[256,1920]{1,0:T(8,128)(2,1)S(1)} %constant_dynamic-update-slice_fusion.6.refs_12_.refs_4_), channel_id=1, source_target_pairs={{0,8},{1,9},{2,10},{3,11},{4,12},{5,13},{6,14},{7,15},{8,0},{9,1},... | collective-permute-start | bytes 2949128 | tf_op jit(solution)/shard_map/ppermute | solution.py:31
  61.6 1.5 %collective-permute-start.17 = (f32[8,128]{1,0:T(8,128)S(1)}, f32[8,128]{1,0:T(8,128)S(1)}, u32[]{:S(2)}, u32[]{:S(2)}) collective-permute-start(f32[8,128]{1,0:T(8,128)S(1)} %get-tuple-element.94), channel_id=1, source_target_pairs={{0,8},{1,9},{2,10},{3,11},{4,12},{5,13},{6,14},{7,15},{8,0},{9,1},... | collective-permute-start | bytes 12296 | tf_op jit(solution)/shard_map/ppermute | solution.py:31
  63.0 7.8 %collective-permute-start.18 = (f32[1024,768]{1,0:T(8,128)S(1)}, f32[1024,768]{1,0:T(8,128)S(1)}, u32[]{:S(2)}, u32[]{:S(2)}) collective-permute-start(f32[1024,768]{1,0:T(8,128)S(1)} %other_grad.1), channel_id=1, source_target_pairs={{0,8},{1,9},{2,10},{3,11},{4,12},{5,13},{6,14},{7,15},{8,0},{9,1},... | collective-permute-start | bytes 9437192 | tf_op jit(solution)/shard_map/ppermute | solution.py:31
  64.2 5.2 %collective-permute-start.21 = (f32[8,128]{1,0:T(8,128)S(1)}, f32[8,128]{1,0:T(8,128)S(1)}, u32[]{:S(2)}, u32[]{:S(2)}) collective-permute-start(f32[8,128]{1,0:T(8,128)S(1)} %add.12), channel_id=1, source_target_pairs={{0,4},{1,5},{2,6},{3,7},{4,0},{5,1},{6,2},{7,3},{8,12},{9,13},{10,... | collective-permute-start | bytes 12296 | tf_op jit(solution)/shard_map/ppermute | solution.py:31
  64.4 5.0 %collective-permute-start.20 = (f32[8,128]{1,0:T(8,128)S(1)}, f32[8,128]{1,0:T(8,128)S(1)}, u32[]{:S(2)}, u32[]{:S(2)}) collective-permute-start(f32[8,128]{1,0:T(8,128)S(1)} %add.12), channel_id=1, source_target_pairs={{0,6},{1,7},{2,0},{3,1},{4,2},{5,3},{6,4},{7,5},{8,14},{9,15},{10,... | collective-permute-start | bytes 12296 | tf_op jit(solution)/shard_map/ppermute | solution.py:31
  66.1 4.8 %collective-permute-start.19 = (f32[8,128]{1,0:T(8,128)S(1)}, f32[8,128]{1,0:T(8,128)S(1)}, u32[]{:S(2)}, u32[]{:S(2)}) collective-permute-start(f32[8,128]{1,0:T(8,128)S(1)} %add.12), channel_id=1, source_target_pairs={{0,2},{1,3},{2,4},{3,5},{4,6},{5,7},{6,0},{7,1},{8,10},{9,11},{10,... | collective-permute-start | bytes 12296 | tf_op jit(solution)/shard_map/ppermute | solution.py:31
  71.4 16.7 %collective-permute-start.22 = (bf16[272,768]{1,0:T(8,128)(2,1)S(1)}, bf16[272,768]{1,0:T(8,128)(2,1)S(1)}, u32[]{:S(2)}, u32[]{:S(2)}) collective-permute-start(bf16[272,768]{1,0:T(8,128)(2,1)S(1)} %get-tuple-element.103), channel_id=1, source_target_pairs={{0,48},{1,49},{2,50},{3,51},{4,52},{5,53},{6,54},{7,55},{8,56},{9,... | collective-permute-start | bytes 1253384 | tf_op jit(solution)/shard_map/ppermute | solution.py:31
  72.5 15.6 %collective-permute-start.23 = (bf16[272,768]{1,0:T(8,128)(2,1)S(1)}, bf16[272,768]{1,0:T(8,128)(2,1)S(1)}, u32[]{:S(2)}, u32[]{:S(2)}) collective-permute-start(bf16[272,768]{1,0:T(8,128)(2,1)S(1)} %get-tuple-element.104), channel_id=1, source_target_pairs={{0,16},{1,17},{2,18},{3,19},{4,20},{5,21},{6,22},{7,23},{8,24},{9,... | collective-permute-start | bytes 1253384 | tf_op jit(solution)/shard_map/ppermute | solution.py:31
  73.5 9.4 %collective-permute-start.26 = (bf16[256,768]{1,0:T(8,128)(2,1)S(1)}, bf16[256,768]{1,0:T(8,128)(2,1)S(1)}, u32[]{:S(2)}, u32[]{:S(2)}) collective-permute-start(bf16[256,768]{1,0:T(8,128)(2,1)S(1)} %get-tuple-element.108), channel_id=1, source_target_pairs={{0,6},{1,7},{2,0},{3,1},{4,2},{5,3},{6,4},{7,5},{8,14},{9,15},{10,... | collective-permute-start | bytes 1179656 | tf_op jit(solution)/shard_map/ppermute | solution.py:31
  74.6 10.3 %collective-permute-start.27 = (bf16[256,768]{1,0:T(8,128)(2,1)S(1)}, bf16[256,768]{1,0:T(8,128)(2,1)S(1)}, u32[]{:S(2)}, u32[]{:S(2)}) collective-permute-start(bf16[256,768]{1,0:T(8,128)(2,1)S(1)} %get-tuple-element.109), channel_id=1, source_target_pairs={{0,2},{1,3},{2,4},{3,5},{4,6},{5,7},{6,0},{7,1},{8,10},{9,11},{10,... | collective-permute-start | bytes 1179656 | tf_op jit(solution)/shard_map/ppermute | solution.py:31
  75.5 5.7 %collective-permute-start.28 = (bf16[128,768]{1,0:T(8,128)(2,1)S(1)}, bf16[128,768]{1,0:T(8,128)(2,1)S(1)}, u32[]{:S(2)}, u32[]{:S(2)}) collective-permute-start(bf16[128,768]{1,0:T(8,128)(2,1)S(1)} %get-tuple-element.111), channel_id=1, source_target_pairs={{0,1},{1,0},{2,3},{3,2},{4,5},{5,4},{6,7},{7,6},{8,9},{9,8},{10,11... | collective-permute-start | bytes 589832 | tf_op jit(solution)/shard_map/ppermute | solution.py:31
  81.2 6.9 %collective-permute-start.24 = (bf16[128,768]{1,0:T(8,128)(2,1)S(1)}, bf16[128,768]{1,0:T(8,128)(2,1)S(1)}, u32[]{:S(2)}, u32[]{:S(2)}) collective-permute-start(bf16[128,768]{1,0:T(8,128)(2,1)S(1)} %get-tuple-element.106), channel_id=1, source_target_pairs={{0,65},{1,64},{2,67},{3,66},{4,69},{5,68},{6,71},{7,70},{8,73},{9,... | collective-permute-start | bytes 589832 | tf_op jit(solution)/shard_map/ppermute | solution.py:31
  82.9 5.1 %collective-permute-start.25 = (f32[8,128]{1,0:T(8,128)S(1)}, f32[8,128]{1,0:T(8,128)S(1)}, u32[]{:S(2)}, u32[]{:S(2)}) collective-permute-start(f32[8,128]{1,0:T(8,128)S(1)} %add_add_fusion.loss), channel_id=1, source_target_pairs={{0,32},{1,33},{2,34},{3,35},{4,36},{5,37},{6,38},{7,39},{8,40},{9,... | collective-permute-start | bytes 12296 | tf_op jit(solution)/shard_map/ppermute | solution.py:31
  84.9 13.6 %copy-start = (bf16[128,768]{1,0:T(8,128)(2,1)S(1)}, bf16[128,768]{1,0:T(8,128)(2,1)}, u32[]{:S(2)}) copy-start(bf16[128,768]{1,0:T(8,128)(2,1)} %si.3) | copy-start | bytes 589828
  84.9 13.7 %copy-start.1 = (bf16[128,768]{1,0:T(8,128)(2,1)S(1)}, bf16[128,768]{1,0:T(8,128)(2,1)}, u32[]{:S(2)}) copy-start(bf16[128,768]{1,0:T(8,128)(2,1)} %st.3) | copy-start | bytes 589828
  88.3 10.2 %collective-permute-start.30 = (bf16[144,768]{1,0:T(8,128)(2,1)S(1)}, bf16[144,768]{1,0:T(8,128)(2,1)S(1)}, u32[]{:S(2)}, u32[]{:S(2)}) collective-permute-start(bf16[144,768]{1,0:T(8,128)(2,1)S(1)} %get-tuple-element.115), channel_id=1, source_target_pairs={{0,65},{1,64},{2,67},{3,66},{4,69},{5,68},{6,71},{7,70},{8,73},{9,... | collective-permute-start | bytes 663560 | tf_op jit(solution)/shard_map/ppermute | solution.py:31
  90.2 8.4 %collective-permute-start.32 = (bf16[144,768]{1,0:T(8,128)(2,1)S(1)}, bf16[144,768]{1,0:T(8,128)(2,1)S(1)}, u32[]{:S(2)}, u32[]{:S(2)}) collective-permute-start(bf16[144,768]{1,0:T(8,128)(2,1)S(1)} %get-tuple-element.118), channel_id=1, source_target_pairs={{0,1},{1,0},{2,3},{3,2},{4,5},{5,4},{6,7},{7,6},{8,9},{9,8},{10,11... | collective-permute-start | bytes 663560 | tf_op jit(solution)/shard_map/ppermute | solution.py:31
  90.5 7.2 %collective-permute-start.33 = (bf16[128,768]{1,0:T(8,128)(2,1)S(1)}, bf16[128,768]{1,0:T(8,128)(2,1)S(1)}, u32[]{:S(2)}, u32[]{:S(2)}) collective-permute-start(bf16[128,768]{1,0:T(8,128)(2,1)S(1)} %get-tuple-element.119), channel_id=1, source_target_pairs={{0,4},{1,5},{2,6},{3,7},{4,0},{5,1},{6,2},{7,3},{8,12},{9,13},{10,... | collective-permute-start | bytes 589832 | tf_op jit(solution)/shard_map/ppermute | solution.py:31
  91.4 7.2 %collective-permute-start.31 = (bf16[128,768]{1,0:T(8,128)(2,1)S(1)}, bf16[128,768]{1,0:T(8,128)(2,1)S(1)}, u32[]{:S(2)}, u32[]{:S(2)}) collective-permute-start(bf16[128,768]{1,0:T(8,128)(2,1)S(1)} %get-tuple-element.116), channel_id=1, source_target_pairs={{0,32},{1,33},{2,34},{3,35},{4,36},{5,37},{6,38},{7,39},{8,40},{9,... | collective-permute-start | bytes 589832 | tf_op jit(solution)/shard_map/ppermute | solution.py:31
  93.1 5.1 %collective-permute-start.29 = (f32[8,128]{1,0:T(8,128)S(1)}, f32[8,128]{1,0:T(8,128)S(1)}, u32[]{:S(2)}, u32[]{:S(2)}) collective-permute-start(f32[8,128]{1,0:T(8,128)S(1)} %get-tuple-element.113.loss), channel_id=1, source_target_pairs={{0,64},{1,65},{2,66},{3,67},{4,68},{5,69},{6,70},{7,71},{8,72},{9,... | collective-permute-start | bytes 12296 | tf_op jit(solution)/shard_map/ppermute | solution.py:31

commit v5 on v3

--- a/solution.py
+++ b/solution.py
@@ -149,29 +149,28 @@
         ref[half:, :] = dot(coef_i[:, n * add:(n + 1) * add], img_s, TN)
 
 
+def coef_blocks(width_t, rows, cols, out, size):
+    cols_t, cols_s = slice(0, width_t), slice(width_t, None)
+    right_t, right_s = stack(cols, cols_t), stack(cols, cols_s)
+    left_t, left_s = stack(rows, cols_t), stack(rows, cols_s)
+    total = jnp.zeros((8, 128), f32)
+    for at in range(0, left_t.shape[0], size):
+        part = slice(at, at + size)
+        coef, loss = tile_terms(dot(left_t[part], right_t, NT), dot(left_s[part], right_s, NT))
+        out[part, :] = coef
+        total = total + loss
+    return total
+
+
 def last_coef_kernel(width_t, *refs):
     imgs, texts, last, (p_loss, coef_p, coef_t, loss_ref) = refs[:8], refs[8:12], refs[12], refs[13:]
-    cols_t, cols_s = slice(0, width_t), slice(width_t, None)
-    late = imgs[6:]
-    part, loss_p = tile_terms(
-        dot(stack(texts, cols_t), stack(late, cols_t), NT), dot(stack(texts, cols_s), stack(late, cols_s), NT)
-    )
-    coef_p[...] = part
-    part, loss_t = tile_terms(
-        dot(stack(imgs, cols_t), last[:, cols_t], NT), dot(stack(imgs, cols_s), last[:, cols_s], NT)
-    )
-    coef_t[...] = part
-    loss_ref[...] = p_loss[...] + loss_p + loss_t
+    loss = coef_blocks(width_t, texts, imgs[6:], coef_p, 256) + coef_blocks(width_t, imgs, [last], coef_t, 256)
+    loss_ref[...] = p_loss[...] + loss
 
 
 def end_coef_kernel(width_t, *refs):
     imgs, (last, p_loss, coef_u, loss_ref) = refs[:8], refs[8:]
-    cols_t, cols_s = slice(0, width_t), slice(width_t, None)
-    part, loss = tile_terms(
-        dot(stack(imgs, cols_t), last[:, cols_t], NT), dot(stack(imgs, cols_s), last[:, cols_s], NT)
-    )
-    coef_u[...] = part
-    loss_ref[...] = p_loss[...] + loss
+    loss_ref[...] = p_loss[...] + coef_blocks(width_t, imgs, [last], coef_u, 256)
 
 
 def text_grad_kernel(width_t, core, *refs):
@@ -321,7 +320,7 @@
     )[0]
     grad_o, loss_core = hold((grad_o, loss_core))
     from_core = to_core(grad_o)
-    loss = loss + loss_core
+    loss, p_txt, p_img = hold((loss + loss_core, p_txt, p_img))
     loss_x = [to_x(loss, 1), to_x(loss, -1), to_x(loss, 2)]
     pair = 2 * rows
     sums = [((rows, width_s), f32), ((rows, width_s), bf16)]

time: 101 us -> 100 us (0.990)
  no operation moved by 1% of the time
where the time goes in v5:
time: 100 us; the launch traced here: 99.4 us
  starting transfers between devices  43.2 us (43%)
  waiting for transfers between devices  32.7 us (33%)
  Pallas kernels  22.4 us (22%)
    ppermute x34, starting transfers between devices, permute(): return lax.ppermute(value, AXES, pairs)  43.2 us
    ppermute x34, waiting for transfers between devices, permute(): return lax.ppermute(value, AXES, pairs)  32.7 us
    pallas_call x12, Pallas kernels, call(): pl.pallas_call(kernel, out_shape=tuple((shape_of(shape, dtype) for shape,...  22.4 us
  transfers between devices with their start and end apart: 34, of which 15 were waited for; matrix products, arithmetic and copies ran while one was open for 0% of the time, Pallas kernels for 18%

profile of v5, /device:TPU:0, one launch (start us, length us, event | category | flops | bytes accessed | tf_op | source)
XLA Modules:
  0.0 99.4 jit_solution(8271550833772300749)
XLA Ops:
  0.6 1.6 %units.1 = (bf16[128,1920]{1,0:T(8,128)(2,1)S(1)}, bf16[128,1920]{1,0:T(8,128)(2,1)S(1)}) custom-call(bf16[128,1152]{1,0:T(8,128)(2,1)} %ti.1, bf16[128,768]{1,0:T(8,128)(2,1)} %si.3, bf16[128,1152]{1,0:T(8,128)(2,1)} %tt.1, bf16[128,768]{1,0:T(8,128)(2,1)} %st.3), custom_call_target="tpu_custom_call" | custom-call | bytes 983040 | tf_op jit(solution)/shard_map/units/pallas_call | solution.py:72
  2.2 4.2 %collective-permute-start.5 = (bf16[128,1920]{1,0:T(8,128)(2,1)S(1)}, bf16[128,1920]{1,0:T(8,128)(2,1)S(1)}, u32[]{:S(2)}, u32[]{:S(2)}) collective-permute-start(bf16[128,1920]{1,0:T(8,128)(2,1)S(1)} %get-tuple-element.67), channel_id=1, source_target_pairs={{0,65},{1,64},{2,67},{3,66},{4,69},{5,68},{6,71},{7,70},{8,73},{9,... | collective-permute-start | bytes 1474568 | tf_op jit(solution)/shard_map/ppermute | solution.py:31
  6.4 1.6 %collective-permute-start.2 = (bf16[128,1920]{1,0:T(8,128)(2,1)S(1)}, bf16[128,1920]{1,0:T(8,128)(2,1)S(1)}, u32[]{:S(2)}, u32[]{:S(2)}) collective-permute-start(bf16[128,1920]{1,0:T(8,128)(2,1)S(1)} %get-tuple-element.67), channel_id=1, source_target_pairs={{0,16},{1,17},{2,18},{3,19},{4,20},{5,21},{6,22},{7,23},{8,24},{9,... | collective-permute-start | bytes 1474568 | tf_op jit(solution)/shard_map/ppermute | solution.py:31
  8.0 1.5 %collective-permute-start.1 = (bf16[128,1920]{1,0:T(8,128)(2,1)S(1)}, bf16[128,1920]{1,0:T(8,128)(2,1)S(1)}, u32[]{:S(2)}, u32[]{:S(2)}) collective-permute-start(bf16[128,1920]{1,0:T(8,128)(2,1)S(1)} %get-tuple-element.70.refs_0_), channel_id=1, source_target_pairs={{0,2},{1,3},{2,4},{3,5},{4,6},{5,7},{6,0},{7,1},{8,10},{9,11},{10,... | collective-permute-start | bytes 1474568 | tf_op jit(solution)/shard_map/ppermute | solution.py:31
  9.5 1.7 %collective-permute-start.9 = (bf16[128,1920]{1,0:T(8,128)(2,1)S(1)}, bf16[128,1920]{1,0:T(8,128)(2,1)S(1)}, u32[]{:S(2)}, u32[]{:S(2)}) collective-permute-start(bf16[128,1920]{1,0:T(8,128)(2,1)S(1)} %get-tuple-element.67), channel_id=1, source_target_pairs={{0,48},{1,49},{2,50},{3,51},{4,52},{5,53},{6,54},{7,55},{8,56},{9,... | collective-permute-start | bytes 1474568 | tf_op jit(solution)/shard_map/ppermute | solution.py:31
  11.2 6.5 %collective-permute-done.5 = bf16[128,1920]{1,0:T(8,128)(2,1)S(1)} collective-permute-done((bf16[128,1920]{1,0:T(8,128)(2,1)S(1)}, bf16[128,1920]{1,0:T(8,128)(2,1)S(1)}, u32[]{:S(2)}, u32[]{:S(2)}) %collective-permute-start.5) | collective-permute-done | bytes 491552 | tf_op jit(solution)/shard_map/ppermute | solution.py:31
  17.6 2.7 %collective-permute-done.2 = bf16[128,1920]{1,0:T(8,128)(2,1)S(1)} collective-permute-done((bf16[128,1920]{1,0:T(8,128)(2,1)S(1)}, bf16[128,1920]{1,0:T(8,128)(2,1)S(1)}, u32[]{:S(2)}, u32[]{:S(2)}) %collective-permute-start.2) | collective-permute-done | bytes 491552 | tf_op jit(solution)/shard_map/ppermute | solution.py:31
  20.4 0.4 collective-permute-start.6
  20.7 0.9 collective-permute-done.1.refs_2_
  21.6 1.7 %collective-permute-start.7 = (bf16[128,1920]{1,0:T(8,128)(2,1)S(1)}, bf16[128,1920]{1,0:T(8,128)(2,1)S(1)}, u32[]{:S(2)}, u32[]{:S(2)}) collective-permute-start(bf16[128,1920]{1,0:T(8,128)(2,1)S(1)} %collective-permute-done.1.refs_2_), channel_id=1, source_target_pairs={{0,1},{1,0},{2,3},{3,2},{4,5},{5,4},{6,7},{7,6},{8,9},{9,8},{10,11... | collective-permute-start | bytes 1474568 | tf_op jit(solution)/shard_map/ppermute | solution.py:31
  23.4 1.6 %collective-permute-start.3 = (bf16[128,1920]{1,0:T(8,128)(2,1)S(1)}, bf16[128,1920]{1,0:T(8,128)(2,1)S(1)}, u32[]{:S(2)}, u32[]{:S(2)}) collective-permute-start(bf16[128,1920]{1,0:T(8,128)(2,1)S(1)} %collective-permute-done.2), channel_id=1, source_target_pairs={{0,16},{1,17},{2,18},{3,19},{4,20},{5,21},{6,22},{7,23},{8,24},{9,... | collective-permute-start | bytes 1474568 | tf_op jit(solution)/shard_map/ppermute | solution.py:31
  24.9 0.3 collective-permute-start.4
  25.2 0.0 collective-permute-done.9
  25.2 3.0 %collective-permute-start.8 = (bf16[128,1920]{1,0:T(8,128)(2,1)S(1)}, bf16[128,1920]{1,0:T(8,128)(2,1)S(1)}, u32[]{:S(2)}, u32[]{:S(2)}) collective-permute-start(bf16[128,1920]{1,0:T(8,128)(2,1)S(1)} %get-tuple-element.70.refs_0_), channel_id=1, source_target_pairs={{0,6},{1,7},{2,0},{3,1},{4,2},{5,3},{6,4},{7,5},{8,14},{9,15},{10,... | collective-permute-start | bytes 1474568 | tf_op jit(solution)/shard_map/ppermute | solution.py:31
  28.2 5.2 %collective-permute-done.6 = bf16[128,1920]{1,0:T(8,128)(2,1)S(1)} collective-permute-done((bf16[128,1920]{1,0:T(8,128)(2,1)S(1)}, bf16[128,1920]{1,0:T(8,128)(2,1)S(1)}, u32[]{:S(2)}, u32[]{:S(2)}) %collective-permute-start.6) | collective-permute-done | bytes 491552 | tf_op jit(solution)/shard_map/ppermute | solution.py:31
  33.4 2.1 %collective-permute-done.3 = bf16[128,1920]{1,0:T(8,128)(2,1)S(1)} collective-permute-done((bf16[128,1920]{1,0:T(8,128)(2,1)S(1)}, bf16[128,1920]{1,0:T(8,128)(2,1)S(1)}, u32[]{:S(2)}, u32[]{:S(2)}) %collective-permute-start.3) | collective-permute-done | bytes 491552 | tf_op jit(solution)/shard_map/ppermute | solution.py:31
  35.5 1.3 %collective-permute-done.4.refs_3_ = bf16[128,1920]{1,0:T(8,128)(2,1)S(1)} collective-permute-done((bf16[128,1920]{1,0:T(8,128)(2,1)S(1)}, bf16[128,1920]{1,0:T(8,128)(2,1)S(1)}, u32[]{:S(2)}, u32[]{:S(2)}) %collective-permute-start.4) | collective-permute-done | bytes 491552 | tf_op jit(solution)/shard_map/ppermute | solution.py:31
  36.9 0.1 collective-permute-start.14
  37.1 0.6 collective-permute-start.15
  37.7 1.7 %collective-permute-start.10 = (bf16[128,1920]{1,0:T(8,128)(2,1)S(1)}, bf16[128,1920]{1,0:T(8,128)(2,1)S(1)}, u32[]{:S(2)}, u32[]{:S(2)}) collective-permute-start(bf16[128,1920]{1,0:T(8,128)(2,1)S(1)} %collective-permute-done.5), channel_id=1, source_target_pairs={{0,48},{1,49},{2,50},{3,51},{4,52},{5,53},{6,54},{7,55},{8,56},{9,... | collective-permute-start | bytes 1474568 | tf_op jit(solution)/shard_map/ppermute | solution.py:31
  39.4 3.0 %collective-permute-start.13 = (bf16[128,1920]{1,0:T(8,128)(2,1)S(1)}, bf16[128,1920]{1,0:T(8,128)(2,1)S(1)}, u32[]{:S(2)}, u32[]{:S(2)}) collective-permute-start(bf16[128,1920]{1,0:T(8,128)(2,1)S(1)} %collective-permute-done.refs_1_), channel_id=1, source_target_pairs={{0,6},{1,7},{2,0},{3,1},{4,2},{5,3},{6,4},{7,5},{8,14},{9,15},{10,... | collective-permute-start | bytes 1474568 | tf_op jit(solution)/shard_map/ppermute | solution.py:31
  42.3 1.0 collective-permute-start.11
  43.3 0.0 collective-permute-done.14.refs_4_.refs_7_.refs_10_.refs_2_
  43.3 1.1 %collective-permute-start.12 = (bf16[128,1920]{1,0:T(8,128)(2,1)S(1)}, bf16[128,1920]{1,0:T(8,128)(2,1)S(1)}, u32[]{:S(2)}, u32[]{:S(2)}) collective-permute-start(bf16[128,1920]{1,0:T(8,128)(2,1)S(1)} %collective-permute-done.4.refs_3_), channel_id=1, source_target_pairs={{0,1},{1,0},{2,3},{3,2},{4,5},{5,4},{6,7},{7,6},{8,9},{9,8},{10,11... | collective-permute-start | bytes 1474568 | tf_op jit(solution)/shard_map/ppermute | solution.py:31
  44.4 3.5 %near_tile.1 = (f32[384,768]{1,0:T(8,128)S(1)}, f32[512,768]{1,0:T(8,128)S(1)}, f32[512,768]{1,0:T(8,128)S(1)}, f32[8,128]{1,0:T(8,128)S(1)}) custom-call(bf16[128,1920]{1,0:T(8,128)(2,1)S(1)} %get-tuple-element.70.refs_0_, bf16[128,1920]{1,0:T(8,128)(2,1)S(1)} %collective-permute-done.refs_1_, bf16[128,1920]{1,0:T(8,128)(2,1)S(1)} %collective-permute-done.1.refs_2_, ...), custom_call_target="tpu_custom_call" | custom-call | flops 2717908992 | bytes 5406720 | tf_op jit(solution)/shard_map/near_tile/pallas_call | solution.py:72
  47.8 0.0 collective-permute-done.15.refs_9_.refs_11_.refs_3_
  47.9 7.1 %mid_tile.1 = (f32[768,768]{1,0:T(8,128)S(1)}, f32[768,768]{1,0:T(8,128)S(1)}, f32[768,768]{1,0:T(8,128)S(1)}, f32[8,128]{1,0:T(8,128)S(1)}) custom-call(bf16[128,1920]{1,0:T(8,128)(2,1)S(1)} %get-tuple-element.70.refs_0_, bf16[128,1920]{1,0:T(8,128)(2,1)S(1)} %collective-permute-done.refs_1_, bf16[128,1920]{1,0:T(8,128)(2,1)S(1)} %collective-permute-done.1.refs_2_, ...), custom_call_target="tpu_custom_call" | custom-call | flops 5435817984 | bytes 13176832 | tf_op jit(solution)/shard_map/mid_tile/pallas_call | solution.py:72
  55.0 1.2 %collective-permute-done.11 = bf16[128,1920]{1,0:T(8,128)(2,1)S(1)} collective-permute-done((bf16[128,1920]{1,0:T(8,128)(2,1)S(1)}, bf16[128,1920]{1,0:T(8,128)(2,1)S(1)}, u32[]{:S(2)}, u32[]{:S(2)}) %collective-permute-start.11) | collective-permute-done | bytes 491552 | tf_op jit(solution)/shard_map/ppermute | solution.py:31
  56.3 0.3 collective-permute-start.16
  56.6 3.2 %last_coef.1 = (bf16[1536,256]{1,0:T(8,128)(2,1)S(1)}, bf16[1024,256]{1,0:T(8,128)(2,1)S(1)}, f32[8,128]{1,0:T(8,128)S(1)}) custom-call(bf16[128,1920]{1,0:T(8,128)(2,1)S(1)} %get-tuple-element.70.refs_0_, bf16[128,1920]{1,0:T(8,128)(2,1)S(1)} %collective-permute-done.refs_1_, bf16[128,1920]{1,0:T(8,128)(2,1)S(1)} %collective-permute-done.1.refs_2_, ...), custom_call_target="tpu_custom_call" | custom-call | flops 2516582400 | bytes 10817536 | tf_op jit(solution)/shard_map/last_coef/pallas_call | solution.py:72
  59.8 1.4 %end_coef.1 = (bf16[1024,256]{1,0:T(8,128)(2,1)S(1)}, f32[8,128]{1,0:T(8,128)S(1)}) custom-call(bf16[128,1920]{1,0:T(8,128)(2,1)S(1)} %get-tuple-element.70.refs_0_, bf16[128,1920]{1,0:T(8,128)(2,1)S(1)} %collective-permute-done.refs_1_, bf16[128,1920]{1,0:T(8,128)(2,1)S(1)} %collective-permute-done.1.refs_2_, ...), custom_call_target="tpu_custom_call" | custom-call | flops 1006632960 | bytes 4919296 | tf_op jit(solution)/shard_map/end_coef/pallas_call | solution.py:72
  61.3 0.6 collective-permute-start.17
  61.9 0.9 other_grad.1
  62.8 0.2 collective-permute-start.18
  63.0 0.1 collective-permute-start.21
  63.1 1.7 %collective-permute-start.20 = (f32[8,128]{1,0:T(8,128)S(1)}, f32[8,128]{1,0:T(8,128)S(1)}, u32[]{:S(2)}, u32[]{:S(2)}) collective-permute-start(f32[8,128]{1,0:T(8,128)S(1)} %add.12), channel_id=1, source_target_pairs={{0,6},{1,7},{2,0},{3,1},{4,2},{5,3},{6,4},{7,5},{8,14},{9,15},{10,... | collective-permute-start | bytes 12296 | tf_op jit(solution)/shard_map/ppermute | solution.py:31
  64.8 0.4 collective-permute-start.19
  65.2 1.7 %image_grad.1 = (f32[256,768]{1,0:T(8,128)S(1)}, bf16[256,768]{1,0:T(8,128)(2,1)S(1)}, bf16[256,768]{1,0:T(8,128)(2,1)S(1)}, f32[128,768]{1,0:T(8,128)S(1)}, bf16[128,768]{1,0:T(8,128)(2,1)S(1)}) custom-call(bf16[512,1920]{1,0:T(8,128)(2,1)S(1)} %constant_dynamic-update-slice_fusion.refs_3_.refs_6_.refs_8_.refs_0_, ...), custom_call_target="tpu_custom_call" | custom-call | flops 1409286144 | bytes 12058624 | tf_op jit(solution)/shard_map/image_grad/pallas_call | solution.py:72
  66.9 0.9 text_grad.1.own
  67.8 0.4 collective-permute-done.21
  68.2 1.4 %collective-permute-done.19 = f32[8,128]{1,0:T(8,128)S(1)} collective-permute-done((f32[8,128]{1,0:T(8,128)S(1)}, f32[8,128]{1,0:T(8,128)S(1)}, u32[]{:S(2)}, u32[]{:S(2)}) %collective-permute-start.19) | collective-permute-done | bytes 4128 | tf_op jit(solution)/shard_map/ppermute | solution.py:31
  69.6 0.4 text_sum.1
  70.0 1.0 %collective-permute-start.22 = (bf16[272,768]{1,0:T(8,128)(2,1)S(1)}, bf16[272,768]{1,0:T(8,128)(2,1)S(1)}, u32[]{:S(2)}, u32[]{:S(2)}) collective-permute-start(bf16[272,768]{1,0:T(8,128)(2,1)S(1)} %get-tuple-element.109), channel_id=1, source_target_pairs={{0,48},{1,49},{2,50},{3,51},{4,52},{5,53},{6,54},{7,55},{8,56},{9,... | collective-permute-start | bytes 1253384 | tf_op jit(solution)/shard_map/ppermute | solution.py:31
  71.0 1.1 %collective-permute-start.23 = (bf16[272,768]{1,0:T(8,128)(2,1)S(1)}, bf16[272,768]{1,0:T(8,128)(2,1)S(1)}, u32[]{:S(2)}, u32[]{:S(2)}) collective-permute-start(bf16[272,768]{1,0:T(8,128)(2,1)S(1)} %get-tuple-element.110), channel_id=1, source_target_pairs={{0,16},{1,17},{2,18},{3,19},{4,20},{5,21},{6,22},{7,23},{8,24},{9,... | collective-permute-start | bytes 1253384 | tf_op jit(solution)/shard_map/ppermute | solution.py:31
  72.1 1.1 %collective-permute-start.26 = (bf16[256,768]{1,0:T(8,128)(2,1)S(1)}, bf16[256,768]{1,0:T(8,128)(2,1)S(1)}, u32[]{:S(2)}, u32[]{:S(2)}) collective-permute-start(bf16[256,768]{1,0:T(8,128)(2,1)S(1)} %get-tuple-element.114), channel_id=1, source_target_pairs={{0,6},{1,7},{2,0},{3,1},{4,2},{5,3},{6,4},{7,5},{8,14},{9,15},{10,... | collective-permute-start | bytes 1179656 | tf_op jit(solution)/shard_map/ppermute | solution.py:31
  73.2 0.9 collective-permute-start.27
  74.1 0.6 collective-permute-start.28
  74.7 5.1 %collective-permute-done.28.from_z = bf16[128,768]{1,0:T(8,128)(2,1)S(1)} collective-permute-done((bf16[128,768]{1,0:T(8,128)(2,1)S(1)}, bf16[128,768]{1,0:T(8,128)(2,1)S(1)}, u32[]{:S(2)}, u32[]{:S(2)}) %collective-permute-start.28) | collective-permute-done | bytes 196640 | tf_op jit(solution)/shard_map/ppermute | solution.py:31
  79.8 1.7 %collective-permute-start.24 = (bf16[128,768]{1,0:T(8,128)(2,1)S(1)}, bf16[128,768]{1,0:T(8,128)(2,1)S(1)}, u32[]{:S(2)}, u32[]{:S(2)}) collective-permute-start(bf16[128,768]{1,0:T(8,128)(2,1)S(1)} %get-tuple-element.112), channel_id=1, source_target_pairs={{0,65},{1,64},{2,67},{3,66},{4,69},{5,68},{6,71},{7,70},{8,73},{9,... | collective-permute-start | bytes 589832 | tf_op jit(solution)/shard_map/ppermute | solution.py:31
  81.5 1.7 %collective-permute-start.25 = (f32[8,128]{1,0:T(8,128)S(1)}, f32[8,128]{1,0:T(8,128)S(1)}, u32[]{:S(2)}, u32[]{:S(2)}) collective-permute-start(f32[8,128]{1,0:T(8,128)S(1)} %add_add_fusion.loss), channel_id=1, source_target_pairs={{0,32},{1,33},{2,34},{3,35},{4,36},{5,37},{6,38},{7,39},{8,40},{9,... | collective-permute-start | bytes 12296 | tf_op jit(solution)/shard_map/ppermute | solution.py:31
  83.2 0.9 collective-permute-done.27.two
  84.1 0.1 image_ring.1
  84.2 2.4 %collective-permute-done.25.loss_far = f32[8,128]{1,0:T(8,128)S(1)} collective-permute-done((f32[8,128]{1,0:T(8,128)S(1)}, f32[8,128]{1,0:T(8,128)S(1)}, u32[]{:S(2)}, u32[]{:S(2)}) %collective-permute-start.25) | collective-permute-done | bytes 4128 | tf_op jit(solution)/shard_map/ppermute | solution.py:31
  86.6 0.0 collective-permute-done.24.from_z
  86.7 0.3 text_ring.1
  86.9 1.8 %collective-permute-start.30 = (bf16[144,768]{1,0:T(8,128)(2,1)S(1)}, bf16[144,768]{1,0:T(8,128)(2,1)S(1)}, u32[]{:S(2)}, u32[]{:S(2)}) collective-permute-start(bf16[144,768]{1,0:T(8,128)(2,1)S(1)} %get-tuple-element.121), channel_id=1, source_target_pairs={{0,65},{1,64},{2,67},{3,66},{4,69},{5,68},{6,71},{7,70},{8,73},{9,... | collective-permute-start | bytes 663560 | tf_op jit(solution)/shard_map/ppermute | solution.py:31
  88.8 0.4 collective-permute-start.32
  89.1 1.8 %collective-permute-start.33 = (bf16[128,768]{1,0:T(8,128)(2,1)S(1)}, bf16[128,768]{1,0:T(8,128)(2,1)S(1)}, u32[]{:S(2)}, u32[]{:S(2)}) collective-permute-start(bf16[128,768]{1,0:T(8,128)(2,1)S(1)} %get-tuple-element.125), channel_id=1, source_target_pairs={{0,4},{1,5},{2,6},{3,7},{4,0},{5,1},{6,2},{7,3},{8,12},{9,13},{10,... | collective-permute-start | bytes 589832 | tf_op jit(solution)/shard_map/ppermute | solution.py:31
  91.0 1.7 %collective-permute-start.31 = (bf16[128,768]{1,0:T(8,128)(2,1)S(1)}, bf16[128,768]{1,0:T(8,128)(2,1)S(1)}, u32[]{:S(2)}, u32[]{:S(2)}) collective-permute-start(bf16[128,768]{1,0:T(8,128)(2,1)S(1)} %get-tuple-element.122), channel_id=1, source_target_pairs={{0,32},{1,33},{2,34},{3,35},{4,36},{5,37},{6,38},{7,39},{8,40},{9,... | collective-permute-start | bytes 589832 | tf_op jit(solution)/shard_map/ppermute | solution.py:31
  92.6 3.0 %collective-permute-start.29 = (f32[8,128]{1,0:T(8,128)S(1)}, f32[8,128]{1,0:T(8,128)S(1)}, u32[]{:S(2)}, u32[]{:S(2)}) collective-permute-start(f32[8,128]{1,0:T(8,128)S(1)} %get-tuple-element.119.loss), channel_id=1, source_target_pairs={{0,64},{1,65},{2,66},{3,67},{4,68},{5,69},{6,70},{7,71},{8,72},{9,... | collective-permute-start | bytes 12296 | tf_op jit(solution)/shard_map/ppermute | solution.py:31
  95.6 0.7 collective-permute-done.33.img_x
  96.3 1.5 %collective-permute-done.29.loss_far = f32[8,128]{1,0:T(8,128)S(1)} collective-permute-done((f32[8,128]{1,0:T(8,128)S(1)}, f32[8,128]{1,0:T(8,128)S(1)}, u32[]{:S(2)}, u32[]{:S(2)}) %collective-permute-start.29) | collective-permute-done | bytes 4128 | tf_op jit(solution)/shard_map/ppermute | solution.py:31
  97.8 0.4 collective-permute-done.31.txt_x
  98.1 1.3 %finish.1 = (f32[128,768]{1,0:T(8,128)}, f32[128,768]{1,0:T(8,128)}, f32[1,1]{1,0:T(1,128)}) custom-call(f32[8,128]{1,0:T(8,128)S(1)} %get-tuple-element.119.loss, f32[8,128]{1,0:T(8,128)S(1)} %collective-permute-done.29.loss_far, f32[128,768]{1,0:T(8,128)S(1)} %get-tuple-element.120.txt, bf16[144,768]{1,0:T(8,128)(2,1)S(1)} %collective-permute-done.30.txt_z, ...), custom_call_target="tpu_custom_call" | custom-call | bytes 2023424 | tf_op jit(solution)/shard_map/finish/pallas_call | solution.py:72
  (30 shorter events, 0.4 us)
Async XLA Ops:
  2.2 15.4 %collective-permute-start.5 = (bf16[128,1920]{1,0:T(8,128)(2,1)S(1)}, bf16[128,1920]{1,0:T(8,128)(2,1)S(1)}, u32[]{:S(2)}, u32[]{:S(2)}) collective-permute-start(bf16[128,1920]{1,0:T(8,128)(2,1)S(1)} %get-tuple-element.67), channel_id=1, source_target_pairs={{0,65},{1,64},{2,67},{3,66},{4,69},{5,68},{6,71},{7,70},{8,73},{9,... | collective-permute-start | bytes 1474568 | tf_op jit(solution)/shard_map/ppermute | solution.py:31
  6.4 14.0 %collective-permute-start.2 = (bf16[128,1920]{1,0:T(8,128)(2,1)S(1)}, bf16[128,1920]{1,0:T(8,128)(2,1)S(1)}, u32[]{:S(2)}, u32[]{:S(2)}) collective-permute-start(bf16[128,1920]{1,0:T(8,128)(2,1)S(1)} %get-tuple-element.67), channel_id=1, source_target_pairs={{0,16},{1,17},{2,18},{3,19},{4,20},{5,21},{6,22},{7,23},{8,24},{9,... | collective-permute-start | bytes 1474568 | tf_op jit(solution)/shard_map/ppermute | solution.py:31
  8.0 12.7 %collective-permute-start = (bf16[128,1920]{1,0:T(8,128)(2,1)S(1)}, bf16[128,1920]{1,0:T(8,128)(2,1)S(1)}, u32[]{:S(2)}, u32[]{:S(2)}) collective-permute-start(bf16[128,1920]{1,0:T(8,128)(2,1)S(1)} %get-tuple-element.70.refs_0_), channel_id=1, source_target_pairs={{0,1},{1,0},{2,3},{3,2},{4,5},{5,4},{6,7},{7,6},{8,9},{9,8},{10,11... | collective-permute-start | bytes 1474568 | tf_op jit(solution)/shard_map/ppermute | solution.py:31
  8.0 13.6 %collective-permute-start.1 = (bf16[128,1920]{1,0:T(8,128)(2,1)S(1)}, bf16[128,1920]{1,0:T(8,128)(2,1)S(1)}, u32[]{:S(2)}, u32[]{:S(2)}) collective-permute-start(bf16[128,1920]{1,0:T(8,128)(2,1)S(1)} %get-tuple-element.70.refs_0_), channel_id=1, source_target_pairs={{0,2},{1,3},{2,4},{3,5},{4,6},{5,7},{6,0},{7,1},{8,10},{9,11},{10,... | collective-permute-start | bytes 1474568 | tf_op jit(solution)/shard_map/ppermute | solution.py:31
  9.5 15.7 %collective-permute-start.9 = (bf16[128,1920]{1,0:T(8,128)(2,1)S(1)}, bf16[128,1920]{1,0:T(8,128)(2,1)S(1)}, u32[]{:S(2)}, u32[]{:S(2)}) collective-permute-start(bf16[128,1920]{1,0:T(8,128)(2,1)S(1)} %get-tuple-element.67), channel_id=1, source_target_pairs={{0,48},{1,49},{2,50},{3,51},{4,52},{5,53},{6,54},{7,55},{8,56},{9,... | collective-permute-start | bytes 1474568 | tf_op jit(solution)/shard_map/ppermute | solution.py:31
  20.4 13.0 %collective-permute-start.6 = (bf16[128,1920]{1,0:T(8,128)(2,1)S(1)}, bf16[128,1920]{1,0:T(8,128)(2,1)S(1)}, u32[]{:S(2)}, u32[]{:S(2)}) collective-permute-start(bf16[128,1920]{1,0:T(8,128)(2,1)S(1)} %collective-permute-done.2), channel_id=1, source_target_pairs={{0,65},{1,64},{2,67},{3,66},{4,69},{5,68},{6,71},{7,70},{8,73},{9,... | collective-permute-start | bytes 1474568 | tf_op jit(solution)/shard_map/ppermute | solution.py:31
  21.6 15.2 %collective-permute-start.7 = (bf16[128,1920]{1,0:T(8,128)(2,1)S(1)}, bf16[128,1920]{1,0:T(8,128)(2,1)S(1)}, u32[]{:S(2)}, u32[]{:S(2)}) collective-permute-start(bf16[128,1920]{1,0:T(8,128)(2,1)S(1)} %collective-permute-done.1.refs_2_), channel_id=1, source_target_pairs={{0,1},{1,0},{2,3},{3,2},{4,5},{5,4},{6,7},{7,6},{8,9},{9,8},{10,11... | collective-permute-start | bytes 1474568 | tf_op jit(solution)/shard_map/ppermute | solution.py:31
  23.4 12.1 %collective-permute-start.3 = (bf16[128,1920]{1,0:T(8,128)(2,1)S(1)}, bf16[128,1920]{1,0:T(8,128)(2,1)S(1)}, u32[]{:S(2)}, u32[]{:S(2)}) collective-permute-start(bf16[128,1920]{1,0:T(8,128)(2,1)S(1)} %collective-permute-done.2), channel_id=1, source_target_pairs={{0,16},{1,17},{2,18},{3,19},{4,20},{5,21},{6,22},{7,23},{8,24},{9,... | collective-permute-start | bytes 1474568 | tf_op jit(solution)/shard_map/ppermute | solution.py:31
  24.9 11.8 %collective-permute-start.4 = (bf16[128,1920]{1,0:T(8,128)(2,1)S(1)}, bf16[128,1920]{1,0:T(8,128)(2,1)S(1)}, u32[]{:S(2)}, u32[]{:S(2)}) collective-permute-start(bf16[128,1920]{1,0:T(8,128)(2,1)S(1)} %collective-permute-done.1.refs_2_), channel_id=1, source_target_pairs={{0,2},{1,3},{2,4},{3,5},{4,6},{5,7},{6,0},{7,1},{8,10},{9,11},{10,... | collective-permute-start | bytes 1474568 | tf_op jit(solution)/shard_map/ppermute | solution.py:31
  25.2 11.6 %collective-permute-start.8 = (bf16[128,1920]{1,0:T(8,128)(2,1)S(1)}, bf16[128,1920]{1,0:T(8,128)(2,1)S(1)}, u32[]{:S(2)}, u32[]{:S(2)}) collective-permute-start(bf16[128,1920]{1,0:T(8,128)(2,1)S(1)} %get-tuple-element.70.refs_0_), channel_id=1, source_target_pairs={{0,6},{1,7},{2,0},{3,1},{4,2},{5,3},{6,4},{7,5},{8,14},{9,15},{10,... | collective-permute-start | bytes 1474568 | tf_op jit(solution)/shard_map/ppermute | solution.py:31
  36.9 6.4 %collective-permute-start.14 = (bf16[512,1920]{1,0:T(8,128)(2,1)S(1)}, bf16[512,1920]{1,0:T(8,128)(2,1)S(1)}, u32[]{:S(2)}, u32[]{:S(2)}) collective-permute-start(bf16[512,1920]{1,0:T(8,128)(2,1)S(1)} %constant_dynamic-update-slice_fusion.refs_3_.refs_6_.refs_8_.refs_0_), channel_id=1, source_target_pairs={{0,8},{1,9},{2,10},{3,11},{4,12},{5,13},{6,14},{7,15},{8,0},{9,1},... | collective-permute-start | bytes 5898248 | tf_op jit(solution)/shard_map/ppermute | solution.py:31
  37.1 10.7 %collective-permute-start.15 = (bf16[256,1920]{1,0:T(8,128)(2,1)S(1)}, bf16[256,1920]{1,0:T(8,128)(2,1)S(1)}, u32[]{:S(2)}, u32[]{:S(2)}) collective-permute-start(bf16[256,1920]{1,0:T(8,128)(2,1)S(1)} %constant_dynamic-update-slice_fusion.4.refs_8_.refs_9_.refs_1_), channel_id=1, source_target_pairs={{0,8},{1,9},{2,10},{3,11},{4,12},{5,13},{6,14},{7,15},{8,0},{9,1},... | collective-permute-start | bytes 2949128 | tf_op jit(solution)/shard_map/ppermute | solution.py:31
  37.7 17.2 %collective-permute-start.10 = (bf16[128,1920]{1,0:T(8,128)(2,1)S(1)}, bf16[128,1920]{1,0:T(8,128)(2,1)S(1)}, u32[]{:S(2)}, u32[]{:S(2)}) collective-permute-start(bf16[128,1920]{1,0:T(8,128)(2,1)S(1)} %collective-permute-done.5), channel_id=1, source_target_pairs={{0,48},{1,49},{2,50},{3,51},{4,52},{5,53},{6,54},{7,55},{8,56},{9,... | collective-permute-start | bytes 1474568 | tf_op jit(solution)/shard_map/ppermute | solution.py:31
  39.4 16.8 %collective-permute-start.13 = (bf16[128,1920]{1,0:T(8,128)(2,1)S(1)}, bf16[128,1920]{1,0:T(8,128)(2,1)S(1)}, u32[]{:S(2)}, u32[]{:S(2)}) collective-permute-start(bf16[128,1920]{1,0:T(8,128)(2,1)S(1)} %collective-permute-done.refs_1_), channel_id=1, source_target_pairs={{0,6},{1,7},{2,0},{3,1},{4,2},{5,3},{6,4},{7,5},{8,14},{9,15},{10,... | collective-permute-start | bytes 1474568 | tf_op jit(solution)/shard_map/ppermute | solution.py:31
  42.3 13.9 %collective-permute-start.11 = (bf16[128,1920]{1,0:T(8,128)(2,1)S(1)}, bf16[128,1920]{1,0:T(8,128)(2,1)S(1)}, u32[]{:S(2)}, u32[]{:S(2)}) collective-permute-start(bf16[128,1920]{1,0:T(8,128)(2,1)S(1)} %collective-permute-done.3), channel_id=1, source_target_pairs={{0,65},{1,64},{2,67},{3,66},{4,69},{5,68},{6,71},{7,70},{8,73},{9,... | collective-permute-start | bytes 1474568 | tf_op jit(solution)/shard_map/ppermute | solution.py:31
  43.3 12.9 %collective-permute-start.12 = (bf16[128,1920]{1,0:T(8,128)(2,1)S(1)}, bf16[128,1920]{1,0:T(8,128)(2,1)S(1)}, u32[]{:S(2)}, u32[]{:S(2)}) collective-permute-start(bf16[128,1920]{1,0:T(8,128)(2,1)S(1)} %collective-permute-done.4.refs_3_), channel_id=1, source_target_pairs={{0,1},{1,0},{2,3},{3,2},{4,5},{5,4},{6,7},{7,6},{8,9},{9,8},{10,11... | collective-permute-start | bytes 1474568 | tf_op jit(solution)/shard_map/ppermute | solution.py:31
  56.3 3.5 %collective-permute-start.16 = (bf16[256,1920]{1,0:T(8,128)(2,1)S(1)}, bf16[256,1920]{1,0:T(8,128)(2,1)S(1)}, u32[]{:S(2)}, u32[]{:S(2)}) collective-permute-start(bf16[256,1920]{1,0:T(8,128)(2,1)S(1)} %constant_dynamic-update-slice_fusion.6.refs_12_.refs_4_), channel_id=1, source_target_pairs={{0,8},{1,9},{2,10},{3,11},{4,12},{5,13},{6,14},{7,15},{8,0},{9,1},... | collective-permute-start | bytes 2949128 | tf_op jit(solution)/shard_map/ppermute | solution.py:31
  61.3 1.5 %collective-permute-start.17 = (f32[8,128]{1,0:T(8,128)S(1)}, f32[8,128]{1,0:T(8,128)S(1)}, u32[]{:S(2)}, u32[]{:S(2)}) collective-permute-start(f32[8,128]{1,0:T(8,128)S(1)} %get-tuple-element.94), channel_id=1, source_target_pairs={{0,8},{1,9},{2,10},{3,11},{4,12},{5,13},{6,14},{7,15},{8,0},{9,1},... | collective-permute-start | bytes 12296 | tf_op jit(solution)/shard_map/ppermute | solution.py:31
  62.8 6.8 %collective-permute-start.18 = (bf16[1024,768]{1,0:T(8,128)(2,1)S(1)}, bf16[1024,768]{1,0:T(8,128)(2,1)S(1)}, u32[]{:S(2)}, u32[]{:S(2)}) collective-permute-start(bf16[1024,768]{1,0:T(8,128)(2,1)S(1)} %other_grad.1), channel_id=1, source_target_pairs={{0,8},{1,9},{2,10},{3,11},{4,12},{5,13},{6,14},{7,15},{8,0},{9,1},... | collective-permute-start | bytes 4718600 | tf_op jit(solution)/shard_map/ppermute | solution.py:31
  63.0 5.1 %collective-permute-start.21 = (f32[8,128]{1,0:T(8,128)S(1)}, f32[8,128]{1,0:T(8,128)S(1)}, u32[]{:S(2)}, u32[]{:S(2)}) collective-permute-start(f32[8,128]{1,0:T(8,128)S(1)} %add.12), channel_id=1, source_target_pairs={{0,4},{1,5},{2,6},{3,7},{4,0},{5,1},{6,2},{7,3},{8,12},{9,13},{10,... | collective-permute-start | bytes 12296 | tf_op jit(solution)/shard_map/ppermute | solution.py:31
  63.1 5.0 %collective-permute-start.20 = (f32[8,128]{1,0:T(8,128)S(1)}, f32[8,128]{1,0:T(8,128)S(1)}, u32[]{:S(2)}, u32[]{:S(2)}) collective-permute-start(f32[8,128]{1,0:T(8,128)S(1)} %add.12), channel_id=1, source_target_pairs={{0,6},{1,7},{2,0},{3,1},{4,2},{5,3},{6,4},{7,5},{8,14},{9,15},{10,... | collective-permute-start | bytes 12296 | tf_op jit(solution)/shard_map/ppermute | solution.py:31
  64.8 4.8 %collective-permute-start.19 = (f32[8,128]{1,0:T(8,128)S(1)}, f32[8,128]{1,0:T(8,128)S(1)}, u32[]{:S(2)}, u32[]{:S(2)}) collective-permute-start(f32[8,128]{1,0:T(8,128)S(1)} %add.12), channel_id=1, source_target_pairs={{0,2},{1,3},{2,4},{3,5},{4,6},{5,7},{6,0},{7,1},{8,10},{9,11},{10,... | collective-permute-start | bytes 12296 | tf_op jit(solution)/shard_map/ppermute | solution.py:31
  70.0 16.7 %collective-permute-start.22 = (bf16[272,768]{1,0:T(8,128)(2,1)S(1)}, bf16[272,768]{1,0:T(8,128)(2,1)S(1)}, u32[]{:S(2)}, u32[]{:S(2)}) collective-permute-start(bf16[272,768]{1,0:T(8,128)(2,1)S(1)} %get-tuple-element.109), channel_id=1, source_target_pairs={{0,48},{1,49},{2,50},{3,51},{4,52},{5,53},{6,54},{7,55},{8,56},{9,... | collective-permute-start | bytes 1253384 | tf_op jit(solution)/shard_map/ppermute | solution.py:31
  71.0 15.6 %collective-permute-start.23 = (bf16[272,768]{1,0:T(8,128)(2,1)S(1)}, bf16[272,768]{1,0:T(8,128)(2,1)S(1)}, u32[]{:S(2)}, u32[]{:S(2)}) collective-permute-start(bf16[272,768]{1,0:T(8,128)(2,1)S(1)} %get-tuple-element.110), channel_id=1, source_target_pairs={{0,16},{1,17},{2,18},{3,19},{4,20},{5,21},{6,22},{7,23},{8,24},{9,... | collective-permute-start | bytes 1253384 | tf_op jit(solution)/shard_map/ppermute | solution.py:31
  72.1 9.4 %collective-permute-start.26 = (bf16[256,768]{1,0:T(8,128)(2,1)S(1)}, bf16[256,768]{1,0:T(8,128)(2,1)S(1)}, u32[]{:S(2)}, u32[]{:S(2)}) collective-permute-start(bf16[256,768]{1,0:T(8,128)(2,1)S(1)} %get-tuple-element.114), channel_id=1, source_target_pairs={{0,6},{1,7},{2,0},{3,1},{4,2},{5,3},{6,4},{7,5},{8,14},{9,15},{10,... | collective-permute-start | bytes 1179656 | tf_op jit(solution)/shard_map/ppermute | solution.py:31
  73.2 10.9 %collective-permute-start.27 = (bf16[256,768]{1,0:T(8,128)(2,1)S(1)}, bf16[256,768]{1,0:T(8,128)(2,1)S(1)}, u32[]{:S(2)}, u32[]{:S(2)}) collective-permute-start(bf16[256,768]{1,0:T(8,128)(2,1)S(1)} %get-tuple-element.115), channel_id=1, source_target_pairs={{0,2},{1,3},{2,4},{3,5},{4,6},{5,7},{6,0},{7,1},{8,10},{9,11},{10,... | collective-permute-start | bytes 1179656 | tf_op jit(solution)/shard_map/ppermute | solution.py:31
  74.1 5.7 %collective-permute-start.28 = (bf16[128,768]{1,0:T(8,128)(2,1)S(1)}, bf16[128,768]{1,0:T(8,128)(2,1)S(1)}, u32[]{:S(2)}, u32[]{:S(2)}) collective-permute-start(bf16[128,768]{1,0:T(8,128)(2,1)S(1)} %get-tuple-element.117), channel_id=1, source_target_pairs={{0,1},{1,0},{2,3},{3,2},{4,5},{5,4},{6,7},{7,6},{8,9},{9,8},{10,11... | collective-permute-start | bytes 589832 | tf_op jit(solution)/shard_map/ppermute | solution.py:31
  79.8 6.9 %collective-permute-start.24 = (bf16[128,768]{1,0:T(8,128)(2,1)S(1)}, bf16[128,768]{1,0:T(8,128)(2,1)S(1)}, u32[]{:S(2)}, u32[]{:S(2)}) collective-permute-start(bf16[128,768]{1,0:T(8,128)(2,1)S(1)} %get-tuple-element.112), channel_id=1, source_target_pairs={{0,65},{1,64},{2,67},{3,66},{4,69},{5,68},{6,71},{7,70},{8,73},{9,... | collective-permute-start | bytes 589832 | tf_op jit(solution)/shard_map/ppermute | solution.py:31
  81.5 5.1 %collective-permute-start.25 = (f32[8,128]{1,0:T(8,128)S(1)}, f32[8,128]{1,0:T(8,128)S(1)}, u32[]{:S(2)}, u32[]{:S(2)}) collective-permute-start(f32[8,128]{1,0:T(8,128)S(1)} %add_add_fusion.loss), channel_id=1, source_target_pairs={{0,32},{1,33},{2,34},{3,35},{4,36},{5,37},{6,38},{7,39},{8,40},{9,... | collective-permute-start | bytes 12296 | tf_op jit(solution)/shard_map/ppermute | solution.py:31
  84.1 14.0 %copy-start = (bf16[128,768]{1,0:T(8,128)(2,1)S(1)}, bf16[128,768]{1,0:T(8,128)(2,1)}, u32[]{:S(2)}) copy-start(bf16[128,768]{1,0:T(8,128)(2,1)} %si.3) | copy-start | bytes 589828
  84.1 14.1 %copy-start.1 = (bf16[128,768]{1,0:T(8,128)(2,1)S(1)}, bf16[128,768]{1,0:T(8,128)(2,1)}, u32[]{:S(2)}) copy-start(bf16[128,768]{1,0:T(8,128)(2,1)} %st.3) | copy-start | bytes 589828
  86.9 11.2 %collective-permute-start.30 = (bf16[144,768]{1,0:T(8,128)(2,1)S(1)}, bf16[144,768]{1,0:T(8,128)(2,1)S(1)}, u32[]{:S(2)}, u32[]{:S(2)}) collective-permute-start(bf16[144,768]{1,0:T(8,128)(2,1)S(1)} %get-tuple-element.121), channel_id=1, source_target_pairs={{0,65},{1,64},{2,67},{3,66},{4,69},{5,68},{6,71},{7,70},{8,73},{9,... | collective-permute-start | bytes 663560 | tf_op jit(solution)/shard_map/ppermute | solution.py:31
  88.8 9.4 %collective-permute-start.32 = (bf16[144,768]{1,0:T(8,128)(2,1)S(1)}, bf16[144,768]{1,0:T(8,128)(2,1)S(1)}, u32[]{:S(2)}, u32[]{:S(2)}) collective-permute-start(bf16[144,768]{1,0:T(8,128)(2,1)S(1)} %get-tuple-element.124), channel_id=1, source_target_pairs={{0,1},{1,0},{2,3},{3,2},{4,5},{5,4},{6,7},{7,6},{8,9},{9,8},{10,11... | collective-permute-start | bytes 663560 | tf_op jit(solution)/shard_map/ppermute | solution.py:31
  89.1 7.2 %collective-permute-start.33 = (bf16[128,768]{1,0:T(8,128)(2,1)S(1)}, bf16[128,768]{1,0:T(8,128)(2,1)S(1)}, u32[]{:S(2)}, u32[]{:S(2)}) collective-permute-start(bf16[128,768]{1,0:T(8,128)(2,1)S(1)} %get-tuple-element.125), channel_id=1, source_target_pairs={{0,4},{1,5},{2,6},{3,7},{4,0},{5,1},{6,2},{7,3},{8,12},{9,13},{10,... | collective-permute-start | bytes 589832 | tf_op jit(solution)/shard_map/ppermute | solution.py:31
  91.0 7.2 %collective-permute-start.31 = (bf16[128,768]{1,0:T(8,128)(2,1)S(1)}, bf16[128,768]{1,0:T(8,128)(2,1)S(1)}, u32[]{:S(2)}, u32[]{:S(2)}) collective-permute-start(bf16[128,768]{1,0:T(8,128)(2,1)S(1)} %get-tuple-element.122), channel_id=1, source_target_pairs={{0,32},{1,33},{2,34},{3,35},{4,36},{5,37},{6,38},{7,39},{8,40},{9,... | collective-permute-start | bytes 589832 | tf_op jit(solution)/shard_map/ppermute | solution.py:31
  92.6 5.1 %collective-permute-start.29 = (f32[8,128]{1,0:T(8,128)S(1)}, f32[8,128]{1,0:T(8,128)S(1)}, u32[]{:S(2)}, u32[]{:S(2)}) collective-permute-start(f32[8,128]{1,0:T(8,128)S(1)} %get-tuple-element.119.loss), channel_id=1, source_target_pairs={{0,64},{1,65},{2,66},{3,67},{4,68},{5,69},{6,70},{7,71},{8,72},{9,... | collective-permute-start | bytes 12296 | tf_op jit(solution)/shard_map/ppermute | solution.py:31

commit v6 on v5

--- a/solution.py
+++ b/solution.py
@@ -119,6 +119,16 @@
     return lax.dot_general(a, b, dims, preferred_element_type=f32)
 
 
+def tile_blocks(left_t, left_s, right_t, right_s, size):
+    coefs, total = [], jnp.zeros((8, 128), f32)
+    for at in range(0, left_t.shape[0], size):
+        part = slice(at, at + size)
+        coef, loss = tile_terms(dot(left_t[part], right_t, NT), dot(left_s[part], right_s, NT))
+        coefs.append(coef)
+        total = total + loss
+    return jnp.concatenate(coefs, axis=0), total
+
+
 def near_tile_kernel(width_t, *refs):
     imgs, texts, (g_img, g_txt, g_oth, loss_ref) = refs[:3], refs[3:5], refs[5:]
     cols_t, cols_s = slice(0, width_t), slice(width_t, None)
@@ -137,8 +147,8 @@
     cols_t, cols_s = slice(0, width_t), slice(width_t, None)
     img_s, add_s = stack(imgs, cols_s), stack(imgs[3:], cols_s)
     old_s, new_s = stack(old, cols_s), stack(new, cols_s)
-    coef_i, loss_i = tile_terms(dot(stack(imgs, cols_t), stack(new, cols_t), NT), dot(img_s, new_s, NT))
-    coef_t, loss_t = tile_terms(dot(stack(old, cols_t), stack(imgs[3:], cols_t), NT), dot(old_s, add_s, NT))
+    coef_i, loss_i = tile_blocks(stack(imgs, cols_t), img_s, stack(new, cols_t), new_s, 256)
+    coef_t, loss_t = tile_blocks(stack(old, cols_t), old_s, stack(imgs[3:], cols_t), add_s, 256)
     loss_ref[...] = p_loss[...] + loss_i + loss_t
     some, half, add = p_img.shape[0], p_txt.shape[0], new[0].shape[0]
     grad = dot(coef_i, new_s)

time: 100 us -> 100 us (level)
  transfers between devices with their start and end apart: 34 -> 34, of which waited for: 15 -> 15; matrix products, arithmetic and copies ran while one was open for 0% -> 0% of each run, Pallas kernels for 18% -> 17%
where the time goes in v6:
time: 100 us; the launch traced here: 99.4 us
  starting transfers between devices  43.2 us (43%)
  waiting for transfers between devices  32.8 us (33%)
  Pallas kernels  22.3 us (22%)
    ppermute x34, starting transfers between devices, permute(): return lax.ppermute(value, AXES, pairs)  43.2 us
    ppermute x34, waiting for transfers between devices, permute(): return lax.ppermute(value, AXES, pairs)  32.8 us
    pallas_call x12, Pallas kernels, call(): pl.pallas_call(kernel, out_shape=tuple((shape_of(shape, dtype) for shape,...  22.3 us
  transfers between devices with their start and end apart: 34, of which 15 were waited for; matrix products, arithmetic and copies ran while one was open for 0% of the time, Pallas kernels for 17%

profile of v6, /device:TPU:0, one launch (start us, length us, event | category | flops | bytes accessed | tf_op | source)
XLA Modules:
  0.0 99.4 jit_solution(14078440021556997652)
XLA Ops:
  0.6 1.6 %units.1 = (bf16[128,1920]{1,0:T(8,128)(2,1)S(1)}, bf16[128,1920]{1,0:T(8,128)(2,1)S(1)}) custom-call(bf16[128,1152]{1,0:T(8,128)(2,1)} %ti.1, bf16[128,768]{1,0:T(8,128)(2,1)} %si.3, bf16[128,1152]{1,0:T(8,128)(2,1)} %tt.1, bf16[128,768]{1,0:T(8,128)(2,1)} %st.3), custom_call_target="tpu_custom_call" | custom-call | bytes 983040 | tf_op jit(solution)/shard_map/units/pallas_call | solution.py:72
  2.2 4.2 %collective-permute-start.5 = (bf16[128,1920]{1,0:T(8,128)(2,1)S(1)}, bf16[128,1920]{1,0:T(8,128)(2,1)S(1)}, u32[]{:S(2)}, u32[]{:S(2)}) collective-permute-start(bf16[128,1920]{1,0:T(8,128)(2,1)S(1)} %get-tuple-element.67), channel_id=1, source_target_pairs={{0,65},{1,64},{2,67},{3,66},{4,69},{5,68},{6,71},{7,70},{8,73},{9,... | collective-permute-start | bytes 1474568 | tf_op jit(solution)/shard_map/ppermute | solution.py:31
  6.4 1.6 %collective-permute-start.2 = (bf16[128,1920]{1,0:T(8,128)(2,1)S(1)}, bf16[128,1920]{1,0:T(8,128)(2,1)S(1)}, u32[]{:S(2)}, u32[]{:S(2)}) collective-permute-start(bf16[128,1920]{1,0:T(8,128)(2,1)S(1)} %get-tuple-element.67), channel_id=1, source_target_pairs={{0,16},{1,17},{2,18},{3,19},{4,20},{5,21},{6,22},{7,23},{8,24},{9,... | collective-permute-start | bytes 1474568 | tf_op jit(solution)/shard_map/ppermute | solution.py:31
  8.0 1.5 %collective-permute-start.1 = (bf16[128,1920]{1,0:T(8,128)(2,1)S(1)}, bf16[128,1920]{1,0:T(8,128)(2,1)S(1)}, u32[]{:S(2)}, u32[]{:S(2)}) collective-permute-start(bf16[128,1920]{1,0:T(8,128)(2,1)S(1)} %get-tuple-element.70.refs_0_), channel_id=1, source_target_pairs={{0,2},{1,3},{2,4},{3,5},{4,6},{5,7},{6,0},{7,1},{8,10},{9,11},{10,... | collective-permute-start | bytes 1474568 | tf_op jit(solution)/shard_map/ppermute | solution.py:31
  9.5 1.7 %collective-permute-start.9 = (bf16[128,1920]{1,0:T(8,128)(2,1)S(1)}, bf16[128,1920]{1,0:T(8,128)(2,1)S(1)}, u32[]{:S(2)}, u32[]{:S(2)}) collective-permute-start(bf16[128,1920]{1,0:T(8,128)(2,1)S(1)} %get-tuple-element.67), channel_id=1, source_target_pairs={{0,48},{1,49},{2,50},{3,51},{4,52},{5,53},{6,54},{7,55},{8,56},{9,... | collective-permute-start | bytes 1474568 | tf_op jit(solution)/shard_map/ppermute | solution.py:31
  11.2 6.5 %collective-permute-done.5 = bf16[128,1920]{1,0:T(8,128)(2,1)S(1)} collective-permute-done((bf16[128,1920]{1,0:T(8,128)(2,1)S(1)}, bf16[128,1920]{1,0:T(8,128)(2,1)S(1)}, u32[]{:S(2)}, u32[]{:S(2)}) %collective-permute-start.5) | collective-permute-done | bytes 491552 | tf_op jit(solution)/shard_map/ppermute | solution.py:31
  17.6 2.7 %collective-permute-done.2 = bf16[128,1920]{1,0:T(8,128)(2,1)S(1)} collective-permute-done((bf16[128,1920]{1,0:T(8,128)(2,1)S(1)}, bf16[128,1920]{1,0:T(8,128)(2,1)S(1)}, u32[]{:S(2)}, u32[]{:S(2)}) %collective-permute-start.2) | collective-permute-done | bytes 491552 | tf_op jit(solution)/shard_map/ppermute | solution.py:31
  20.4 0.4 collective-permute-start.6
  20.7 0.9 collective-permute-done.1.refs_2_
  21.6 1.7 %collective-permute-start.7 = (bf16[128,1920]{1,0:T(8,128)(2,1)S(1)}, bf16[128,1920]{1,0:T(8,128)(2,1)S(1)}, u32[]{:S(2)}, u32[]{:S(2)}) collective-permute-start(bf16[128,1920]{1,0:T(8,128)(2,1)S(1)} %collective-permute-done.1.refs_2_), channel_id=1, source_target_pairs={{0,1},{1,0},{2,3},{3,2},{4,5},{5,4},{6,7},{7,6},{8,9},{9,8},{10,11... | collective-permute-start | bytes 1474568 | tf_op jit(solution)/shard_map/ppermute | solution.py:31
  23.4 1.6 %collective-permute-start.3 = (bf16[128,1920]{1,0:T(8,128)(2,1)S(1)}, bf16[128,1920]{1,0:T(8,128)(2,1)S(1)}, u32[]{:S(2)}, u32[]{:S(2)}) collective-permute-start(bf16[128,1920]{1,0:T(8,128)(2,1)S(1)} %collective-permute-done.2), channel_id=1, source_target_pairs={{0,16},{1,17},{2,18},{3,19},{4,20},{5,21},{6,22},{7,23},{8,24},{9,... | collective-permute-start | bytes 1474568 | tf_op jit(solution)/shard_map/ppermute | solution.py:31
  24.9 0.3 collective-permute-start.4
  25.2 0.0 collective-permute-done.9
  25.2 3.0 %collective-permute-start.8 = (bf16[128,1920]{1,0:T(8,128)(2,1)S(1)}, bf16[128,1920]{1,0:T(8,128)(2,1)S(1)}, u32[]{:S(2)}, u32[]{:S(2)}) collective-permute-start(bf16[128,1920]{1,0:T(8,128)(2,1)S(1)} %get-tuple-element.70.refs_0_), channel_id=1, source_target_pairs={{0,6},{1,7},{2,0},{3,1},{4,2},{5,3},{6,4},{7,5},{8,14},{9,15},{10,... | collective-permute-start | bytes 1474568 | tf_op jit(solution)/shard_map/ppermute | solution.py:31
  28.2 5.2 %collective-permute-done.6 = bf16[128,1920]{1,0:T(8,128)(2,1)S(1)} collective-permute-done((bf16[128,1920]{1,0:T(8,128)(2,1)S(1)}, bf16[128,1920]{1,0:T(8,128)(2,1)S(1)}, u32[]{:S(2)}, u32[]{:S(2)}) %collective-permute-start.6) | collective-permute-done | bytes 491552 | tf_op jit(solution)/shard_map/ppermute | solution.py:31
  33.4 2.1 %collective-permute-done.3 = bf16[128,1920]{1,0:T(8,128)(2,1)S(1)} collective-permute-done((bf16[128,1920]{1,0:T(8,128)(2,1)S(1)}, bf16[128,1920]{1,0:T(8,128)(2,1)S(1)}, u32[]{:S(2)}, u32[]{:S(2)}) %collective-permute-start.3) | collective-permute-done | bytes 491552 | tf_op jit(solution)/shard_map/ppermute | solution.py:31
  35.5 1.3 %collective-permute-done.4.refs_3_ = bf16[128,1920]{1,0:T(8,128)(2,1)S(1)} collective-permute-done((bf16[128,1920]{1,0:T(8,128)(2,1)S(1)}, bf16[128,1920]{1,0:T(8,128)(2,1)S(1)}, u32[]{:S(2)}, u32[]{:S(2)}) %collective-permute-start.4) | collective-permute-done | bytes 491552 | tf_op jit(solution)/shard_map/ppermute | solution.py:31
  36.9 0.1 collective-permute-start.14
  37.1 0.6 collective-permute-start.15
  37.7 1.7 %collective-permute-start.10 = (bf16[128,1920]{1,0:T(8,128)(2,1)S(1)}, bf16[128,1920]{1,0:T(8,128)(2,1)S(1)}, u32[]{:S(2)}, u32[]{:S(2)}) collective-permute-start(bf16[128,1920]{1,0:T(8,128)(2,1)S(1)} %collective-permute-done.5), channel_id=1, source_target_pairs={{0,48},{1,49},{2,50},{3,51},{4,52},{5,53},{6,54},{7,55},{8,56},{9,... | collective-permute-start | bytes 1474568 | tf_op jit(solution)/shard_map/ppermute | solution.py:31
  39.4 3.0 %collective-permute-start.13 = (bf16[128,1920]{1,0:T(8,128)(2,1)S(1)}, bf16[128,1920]{1,0:T(8,128)(2,1)S(1)}, u32[]{:S(2)}, u32[]{:S(2)}) collective-permute-start(bf16[128,1920]{1,0:T(8,128)(2,1)S(1)} %collective-permute-done.refs_1_), channel_id=1, source_target_pairs={{0,6},{1,7},{2,0},{3,1},{4,2},{5,3},{6,4},{7,5},{8,14},{9,15},{10,... | collective-permute-start | bytes 1474568 | tf_op jit(solution)/shard_map/ppermute | solution.py:31
  42.3 1.0 collective-permute-start.11
  43.3 0.0 collective-permute-done.14.refs_4_.refs_7_.refs_10_.refs_2_
  43.3 1.1 %collective-permute-start.12 = (bf16[128,1920]{1,0:T(8,128)(2,1)S(1)}, bf16[128,1920]{1,0:T(8,128)(2,1)S(1)}, u32[]{:S(2)}, u32[]{:S(2)}) collective-permute-start(bf16[128,1920]{1,0:T(8,128)(2,1)S(1)} %collective-permute-done.4.refs_3_), channel_id=1, source_target_pairs={{0,1},{1,0},{2,3},{3,2},{4,5},{5,4},{6,7},{7,6},{8,9},{9,8},{10,11... | collective-permute-start | bytes 1474568 | tf_op jit(solution)/shard_map/ppermute | solution.py:31
  44.4 3.5 %near_tile.1 = (f32[384,768]{1,0:T(8,128)S(1)}, f32[512,768]{1,0:T(8,128)S(1)}, f32[512,768]{1,0:T(8,128)S(1)}, f32[8,128]{1,0:T(8,128)S(1)}) custom-call(bf16[128,1920]{1,0:T(8,128)(2,1)S(1)} %get-tuple-element.70.refs_0_, bf16[128,1920]{1,0:T(8,128)(2,1)S(1)} %collective-permute-done.refs_1_, bf16[128,1920]{1,0:T(8,128)(2,1)S(1)} %collective-permute-done.1.refs_2_, ...), custom_call_target="tpu_custom_call" | custom-call | flops 2717908992 | bytes 5406720 | tf_op jit(solution)/shard_map/near_tile/pallas_call | solution.py:72
  47.8 0.0 collective-permute-done.15.refs_9_.refs_11_.refs_3_
  47.9 6.9 %mid_tile.1 = (f32[768,768]{1,0:T(8,128)S(1)}, f32[768,768]{1,0:T(8,128)S(1)}, f32[768,768]{1,0:T(8,128)S(1)}, f32[8,128]{1,0:T(8,128)S(1)}) custom-call(bf16[128,1920]{1,0:T(8,128)(2,1)S(1)} %get-tuple-element.70.refs_0_, bf16[128,1920]{1,0:T(8,128)(2,1)S(1)} %collective-permute-done.refs_1_, bf16[128,1920]{1,0:T(8,128)(2,1)S(1)} %collective-permute-done.1.refs_2_, ...), custom_call_target="tpu_custom_call" | custom-call | flops 5435817984 | bytes 13176832 | tf_op jit(solution)/shard_map/mid_tile/pallas_call | solution.py:72
  54.8 1.4 %collective-permute-done.11 = bf16[128,1920]{1,0:T(8,128)(2,1)S(1)} collective-permute-done((bf16[128,1920]{1,0:T(8,128)(2,1)S(1)}, bf16[128,1920]{1,0:T(8,128)(2,1)S(1)}, u32[]{:S(2)}, u32[]{:S(2)}) %collective-permute-start.11) | collective-permute-done | bytes 491552 | tf_op jit(solution)/shard_map/ppermute | solution.py:31
  56.3 0.3 collective-permute-start.16
  56.6 3.2 %last_coef.1 = (bf16[1536,256]{1,0:T(8,128)(2,1)S(1)}, bf16[1024,256]{1,0:T(8,128)(2,1)S(1)}, f32[8,128]{1,0:T(8,128)S(1)}) custom-call(bf16[128,1920]{1,0:T(8,128)(2,1)S(1)} %get-tuple-element.70.refs_0_, bf16[128,1920]{1,0:T(8,128)(2,1)S(1)} %collective-permute-done.refs_1_, bf16[128,1920]{1,0:T(8,128)(2,1)S(1)} %collective-permute-done.1.refs_2_, ...), custom_call_target="tpu_custom_call" | custom-call | flops 2516582400 | bytes 10817536 | tf_op jit(solution)/shard_map/last_coef/pallas_call | solution.py:72
  59.8 1.4 %end_coef.1 = (bf16[1024,256]{1,0:T(8,128)(2,1)S(1)}, f32[8,128]{1,0:T(8,128)S(1)}) custom-call(bf16[128,1920]{1,0:T(8,128)(2,1)S(1)} %get-tuple-element.70.refs_0_, bf16[128,1920]{1,0:T(8,128)(2,1)S(1)} %collective-permute-done.refs_1_, bf16[128,1920]{1,0:T(8,128)(2,1)S(1)} %collective-permute-done.1.refs_2_, ...), custom_call_target="tpu_custom_call" | custom-call | flops 1006632960 | bytes 4919296 | tf_op jit(solution)/shard_map/end_coef/pallas_call | solution.py:72
  61.3 0.6 collective-permute-start.17
  61.9 0.9 other_grad.1
  62.8 0.2 collective-permute-start.18
  63.0 0.1 collective-permute-start.21
  63.1 1.7 %collective-permute-start.20 = (f32[8,128]{1,0:T(8,128)S(1)}, f32[8,128]{1,0:T(8,128)S(1)}, u32[]{:S(2)}, u32[]{:S(2)}) collective-permute-start(f32[8,128]{1,0:T(8,128)S(1)} %add.12), channel_id=1, source_target_pairs={{0,6},{1,7},{2,0},{3,1},{4,2},{5,3},{6,4},{7,5},{8,14},{9,15},{10,... | collective-permute-start | bytes 12296 | tf_op jit(solution)/shard_map/ppermute | solution.py:31
  64.8 0.4 collective-permute-start.19
  65.2 1.7 %image_grad.1 = (f32[256,768]{1,0:T(8,128)S(1)}, bf16[256,768]{1,0:T(8,128)(2,1)S(1)}, bf16[256,768]{1,0:T(8,128)(2,1)S(1)}, f32[128,768]{1,0:T(8,128)S(1)}, bf16[128,768]{1,0:T(8,128)(2,1)S(1)}) custom-call(bf16[512,1920]{1,0:T(8,128)(2,1)S(1)} %constant_dynamic-update-slice_fusion.refs_3_.refs_6_.refs_8_.refs_0_, ...), custom_call_target="tpu_custom_call" | custom-call | flops 1409286144 | bytes 12058624 | tf_op jit(solution)/shard_map/image_grad/pallas_call | solution.py:72
  66.9 0.9 text_grad.1.own
  67.8 0.4 collective-permute-done.21
  68.2 1.4 %collective-permute-done.19 = f32[8,128]{1,0:T(8,128)S(1)} collective-permute-done((f32[8,128]{1,0:T(8,128)S(1)}, f32[8,128]{1,0:T(8,128)S(1)}, u32[]{:S(2)}, u32[]{:S(2)}) %collective-permute-start.19) | collective-permute-done | bytes 4128 | tf_op jit(solution)/shard_map/ppermute | solution.py:31
  69.6 0.4 text_sum.1
  70.0 1.0 %collective-permute-start.22 = (bf16[272,768]{1,0:T(8,128)(2,1)S(1)}, bf16[272,768]{1,0:T(8,128)(2,1)S(1)}, u32[]{:S(2)}, u32[]{:S(2)}) collective-permute-start(bf16[272,768]{1,0:T(8,128)(2,1)S(1)} %get-tuple-element.109), channel_id=1, source_target_pairs={{0,48},{1,49},{2,50},{3,51},{4,52},{5,53},{6,54},{7,55},{8,56},{9,... | collective-permute-start | bytes 1253384 | tf_op jit(solution)/shard_map/ppermute | solution.py:31
  71.0 1.1 %collective-permute-start.23 = (bf16[272,768]{1,0:T(8,128)(2,1)S(1)}, bf16[272,768]{1,0:T(8,128)(2,1)S(1)}, u32[]{:S(2)}, u32[]{:S(2)}) collective-permute-start(bf16[272,768]{1,0:T(8,128)(2,1)S(1)} %get-tuple-element.110), channel_id=1, source_target_pairs={{0,16},{1,17},{2,18},{3,19},{4,20},{5,21},{6,22},{7,23},{8,24},{9,... | collective-permute-start | bytes 1253384 | tf_op jit(solution)/shard_map/ppermute | solution.py:31
  72.1 1.1 %collective-permute-start.26 = (bf16[256,768]{1,0:T(8,128)(2,1)S(1)}, bf16[256,768]{1,0:T(8,128)(2,1)S(1)}, u32[]{:S(2)}, u32[]{:S(2)}) collective-permute-start(bf16[256,768]{1,0:T(8,128)(2,1)S(1)} %get-tuple-element.114), channel_id=1, source_target_pairs={{0,6},{1,7},{2,0},{3,1},{4,2},{5,3},{6,4},{7,5},{8,14},{9,15},{10,... | collective-permute-start | bytes 1179656 | tf_op jit(solution)/shard_map/ppermute | solution.py:31
  73.2 0.9 collective-permute-start.27
  74.1 0.6 collective-permute-start.28
  74.7 5.1 %collective-permute-done.28.from_z = bf16[128,768]{1,0:T(8,128)(2,1)S(1)} collective-permute-done((bf16[128,768]{1,0:T(8,128)(2,1)S(1)}, bf16[128,768]{1,0:T(8,128)(2,1)S(1)}, u32[]{:S(2)}, u32[]{:S(2)}) %collective-permute-start.28) | collective-permute-done | bytes 196640 | tf_op jit(solution)/shard_map/ppermute | solution.py:31
  79.8 1.7 %collective-permute-start.24 = (bf16[128,768]{1,0:T(8,128)(2,1)S(1)}, bf16[128,768]{1,0:T(8,128)(2,1)S(1)}, u32[]{:S(2)}, u32[]{:S(2)}) collective-permute-start(bf16[128,768]{1,0:T(8,128)(2,1)S(1)} %get-tuple-element.112), channel_id=1, source_target_pairs={{0,65},{1,64},{2,67},{3,66},{4,69},{5,68},{6,71},{7,70},{8,73},{9,... | collective-permute-start | bytes 589832 | tf_op jit(solution)/shard_map/ppermute | solution.py:31
  81.5 1.7 %collective-permute-start.25 = (f32[8,128]{1,0:T(8,128)S(1)}, f32[8,128]{1,0:T(8,128)S(1)}, u32[]{:S(2)}, u32[]{:S(2)}) collective-permute-start(f32[8,128]{1,0:T(8,128)S(1)} %add_add_fusion.loss), channel_id=1, source_target_pairs={{0,32},{1,33},{2,34},{3,35},{4,36},{5,37},{6,38},{7,39},{8,40},{9,... | collective-permute-start | bytes 12296 | tf_op jit(solution)/shard_map/ppermute | solution.py:31
  83.2 0.9 collective-permute-done.27.two
  84.1 0.1 image_ring.1
  84.2 2.4 %collective-permute-done.25.loss_far = f32[8,128]{1,0:T(8,128)S(1)} collective-permute-done((f32[8,128]{1,0:T(8,128)S(1)}, f32[8,128]{1,0:T(8,128)S(1)}, u32[]{:S(2)}, u32[]{:S(2)}) %collective-permute-start.25) | collective-permute-done | bytes 4128 | tf_op jit(solution)/shard_map/ppermute | solution.py:31
  86.6 0.0 collective-permute-done.24.from_z
  86.7 0.3 text_ring.1
  86.9 1.8 %collective-permute-start.30 = (bf16[144,768]{1,0:T(8,128)(2,1)S(1)}, bf16[144,768]{1,0:T(8,128)(2,1)S(1)}, u32[]{:S(2)}, u32[]{:S(2)}) collective-permute-start(bf16[144,768]{1,0:T(8,128)(2,1)S(1)} %get-tuple-element.121), channel_id=1, source_target_pairs={{0,65},{1,64},{2,67},{3,66},{4,69},{5,68},{6,71},{7,70},{8,73},{9,... | collective-permute-start | bytes 663560 | tf_op jit(solution)/shard_map/ppermute | solution.py:31
  88.8 0.4 collective-permute-start.32
  89.1 1.8 %collective-permute-start.33 = (bf16[128,768]{1,0:T(8,128)(2,1)S(1)}, bf16[128,768]{1,0:T(8,128)(2,1)S(1)}, u32[]{:S(2)}, u32[]{:S(2)}) collective-permute-start(bf16[128,768]{1,0:T(8,128)(2,1)S(1)} %get-tuple-element.125), channel_id=1, source_target_pairs={{0,4},{1,5},{2,6},{3,7},{4,0},{5,1},{6,2},{7,3},{8,12},{9,13},{10,... | collective-permute-start | bytes 589832 | tf_op jit(solution)/shard_map/ppermute | solution.py:31
  91.0 1.7 %collective-permute-start.31 = (bf16[128,768]{1,0:T(8,128)(2,1)S(1)}, bf16[128,768]{1,0:T(8,128)(2,1)S(1)}, u32[]{:S(2)}, u32[]{:S(2)}) collective-permute-start(bf16[128,768]{1,0:T(8,128)(2,1)S(1)} %get-tuple-element.122), channel_id=1, source_target_pairs={{0,32},{1,33},{2,34},{3,35},{4,36},{5,37},{6,38},{7,39},{8,40},{9,... | collective-permute-start | bytes 589832 | tf_op jit(solution)/shard_map/ppermute | solution.py:31
  92.6 3.0 %collective-permute-start.29 = (f32[8,128]{1,0:T(8,128)S(1)}, f32[8,128]{1,0:T(8,128)S(1)}, u32[]{:S(2)}, u32[]{:S(2)}) collective-permute-start(f32[8,128]{1,0:T(8,128)S(1)} %get-tuple-element.119.loss), channel_id=1, source_target_pairs={{0,64},{1,65},{2,66},{3,67},{4,68},{5,69},{6,70},{7,71},{8,72},{9,... | collective-permute-start | bytes 12296 | tf_op jit(solution)/shard_map/ppermute | solution.py:31
  95.6 0.7 collective-permute-done.33.img_x
  96.3 1.5 %collective-permute-done.29.loss_far = f32[8,128]{1,0:T(8,128)S(1)} collective-permute-done((f32[8,128]{1,0:T(8,128)S(1)}, f32[8,128]{1,0:T(8,128)S(1)}, u32[]{:S(2)}, u32[]{:S(2)}) %collective-permute-start.29) | collective-permute-done | bytes 4128 | tf_op jit(solution)/shard_map/ppermute | solution.py:31
  97.8 0.4 collective-permute-done.31.txt_x
  98.1 1.3 %finish.1 = (f32[128,768]{1,0:T(8,128)}, f32[128,768]{1,0:T(8,128)}, f32[1,1]{1,0:T(1,128)}) custom-call(f32[8,128]{1,0:T(8,128)S(1)} %get-tuple-element.119.loss, f32[8,128]{1,0:T(8,128)S(1)} %collective-permute-done.29.loss_far, f32[128,768]{1,0:T(8,128)S(1)} %get-tuple-element.120.txt, bf16[144,768]{1,0:T(8,128)(2,1)S(1)} %collective-permute-done.30.txt_z, ...), custom_call_target="tpu_custom_call" | custom-call | bytes 2023424 | tf_op jit(solution)/shard_map/finish/pallas_call | solution.py:72
  (30 shorter events, 0.4 us)
Async XLA Ops:
  2.2 15.4 %collective-permute-start.5 = (bf16[128,1920]{1,0:T(8,128)(2,1)S(1)}, bf16[128,1920]{1,0:T(8,128)(2,1)S(1)}, u32[]{:S(2)}, u32[]{:S(2)}) collective-permute-start(bf16[128,1920]{1,0:T(8,128)(2,1)S(1)} %get-tuple-element.67), channel_id=1, source_target_pairs={{0,65},{1,64},{2,67},{3,66},{4,69},{5,68},{6,71},{7,70},{8,73},{9,... | collective-permute-start | bytes 1474568 | tf_op jit(solution)/shard_map/ppermute | solution.py:31
  6.4 14.0 %collective-permute-start.2 = (bf16[128,1920]{1,0:T(8,128)(2,1)S(1)}, bf16[128,1920]{1,0:T(8,128)(2,1)S(1)}, u32[]{:S(2)}, u32[]{:S(2)}) collective-permute-start(bf16[128,1920]{1,0:T(8,128)(2,1)S(1)} %get-tuple-element.67), channel_id=1, source_target_pairs={{0,16},{1,17},{2,18},{3,19},{4,20},{5,21},{6,22},{7,23},{8,24},{9,... | collective-permute-start | bytes 1474568 | tf_op jit(solution)/shard_map/ppermute | solution.py:31
  8.0 12.7 %collective-permute-start = (bf16[128,1920]{1,0:T(8,128)(2,1)S(1)}, bf16[128,1920]{1,0:T(8,128)(2,1)S(1)}, u32[]{:S(2)}, u32[]{:S(2)}) collective-permute-start(bf16[128,1920]{1,0:T(8,128)(2,1)S(1)} %get-tuple-element.70.refs_0_), channel_id=1, source_target_pairs={{0,1},{1,0},{2,3},{3,2},{4,5},{5,4},{6,7},{7,6},{8,9},{9,8},{10,11... | collective-permute-start | bytes 1474568 | tf_op jit(solution)/shard_map/ppermute | solution.py:31
  8.0 13.6 %collective-permute-start.1 = (bf16[128,1920]{1,0:T(8,128)(2,1)S(1)}, bf16[128,1920]{1,0:T(8,128)(2,1)S(1)}, u32[]{:S(2)}, u32[]{:S(2)}) collective-permute-start(bf16[128,1920]{1,0:T(8,128)(2,1)S(1)} %get-tuple-element.70.refs_0_), channel_id=1, source_target_pairs={{0,2},{1,3},{2,4},{3,5},{4,6},{5,7},{6,0},{7,1},{8,10},{9,11},{10,... | collective-permute-start | bytes 1474568 | tf_op jit(solution)/shard_map/ppermute | solution.py:31
  9.5 15.7 %collective-permute-start.9 = (bf16[128,1920]{1,0:T(8,128)(2,1)S(1)}, bf16[128,1920]{1,0:T(8,128)(2,1)S(1)}, u32[]{:S(2)}, u32[]{:S(2)}) collective-permute-start(bf16[128,1920]{1,0:T(8,128)(2,1)S(1)} %get-tuple-element.67), channel_id=1, source_target_pairs={{0,48},{1,49},{2,50},{3,51},{4,52},{5,53},{6,54},{7,55},{8,56},{9,... | collective-permute-start | bytes 1474568 | tf_op jit(solution)/shard_map/ppermute | solution.py:31
  20.4 13.0 %collective-permute-start.6 = (bf16[128,1920]{1,0:T(8,128)(2,1)S(1)}, bf16[128,1920]{1,0:T(8,128)(2,1)S(1)}, u32[]{:S(2)}, u32[]{:S(2)}) collective-permute-start(bf16[128,1920]{1,0:T(8,128)(2,1)S(1)} %collective-permute-done.2), channel_id=1, source_target_pairs={{0,65},{1,64},{2,67},{3,66},{4,69},{5,68},{6,71},{7,70},{8,73},{9,... | collective-permute-start | bytes 1474568 | tf_op jit(solution)/shard_map/ppermute | solution.py:31
  21.6 15.2 %collective-permute-start.7 = (bf16[128,1920]{1,0:T(8,128)(2,1)S(1)}, bf16[128,1920]{1,0:T(8,128)(2,1)S(1)}, u32[]{:S(2)}, u32[]{:S(2)}) collective-permute-start(bf16[128,1920]{1,0:T(8,128)(2,1)S(1)} %collective-permute-done.1.refs_2_), channel_id=1, source_target_pairs={{0,1},{1,0},{2,3},{3,2},{4,5},{5,4},{6,7},{7,6},{8,9},{9,8},{10,11... | collective-permute-start | bytes 1474568 | tf_op jit(solution)/shard_map/ppermute | solution.py:31
  23.4 12.1 %collective-permute-start.3 = (bf16[128,1920]{1,0:T(8,128)(2,1)S(1)}, bf16[128,1920]{1,0:T(8,128)(2,1)S(1)}, u32[]{:S(2)}, u32[]{:S(2)}) collective-permute-start(bf16[128,1920]{1,0:T(8,128)(2,1)S(1)} %collective-permute-done.2), channel_id=1, source_target_pairs={{0,16},{1,17},{2,18},{3,19},{4,20},{5,21},{6,22},{7,23},{8,24},{9,... | collective-permute-start | bytes 1474568 | tf_op jit(solution)/shard_map/ppermute | solution.py:31
  24.9 11.8 %collective-permute-start.4 = (bf16[128,1920]{1,0:T(8,128)(2,1)S(1)}, bf16[128,1920]{1,0:T(8,128)(2,1)S(1)}, u32[]{:S(2)}, u32[]{:S(2)}) collective-permute-start(bf16[128,1920]{1,0:T(8,128)(2,1)S(1)} %collective-permute-done.1.refs_2_), channel_id=1, source_target_pairs={{0,2},{1,3},{2,4},{3,5},{4,6},{5,7},{6,0},{7,1},{8,10},{9,11},{10,... | collective-permute-start | bytes 1474568 | tf_op jit(solution)/shard_map/ppermute | solution.py:31
  25.2 11.6 %collective-permute-start.8 = (bf16[128,1920]{1,0:T(8,128)(2,1)S(1)}, bf16[128,1920]{1,0:T(8,128)(2,1)S(1)}, u32[]{:S(2)}, u32[]{:S(2)}) collective-permute-start(bf16[128,1920]{1,0:T(8,128)(2,1)S(1)} %get-tuple-element.70.refs_0_), channel_id=1, source_target_pairs={{0,6},{1,7},{2,0},{3,1},{4,2},{5,3},{6,4},{7,5},{8,14},{9,15},{10,... | collective-permute-start | bytes 1474568 | tf_op jit(solution)/shard_map/ppermute | solution.py:31
  36.9 6.4 %collective-permute-start.14 = (bf16[512,1920]{1,0:T(8,128)(2,1)S(1)}, bf16[512,1920]{1,0:T(8,128)(2,1)S(1)}, u32[]{:S(2)}, u32[]{:S(2)}) collective-permute-start(bf16[512,1920]{1,0:T(8,128)(2,1)S(1)} %constant_dynamic-update-slice_fusion.refs_3_.refs_6_.refs_8_.refs_0_), channel_id=1, source_target_pairs={{0,8},{1,9},{2,10},{3,11},{4,12},{5,13},{6,14},{7,15},{8,0},{9,1},... | collective-permute-start | bytes 5898248 | tf_op jit(solution)/shard_map/ppermute | solution.py:31
  37.1 10.7 %collective-permute-start.15 = (bf16[256,1920]{1,0:T(8,128)(2,1)S(1)}, bf16[256,1920]{1,0:T(8,128)(2,1)S(1)}, u32[]{:S(2)}, u32[]{:S(2)}) collective-permute-start(bf16[256,1920]{1,0:T(8,128)(2,1)S(1)} %constant_dynamic-update-slice_fusion.4.refs_8_.refs_9_.refs_1_), channel_id=1, source_target_pairs={{0,8},{1,9},{2,10},{3,11},{4,12},{5,13},{6,14},{7,15},{8,0},{9,1},... | collective-permute-start | bytes 2949128 | tf_op jit(solution)/shard_map/ppermute | solution.py:31
  37.7 17.1 %collective-permute-start.10 = (bf16[128,1920]{1,0:T(8,128)(2,1)S(1)}, bf16[128,1920]{1,0:T(8,128)(2,1)S(1)}, u32[]{:S(2)}, u32[]{:S(2)}) collective-permute-start(bf16[128,1920]{1,0:T(8,128)(2,1)S(1)} %collective-permute-done.5), channel_id=1, source_target_pairs={{0,48},{1,49},{2,50},{3,51},{4,52},{5,53},{6,54},{7,55},{8,56},{9,... | collective-permute-start | bytes 1474568 | tf_op jit(solution)/shard_map/ppermute | solution.py:31
  39.4 16.8 %collective-permute-start.13 = (bf16[128,1920]{1,0:T(8,128)(2,1)S(1)}, bf16[128,1920]{1,0:T(8,128)(2,1)S(1)}, u32[]{:S(2)}, u32[]{:S(2)}) collective-permute-start(bf16[128,1920]{1,0:T(8,128)(2,1)S(1)} %collective-permute-done.refs_1_), channel_id=1, source_target_pairs={{0,6},{1,7},{2,0},{3,1},{4,2},{5,3},{6,4},{7,5},{8,14},{9,15},{10,... | collective-permute-start | bytes 1474568 | tf_op jit(solution)/shard_map/ppermute | solution.py:31
  42.3 13.9 %collective-permute-start.11 = (bf16[128,1920]{1,0:T(8,128)(2,1)S(1)}, bf16[128,1920]{1,0:T(8,128)(2,1)S(1)}, u32[]{:S(2)}, u32[]{:S(2)}) collective-permute-start(bf16[128,1920]{1,0:T(8,128)(2,1)S(1)} %collective-permute-done.3), channel_id=1, source_target_pairs={{0,65},{1,64},{2,67},{3,66},{4,69},{5,68},{6,71},{7,70},{8,73},{9,... | collective-permute-start | bytes 1474568 | tf_op jit(solution)/shard_map/ppermute | solution.py:31
  43.3 12.9 %collective-permute-start.12 = (bf16[128,1920]{1,0:T(8,128)(2,1)S(1)}, bf16[128,1920]{1,0:T(8,128)(2,1)S(1)}, u32[]{:S(2)}, u32[]{:S(2)}) collective-permute-start(bf16[128,1920]{1,0:T(8,128)(2,1)S(1)} %collective-permute-done.4.refs_3_), channel_id=1, source_target_pairs={{0,1},{1,0},{2,3},{3,2},{4,5},{5,4},{6,7},{7,6},{8,9},{9,8},{10,11... | collective-permute-start | bytes 1474568 | tf_op jit(solution)/shard_map/ppermute | solution.py:31
  56.3 3.5 %collective-permute-start.16 = (bf16[256,1920]{1,0:T(8,128)(2,1)S(1)}, bf16[256,1920]{1,0:T(8,128)(2,1)S(1)}, u32[]{:S(2)}, u32[]{:S(2)}) collective-permute-start(bf16[256,1920]{1,0:T(8,128)(2,1)S(1)} %constant_dynamic-update-slice_fusion.6.refs_12_.refs_4_), channel_id=1, source_target_pairs={{0,8},{1,9},{2,10},{3,11},{4,12},{5,13},{6,14},{7,15},{8,0},{9,1},... | collective-permute-start | bytes 2949128 | tf_op jit(solution)/shard_map/ppermute | solution.py:31
  61.3 1.5 %collective-permute-start.17 = (f32[8,128]{1,0:T(8,128)S(1)}, f32[8,128]{1,0:T(8,128)S(1)}, u32[]{:S(2)}, u32[]{:S(2)}) collective-permute-start(f32[8,128]{1,0:T(8,128)S(1)} %get-tuple-element.94), channel_id=1, source_target_pairs={{0,8},{1,9},{2,10},{3,11},{4,12},{5,13},{6,14},{7,15},{8,0},{9,1},... | collective-permute-start | bytes 12296 | tf_op jit(solution)/shard_map/ppermute | solution.py:31
  62.8 6.8 %collective-permute-start.18 = (bf16[1024,768]{1,0:T(8,128)(2,1)S(1)}, bf16[1024,768]{1,0:T(8,128)(2,1)S(1)}, u32[]{:S(2)}, u32[]{:S(2)}) collective-permute-start(bf16[1024,768]{1,0:T(8,128)(2,1)S(1)} %other_grad.1), channel_id=1, source_target_pairs={{0,8},{1,9},{2,10},{3,11},{4,12},{5,13},{6,14},{7,15},{8,0},{9,1},... | collective-permute-start | bytes 4718600 | tf_op jit(solution)/shard_map/ppermute | solution.py:31
  63.0 5.1 %collective-permute-start.21 = (f32[8,128]{1,0:T(8,128)S(1)}, f32[8,128]{1,0:T(8,128)S(1)}, u32[]{:S(2)}, u32[]{:S(2)}) collective-permute-start(f32[8,128]{1,0:T(8,128)S(1)} %add.12), channel_id=1, source_target_pairs={{0,4},{1,5},{2,6},{3,7},{4,0},{5,1},{6,2},{7,3},{8,12},{9,13},{10,... | collective-permute-start | bytes 12296 | tf_op jit(solution)/shard_map/ppermute | solution.py:31
  63.1 5.0 %collective-permute-start.20 = (f32[8,128]{1,0:T(8,128)S(1)}, f32[8,128]{1,0:T(8,128)S(1)}, u32[]{:S(2)}, u32[]{:S(2)}) collective-permute-start(f32[8,128]{1,0:T(8,128)S(1)} %add.12), channel_id=1, source_target_pairs={{0,6},{1,7},{2,0},{3,1},{4,2},{5,3},{6,4},{7,5},{8,14},{9,15},{10,... | collective-permute-start | bytes 12296 | tf_op jit(solution)/shard_map/ppermute | solution.py:31
  64.8 4.8 %collective-permute-start.19 = (f32[8,128]{1,0:T(8,128)S(1)}, f32[8,128]{1,0:T(8,128)S(1)}, u32[]{:S(2)}, u32[]{:S(2)}) collective-permute-start(f32[8,128]{1,0:T(8,128)S(1)} %add.12), channel_id=1, source_target_pairs={{0,2},{1,3},{2,4},{3,5},{4,6},{5,7},{6,0},{7,1},{8,10},{9,11},{10,... | collective-permute-start | bytes 12296 | tf_op jit(solution)/shard_map/ppermute | solution.py:31
  70.0 16.7 %collective-permute-start.22 = (bf16[272,768]{1,0:T(8,128)(2,1)S(1)}, bf16[272,768]{1,0:T(8,128)(2,1)S(1)}, u32[]{:S(2)}, u32[]{:S(2)}) collective-permute-start(bf16[272,768]{1,0:T(8,128)(2,1)S(1)} %get-tuple-element.109), channel_id=1, source_target_pairs={{0,48},{1,49},{2,50},{3,51},{4,52},{5,53},{6,54},{7,55},{8,56},{9,... | collective-permute-start | bytes 1253384 | tf_op jit(solution)/shard_map/ppermute | solution.py:31
  71.0 15.6 %collective-permute-start.23 = (bf16[272,768]{1,0:T(8,128)(2,1)S(1)}, bf16[272,768]{1,0:T(8,128)(2,1)S(1)}, u32[]{:S(2)}, u32[]{:S(2)}) collective-permute-start(bf16[272,768]{1,0:T(8,128)(2,1)S(1)} %get-tuple-element.110), channel_id=1, source_target_pairs={{0,16},{1,17},{2,18},{3,19},{4,20},{5,21},{6,22},{7,23},{8,24},{9,... | collective-permute-start | bytes 1253384 | tf_op jit(solution)/shard_map/ppermute | solution.py:31
  72.1 9.4 %collective-permute-start.26 = (bf16[256,768]{1,0:T(8,128)(2,1)S(1)}, bf16[256,768]{1,0:T(8,128)(2,1)S(1)}, u32[]{:S(2)}, u32[]{:S(2)}) collective-permute-start(bf16[256,768]{1,0:T(8,128)(2,1)S(1)} %get-tuple-element.114), channel_id=1, source_target_pairs={{0,6},{1,7},{2,0},{3,1},{4,2},{5,3},{6,4},{7,5},{8,14},{9,15},{10,... | collective-permute-start | bytes 1179656 | tf_op jit(solution)/shard_map/ppermute | solution.py:31
  73.2 10.9 %collective-permute-start.27 = (bf16[256,768]{1,0:T(8,128)(2,1)S(1)}, bf16[256,768]{1,0:T(8,128)(2,1)S(1)}, u32[]{:S(2)}, u32[]{:S(2)}) collective-permute-start(bf16[256,768]{1,0:T(8,128)(2,1)S(1)} %get-tuple-element.115), channel_id=1, source_target_pairs={{0,2},{1,3},{2,4},{3,5},{4,6},{5,7},{6,0},{7,1},{8,10},{9,11},{10,... | collective-permute-start | bytes 1179656 | tf_op jit(solution)/shard_map/ppermute | solution.py:31
  74.1 5.7 %collective-permute-start.28 = (bf16[128,768]{1,0:T(8,128)(2,1)S(1)}, bf16[128,768]{1,0:T(8,128)(2,1)S(1)}, u32[]{:S(2)}, u32[]{:S(2)}) collective-permute-start(bf16[128,768]{1,0:T(8,128)(2,1)S(1)} %get-tuple-element.117), channel_id=1, source_target_pairs={{0,1},{1,0},{2,3},{3,2},{4,5},{5,4},{6,7},{7,6},{8,9},{9,8},{10,11... | collective-permute-start | bytes 589832 | tf_op jit(solution)/shard_map/ppermute | solution.py:31
  79.8 6.9 %collective-permute-start.24 = (bf16[128,768]{1,0:T(8,128)(2,1)S(1)}, bf16[128,768]{1,0:T(8,128)(2,1)S(1)}, u32[]{:S(2)}, u32[]{:S(2)}) collective-permute-start(bf16[128,768]{1,0:T(8,128)(2,1)S(1)} %get-tuple-element.112), channel_id=1, source_target_pairs={{0,65},{1,64},{2,67},{3,66},{4,69},{5,68},{6,71},{7,70},{8,73},{9,... | collective-permute-start | bytes 589832 | tf_op jit(solution)/shard_map/ppermute | solution.py:31
  81.5 5.1 %collective-permute-start.25 = (f32[8,128]{1,0:T(8,128)S(1)}, f32[8,128]{1,0:T(8,128)S(1)}, u32[]{:S(2)}, u32[]{:S(2)}) collective-permute-start(f32[8,128]{1,0:T(8,128)S(1)} %add_add_fusion.loss), channel_id=1, source_target_pairs={{0,32},{1,33},{2,34},{3,35},{4,36},{5,37},{6,38},{7,39},{8,40},{9,... | collective-permute-start | bytes 12296 | tf_op jit(solution)/shard_map/ppermute | solution.py:31
  84.1 14.0 %copy-start = (bf16[128,768]{1,0:T(8,128)(2,1)S(1)}, bf16[128,768]{1,0:T(8,128)(2,1)}, u32[]{:S(2)}) copy-start(bf16[128,768]{1,0:T(8,128)(2,1)} %si.3) | copy-start | bytes 589828
  84.1 14.1 %copy-start.1 = (bf16[128,768]{1,0:T(8,128)(2,1)S(1)}, bf16[128,768]{1,0:T(8,128)(2,1)}, u32[]{:S(2)}) copy-start(bf16[128,768]{1,0:T(8,128)(2,1)} %st.3) | copy-start | bytes 589828
  86.9 11.2 %collective-permute-start.30 = (bf16[144,768]{1,0:T(8,128)(2,1)S(1)}, bf16[144,768]{1,0:T(8,128)(2,1)S(1)}, u32[]{:S(2)}, u32[]{:S(2)}) collective-permute-start(bf16[144,768]{1,0:T(8,128)(2,1)S(1)} %get-tuple-element.121), channel_id=1, source_target_pairs={{0,65},{1,64},{2,67},{3,66},{4,69},{5,68},{6,71},{7,70},{8,73},{9,... | collective-permute-start | bytes 663560 | tf_op jit(solution)/shard_map/ppermute | solution.py:31
  88.8 9.4 %collective-permute-start.32 = (bf16[144,768]{1,0:T(8,128)(2,1)S(1)}, bf16[144,768]{1,0:T(8,128)(2,1)S(1)}, u32[]{:S(2)}, u32[]{:S(2)}) collective-permute-start(bf16[144,768]{1,0:T(8,128)(2,1)S(1)} %get-tuple-element.124), channel_id=1, source_target_pairs={{0,1},{1,0},{2,3},{3,2},{4,5},{5,4},{6,7},{7,6},{8,9},{9,8},{10,11... | collective-permute-start | bytes 663560 | tf_op jit(solution)/shard_map/ppermute | solution.py:31
  89.1 7.2 %collective-permute-start.33 = (bf16[128,768]{1,0:T(8,128)(2,1)S(1)}, bf16[128,768]{1,0:T(8,128)(2,1)S(1)}, u32[]{:S(2)}, u32[]{:S(2)}) collective-permute-start(bf16[128,768]{1,0:T(8,128)(2,1)S(1)} %get-tuple-element.125), channel_id=1, source_target_pairs={{0,4},{1,5},{2,6},{3,7},{4,0},{5,1},{6,2},{7,3},{8,12},{9,13},{10,... | collective-permute-start | bytes 589832 | tf_op jit(solution)/shard_map/ppermute | solution.py:31
  91.0 7.2 %collective-permute-start.31 = (bf16[128,768]{1,0:T(8,128)(2,1)S(1)}, bf16[128,768]{1,0:T(8,128)(2,1)S(1)}, u32[]{:S(2)}, u32[]{:S(2)}) collective-permute-start(bf16[128,768]{1,0:T(8,128)(2,1)S(1)} %get-tuple-element.122), channel_id=1, source_target_pairs={{0,32},{1,33},{2,34},{3,35},{4,36},{5,37},{6,38},{7,39},{8,40},{9,... | collective-permute-start | bytes 589832 | tf_op jit(solution)/shard_map/ppermute | solution.py:31
  92.6 5.1 %collective-permute-start.29 = (f32[8,128]{1,0:T(8,128)S(1)}, f32[8,128]{1,0:T(8,128)S(1)}, u32[]{:S(2)}, u32[]{:S(2)}) collective-permute-start(f32[8,128]{1,0:T(8,128)S(1)} %get-tuple-element.119.loss), channel_id=1, source_target_pairs={{0,64},{1,65},{2,66},{3,67},{4,68},{5,69},{6,70},{7,71},{8,72},{9,... | collective-permute-start | bytes 12296 | tf_op jit(solution)/shard_map/ppermute | solution.py:31
